TPU v7x, 256 devices: a whole 4x4x8 slice. The times are simulated.
256 devices in a mesh: group: 8 (over y, x_hi), row: 32 (over x_lo, z, core).
Axes of the slice: x: 4 (x_hi: 2, x_lo: 2; x = x_hi * 2 + x_lo), y: 4, z: 8, core: 2. Of those that a mesh axis runs over, the one named last changes fastest.
Arguments:
- embeddings: bfloat16 [1048576, 128], P(('group', 'row')), parts along dimension 0, may hold values from -6 to 6
- band_tiles: bfloat16 [8192, 4, 128, 128], P(('group', 'row')), parts along dimension 0, may hold values from -0.1875 to 0.1875
- band_offsets: int32 [8192, 4], P(('group', 'row')), parts along dimension 0, may hold values from -3 to 3
- hub_tiles: bfloat16 [8192, 4, 128, 128], P(('group', 'row')), parts along dimension 0, may hold values from -0.1875 to 0.1875
- hub_blocks: int32 [8192, 4], P(('group', 'row')), parts along dimension 0, may hold values from 0 to 31, all different within a row
- hub_ids: int32 [3, 32768], P(None, ('group', 'row')), parts along dimension 1, may hold values from 0 to 131071, as said below
Outputs:
- averaged: bfloat16 [1048576, 128], P(('group', 'row')), parts along dimension 0
There are 8 independent parts, one for each index of `group`. A program takes and returns all parts, laid end to end along the dimension named above; each array names one. Nothing has to cross between parts.
Inputs may be any that keep to these rules, and one draw needn't show every extreme that they name: `hub_ids`: in each layer, entries k * 128 to (k+1) * 128 - 1 are distinct rows among k * 4096 to (k+1) * 4096 - 1.
All inputs are finite; a program needn't handle non-finite values.
Results may differ from a plain program's by a relative error of at most 0.0075.
Values may be sent and summed in bfloat16 or wider, within the bound.
No kernel may reach another device: no remote copies, remote signals or barrier semaphores. Data moves between devices by JAX's collectives and lax.ppermute only.
A program may use at most 64 MiB of HBM per device.

v0:
```python
import jax
import jax.numpy as jnp
from jax import lax
from jax.sharding import PartitionSpec as P

BAND = 3
LAYERS = 3


def padded_2(cells, sides, width):
    for axis, dim in sides:
        count = lax.axis_size(axis)
        ends = count - 1
        head = lax.slice_in_dim(cells, 0, width, axis=dim)
        tail = lax.slice_in_dim(cells, cells.shape[dim] - width, cells.shape[dim], axis=dim)
        cells = jnp.concatenate(
            [
                lax.ppermute(tail, axis, [(i, (i + 1) % count) for i in range(ends)]),
                cells,
                lax.ppermute(head, axis, [((i + 1) % count, i) for i in range(ends)]),
            ],
            axis=dim,
        )
    return cells


def tile_products(tiles, operands):
    return jnp.einsum("bkij,bkjf->bif", tiles, operands, preferred_element_type=jnp.float32)


def propagate(current, band_tiles, band_offsets, hub_tiles, hub_blocks, local_ids):
    rows_dev, feature_count = current.shape
    tile_rows = band_tiles.shape[-1]
    block_count = rows_dev // tile_rows
    owned_hubs = jnp.take(current, local_ids, axis=0)
    hub_panel = lax.all_gather(owned_hubs, "row", axis=0, tiled=True)
    hub_near = hub_panel.reshape(-1, tile_rows, feature_count)[hub_blocks]
    padded = padded_2(current, (("row", 0),), BAND * tile_rows)
    padded_blocks = padded.reshape(block_count + 2 * BAND, tile_rows, feature_count)
    block_index = jnp.arange(block_count, dtype=jnp.int32)[:, None] + band_offsets + BAND
    nearby = padded_blocks[block_index]
    band_part = tile_products(band_tiles, nearby)
    hub_part = tile_products(hub_tiles, hub_near)
    return (band_part + hub_part).reshape(rows_dev, feature_count).astype(jnp.bfloat16)


def body(embeddings, band_tiles, band_offsets, hub_tiles, hub_blocks, hub_ids):
    rows_dev = embeddings.shape[0]
    row_start = lax.axis_index("row") * rows_dev
    local_lists = hub_ids - row_start
    current = embeddings
    layer_sum = embeddings.astype(jnp.float32)
    for level_index in range(LAYERS):
        current = propagate(
            current, band_tiles, band_offsets, hub_tiles, hub_blocks, local_lists[level_index]
        )
        layer_sum = layer_sum + current.astype(jnp.float32)
    return (layer_sum / (LAYERS + 1.0)).astype(jnp.bfloat16)


def solution(mesh):
    return jax.shard_map(
        body,
        mesh=mesh,
        in_specs=(
            P(("group", "row"), None),
            P(("group", "row"), None, None, None),
            P(("group", "row"), None),
            P(("group", "row"), None, None, None),
            P(("group", "row"), None),
            P(None, ("group", "row")),
        ),
        out_specs=P(("group", "row"), None),
        check_vma=False,
    )
```

profile of v0, /device:TPU:1, one launch (start us, length us, event | category | flops | bytes accessed | tf_op | source)
XLA Modules:
  0.0 245.2 jit_solution(17380510441997182037)
XLA Ops:
  7.2 2.0 gather_fusion.6
  11.0 4.9 %collective-permute-start = (bf16[384,128]{1,0:T(8,128)(2,1)S(1)}, bf16[384,128]{1,0:T(8,128)(2,1)S(1)}, u32[]{:S(2)}, u32[]{:S(2)}) collective-permute-start(bf16[384,128]{1,0:T(8,128)(2,1)S(1)} %get-tuple-element.16), channel_id=1, source_target_pairs={{0,1},{1,2},{2,3},{3,4},{4,5},{5,6},{6,7},{7,8},{8,9},{9,10},{10,1... | collective-permute-start | bytes 294920 | tf_op jit(solution)/shard_map/ppermute | solution.py:18
  15.9 1.9 collective-permute-start.1
  19.7 2.2 collective-permute-done.1
  23.2 3.0 %gather_fusion = bf16[128,128,128]{2,1,0:T(8,128)(2,1)} fusion(bf16[38,128,128]{2,1,0:T(8,128)(2,1)S(1)} %bitcast.85, s32[1024]{0:T(1024)S(1)} %pad_clamp_fusion.4), kind=kCustom, calls=%fused_computation.3 | custom fusion | bytes 8389120 | tf_op jit(solution)/shard_map/gather | solution.py:41
  26.2 4.7 %fusion.9 = f32[32,128,128,1]{1,2,3,0:T(8,128)S(1)} fusion(bf16[32,4,128,128]{3,2,1,0:T(8,128)(2,1)} %param.9, bf16[32,4,128,128]{3,2,1,0:T(8,128)(2,1)} %bitcast.82), kind=kOutput, calls=%fused_computation.42 | convolution fusion | flops 536870912 | bytes 10485760 | tf_op jit(solution)/shard_map/bkij,bkjf->bif/dot_general | solution.py:28
  31.0 47.0 %all-gather.4.cloned.1.call-done = bf16[4096,128]{1,0:T(8,128)(2,1)} async-done(((bf16[128,128]{1,0:T(8,128)(2,1)}), bf16[4096,128]{1,0:T(8,128)(2,1)}) %all-gather.4.cloned.1.call-update) | async-done | bytes 1048592 | tf_op jit(solution)/shard_map/all_gather | solution.py:36
  77.9 4.3 %gather_fusion.1 = bf16[128,128,128]{2,1,0:T(8,128)(2,1)} fusion(bf16[32,128,128]{2,1,0:T(8,128)(2,1)} %bitcast.88, s32[1024]{0:T(1024)S(1)} %pad_clamp_fusion.2), kind=kCustom, calls=%fused_computation.4 | custom fusion | bytes 8389120 | tf_op jit(solution)/shard_map/gather | solution.py:37
  82.2 4.7 %fusion.4 = bf16[32,128,128]{1,2,0:T(8,128)(2,1)S(1)} fusion(f32[32,128,128,1]{1,2,3,0:T(8,128)S(1)} %fusion.9, bf16[32,4,128,128]{3,2,1,0:T(8,128)(2,1)} %param.11, bf16[32,4,128,128]{3,2,1,0:T(8,128)(2,1)} %bitcast.91), kind=kOutput, calls=%fused_computation.17 | convolution fusion | flops 537919488 | bytes 11534336 | tf_op jit(solution)/shard_map/bkij,bkjf->bif/dot_general | solution.py:28
  88.4 2.2 collective-permute-start.3
  90.6 3.4 %collective-permute-start.2 = (bf16[384,128]{1,0:T(8,128)(2,1)S(1)}, bf16[384,128]{1,0:T(8,128)(2,1)S(1)}, u32[]{:S(2)}, u32[]{:S(2)}) collective-permute-start(bf16[384,128]{1,0:T(8,128)(2,1)S(1)} %bitcast.99), channel_id=1, source_target_pairs={{0,1},{1,2},{2,3},{3,4},{4,5},{5,6},{6,7},{7,8},{8,9},{9,10},{10,1... | collective-permute-start | bytes 294920 | tf_op jit(solution)/shard_map/ppermute | solution.py:18
  95.7 3.0 %gather_fusion.2 = bf16[128,128,128]{2,1,0:T(8,128)(2,1)} fusion(bf16[38,128,128]{2,1,0:T(8,128)(2,1)S(1)} %bitcast.86, s32[1024]{0:T(1024)S(1)} %pad_clamp_fusion.4), kind=kCustom, calls=%fused_computation.5 | custom fusion | bytes 8389120 | tf_op jit(solution)/shard_map/gather | solution.py:41
  98.7 4.7 %fusion.10 = f32[32,128,128,1]{1,2,3,0:T(8,128)S(1)} fusion(bf16[32,4,128,128]{3,2,1,0:T(8,128)(2,1)} %param.9, bf16[32,4,128,128]{3,2,1,0:T(8,128)(2,1)} %bitcast.83), kind=kOutput, calls=%fused_computation.43 | convolution fusion | flops 536870912 | bytes 10485760 | tf_op jit(solution)/shard_map/bkij,bkjf->bif/dot_general | solution.py:28
  103.5 48.3 %all-gather.6.cloned.1.call-done = bf16[4096,128]{1,0:T(8,128)(2,1)} async-done(((bf16[128,128]{1,0:T(8,128)(2,1)}), bf16[4096,128]{1,0:T(8,128)(2,1)}) %all-gather.6.cloned.1.call-update) | async-done | bytes 1048592 | tf_op jit(solution)/shard_map/all_gather | solution.py:36
  151.8 4.3 %gather_fusion.3 = bf16[128,128,128]{2,1,0:T(8,128)(2,1)} fusion(bf16[32,128,128]{2,1,0:T(8,128)(2,1)} %bitcast.89, s32[1024]{0:T(1024)S(1)} %pad_clamp_fusion.2), kind=kCustom, calls=%fused_computation.6 | custom fusion | bytes 8389120 | tf_op jit(solution)/shard_map/gather | solution.py:37
  156.0 5.7 %fusion.3 = bf16[32,128,128]{1,2,0:T(8,128)(2,1)} fusion(f32[32,128,128,1]{1,2,3,0:T(8,128)S(1)} %fusion.10, bf16[32,4,128,128]{3,2,1,0:T(8,128)(2,1)} %param.11, bf16[32,4,128,128]{3,2,1,0:T(8,128)(2,1)} %bitcast.92), kind=kOutput, calls=%fused_computation.15 | convolution fusion | flops 537919488 | bytes 11534336 | tf_op jit(solution)/shard_map/bkij,bkjf->bif/dot_general | solution.py:28
  161.7 2.0 gather_fusion.8
  165.4 2.2 collective-permute-start.5
  167.6 3.6 %collective-permute-start.4 = (bf16[384,128]{1,0:T(8,128)(2,1)S(1)}, bf16[384,128]{1,0:T(8,128)(2,1)S(1)}, u32[]{:S(2)}, u32[]{:S(2)}) collective-permute-start(bf16[384,128]{1,0:T(8,128)(2,1)S(1)} %bitcast.100), channel_id=1, source_target_pairs={{0,1},{1,2},{2,3},{3,4},{4,5},{5,6},{6,7},{7,8},{8,9},{9,10},{10,1... | collective-permute-start | bytes 294920 | tf_op jit(solution)/shard_map/ppermute | solution.py:18
  173.9 3.0 %gather_fusion.4 = bf16[128,128,128]{2,1,0:T(8,128)(2,1)} fusion(bf16[38,128,128]{2,1,0:T(8,128)(2,1)S(1)} %bitcast.84, s32[1024]{0:T(1024)S(1)} %pad_clamp_fusion.4), kind=kCustom, calls=%fused_computation.7 | custom fusion | bytes 8389120 | tf_op jit(solution)/shard_map/gather | solution.py:41
  177.0 4.7 %fusion.11 = f32[32,128,128,1]{1,2,3,0:T(8,128)S(1)} fusion(bf16[32,4,128,128]{3,2,1,0:T(8,128)(2,1)} %param.9, bf16[32,4,128,128]{3,2,1,0:T(8,128)(2,1)} %bitcast.81), kind=kOutput, calls=%fused_computation.44 | convolution fusion | flops 536870912 | bytes 10485760 | tf_op jit(solution)/shard_map/bkij,bkjf->bif/dot_general | solution.py:28
  181.7 46.2 %all-gather.8.cloned.1.call-done = bf16[4096,128]{1,0:T(8,128)(2,1)} async-done(((bf16[128,128]{1,0:T(8,128)(2,1)}), bf16[4096,128]{1,0:T(8,128)(2,1)}) %all-gather.8.cloned.1.call-update) | async-done | bytes 1048592 | tf_op jit(solution)/shard_map/all_gather | solution.py:36
  227.9 4.3 %gather_fusion.5 = bf16[128,128,128]{2,1,0:T(8,128)(2,1)} fusion(bf16[32,128,128]{2,1,0:T(8,128)(2,1)} %bitcast.90, s32[1024]{0:T(1024)S(1)} %pad_clamp_fusion.2), kind=kCustom, calls=%fused_computation.8 | custom fusion | bytes 8389120 | tf_op jit(solution)/shard_map/gather | solution.py:37
  232.2 4.8 %fusion.5 = f32[32,128,128]{1,2,0:T(8,128)S(1)} fusion(bf16[32,4,128,128]{3,2,1,0:T(8,128)(2,1)} %param.11, bf16[32,4,128,128]{3,2,1,0:T(8,128)(2,1)} %bitcast.87, f32[32,128,128,1]{1,2,3,0:T(8,128)S(1)} %fusion.11), kind=kOutput, calls=%fused_computation.18 | convolution fusion | flops 538443776 | bytes 12582912 | tf_op jit(solution)/shard_map/bkij,bkjf->bif/dot_general | solution.py:28
  (39 shorter events, 14.8 us)
Async XLA Ops:
  6.5 71.4 %all-gather.4.cloned.1.call-start = ((), (), s32[]{:S(2)}) async-start(), calls=%async_computation | async-start | bytes 1081344 | tf_op jit(solution)/shard_map/all_gather | solution.py:36
  10.0 141.8 %all-gather.6.cloned.1.call-start = ((), (), s32[]{:S(2)}) async-start(), calls=%async_computation.1 | async-start | bytes 1081344 | tf_op jit(solution)/shard_map/all_gather | solution.py:36
  11.0 8.7 %collective-permute-start = (bf16[384,128]{1,0:T(8,128)(2,1)S(1)}, bf16[384,128]{1,0:T(8,128)(2,1)S(1)}, u32[]{:S(2)}, u32[]{:S(2)}) collective-permute-start(bf16[384,128]{1,0:T(8,128)(2,1)S(1)} %get-tuple-element.16), channel_id=1, source_target_pairs={{0,1},{1,2},{2,3},{3,4},{4,5},{5,6},{6,7},{7,8},{8,9},{9,10},{10,1... | collective-permute-start | bytes 294920 | tf_op jit(solution)/shard_map/ppermute | solution.py:18
  15.9 5.9 %collective-permute-start.1 = (bf16[384,128]{1,0:T(8,128)(2,1)S(1)}, bf16[384,128]{1,0:T(8,128)(2,1)S(1)}, u32[]{:S(2)}, u32[]{:S(2)}) collective-permute-start(bf16[384,128]{1,0:T(8,128)(2,1)S(1)} %get-tuple-element.17), channel_id=1, source_target_pairs={{1,0},{2,1},{3,2},{4,3},{5,4},{6,5},{7,6},{8,7},{9,8},{10,9},{11,1... | collective-permute-start | bytes 294920 | tf_op jit(solution)/shard_map/ppermute | solution.py:20
  88.3 139.6 %all-gather.8.cloned.1.call-start = ((), (), s32[]{:S(2)}) async-start(), calls=%async_computation.2 | async-start | bytes 1081344 | tf_op jit(solution)/shard_map/all_gather | solution.py:36
  88.4 5.9 %collective-permute-start.3 = (bf16[384,128]{1,0:T(8,128)(2,1)S(1)}, bf16[384,128]{1,0:T(8,128)(2,1)S(1)}, u32[]{:S(2)}, u32[]{:S(2)}) collective-permute-start(bf16[384,128]{1,0:T(8,128)(2,1)S(1)} %bitcast.101), channel_id=1, source_target_pairs={{1,0},{2,1},{3,2},{4,3},{5,4},{6,5},{7,6},{8,7},{9,8},{10,9},{11,1... | collective-permute-start | bytes 294920 | tf_op jit(solution)/shard_map/ppermute | solution.py:20
  90.6 5.0 %collective-permute-start.2 = (bf16[384,128]{1,0:T(8,128)(2,1)S(1)}, bf16[384,128]{1,0:T(8,128)(2,1)S(1)}, u32[]{:S(2)}, u32[]{:S(2)}) collective-permute-start(bf16[384,128]{1,0:T(8,128)(2,1)S(1)} %bitcast.99), channel_id=1, source_target_pairs={{0,1},{1,2},{2,3},{3,4},{4,5},{5,6},{6,7},{7,8},{8,9},{9,10},{10,1... | collective-permute-start | bytes 294920 | tf_op jit(solution)/shard_map/ppermute | solution.py:18
  165.4 5.9 %collective-permute-start.5 = (bf16[384,128]{1,0:T(8,128)(2,1)S(1)}, bf16[384,128]{1,0:T(8,128)(2,1)S(1)}, u32[]{:S(2)}, u32[]{:S(2)}) collective-permute-start(bf16[384,128]{1,0:T(8,128)(2,1)S(1)} %bitcast.102), channel_id=1, source_target_pairs={{1,0},{2,1},{3,2},{4,3},{5,4},{6,5},{7,6},{8,7},{9,8},{10,9},{11,1... | collective-permute-start | bytes 294920 | tf_op jit(solution)/shard_map/ppermute | solution.py:20
  167.6 5.0 %collective-permute-start.4 = (bf16[384,128]{1,0:T(8,128)(2,1)S(1)}, bf16[384,128]{1,0:T(8,128)(2,1)S(1)}, u32[]{:S(2)}, u32[]{:S(2)}) collective-permute-start(bf16[384,128]{1,0:T(8,128)(2,1)S(1)} %bitcast.100), channel_id=1, source_target_pairs={{0,1},{1,2},{2,3},{3,4},{4,5},{5,6},{6,7},{7,8},{8,9},{9,10},{10,1... | collective-permute-start | bytes 294920 | tf_op jit(solution)/shard_map/ppermute | solution.py:18
  232.2 4.9 %copy-start = (bf16[32,128,128]{1,2,0:T(8,128)(2,1)S(1)}, bf16[32,128,128]{1,2,0:T(8,128)(2,1)}, u32[]{:S(2)}) copy-start(bf16[32,128,128]{1,2,0:T(8,128)(2,1)} %fusion.3) | copy-start | bytes 3145732
  232.2 4.9 %copy-start.1 = (bf16[4096,128]{1,0:T(8,128)(2,1)S(1)}, bf16[4096,128]{1,0:T(8,128)(2,1)}, u32[]{:S(2)}) copy-start(bf16[4096,128]{1,0:T(8,128)(2,1)} %param.8) | copy-start | bytes 3145732
Sparse Core Ops, SparseCore 0:
  10.1 67.7 all-gather.3
  88.5 63.2 all-gather.5
  164.6 63.2 all-gather.7
where the time goes:
time: 246 us; the launch traced here: 245 us
  waiting for transfers between devices  147 us (60%)
  matrix products  29.4 us (12%)
  local copies, waits for them, and re-layouts  28.9 us (12%)
  starting transfers between devices  18.2 us (7%)
  between operations  13.3 us (5%)
  other arithmetic  8.55 us (3%)
    all_gather x3, waiting for transfers between devices, propagate(): hub_panel = lax.all_gather(owned_hubs, 'row', axis=0, tiled=True)  142 us
    dot_general x6, matrix products, tile_products(): jnp.einsum('bkij,bkjf->bif', tiles, operands, preferred_element_type=jnp....  29.4 us
    gather x3, local copies, waits for them, and re-layouts, propagate(): hub_near = hub_panel.reshape(-1, tile_rows, feature_count)[hub_blocks]  12.8 us
    ppermute x3, starting transfers between devices, padded_2(): lax.ppermute(tail, axis, [(i, (i + 1) % count) for i in range(ends)])  11.9 us
    gather x3, local copies, waits for them, and re-layouts, propagate(): nearby = padded_blocks[block_index]  9.1 us
    ppermute x3, starting transfers between devices, padded_2(): lax.ppermute(head, axis, [((i + 1) % count, i) for i in range(ends)])  6.3 us
  transfers between devices with their start and end apart: 9, of which 8 were waited for; matrix products, arithmetic and copies ran while one was open for 12% of the time, Pallas kernels for 0%

commit v1 on v0

v1 whole, which is shorter than its diff:
```python
import functools

import jax
import jax.numpy as jnp
from jax import lax
from jax.experimental import pallas as pl
from jax.experimental.pallas import tpu as pltpu
from jax.sharding import PartitionSpec as P

BAND = 3
LAYERS = 3
BLOCK = 128
STEP = 4
DEVICES = 32


def index_of(x, z, c):
    return x * 16 + z * 2 + c


def permutation(move):
    return [
        (index_of(x, z, c), index_of(*move(x, z, c)))
        for x in range(2)
        for z in range(8)
        for c in range(2)
    ]


def along_z(step):
    return permutation(lambda x, z, c: (x, z ^ step, c))


ACROSS_X = permutation(lambda x, z, c: (1 - x, z, c))
ACROSS_CORE = permutation(lambda x, z, c: (x, z, 1 - c))
ACROSS_EDGE = [
    (i, (i + 1) % DEVICES if i % 2 else (i - 1) % DEVICES) for i in range(DEVICES)
]


def permute(array, pairs):
    return lax.ppermute(array, "row", pairs)


def gather_rows(own):
    pair = jnp.concatenate([own, permute(own, along_z(6))])
    column = jnp.concatenate([pair] + [permute(pair, along_z(g)) for g in (1, 2, 3)])
    plane = jnp.concatenate([column, permute(column, ACROSS_X)])
    return jnp.concatenate([plane, permute(plane, ACROSS_CORE)])


def places(hub_blocks, me):
    delta = hub_blocks ^ me
    dx, dz, dc = delta >> 4, (delta >> 1) & 7, delta & 1
    s = dz >> 2
    g = (dz & 3) ^ (2 * s)
    return 16 * dc + 8 * dx + 2 * g + s


def dot(a, b):
    return jnp.dot(a, b, preferred_element_type=jnp.float32)


def one_hot(ids, first, width):
    columns = lax.broadcasted_iota(jnp.int32, (ids.shape[0], width), 1) + first
    return (columns == ids).astype(jnp.bfloat16)


def pick_kernel(ids_ref, table_ref, out_ref):
    rows = table_ref.shape[0]
    wide = 2 * BLOCK
    ids = ids_ref[...]
    total = jnp.zeros(out_ref.shape, jnp.float32)
    for first in range(0, rows, wide):
        total += dot(one_hot(ids, first, wide), table_ref[first : first + wide, :])
    out_ref[...] = total.astype(out_ref.dtype)


def pick(ids, table):
    return pl.pallas_call(
        pick_kernel,
        out_shape=jax.ShapeDtypeStruct((ids.shape[0], table.shape[1]), table.dtype),
        cost_estimate=pl.CostEstimate(flops=2**27, bytes_accessed=2**20, transcendentals=0),
    )(ids, table)


def band_kernel(offsets_ref, side_ref, table_ref, inner_ref, outer_ref, tiles_ref, out_ref, padded):
    step = pl.program_id(0)
    blocks = table_ref.shape[0]

    @pl.when(step == 0)
    def _():
        padded[BAND : BAND + blocks] = table_ref[...]
        core, has_left, has_right = side_ref[0], side_ref[1], side_ref[2]
        inner, outer = inner_ref[...], outer_ref[...]
        left = jnp.where(core == 0, outer, inner)
        right = jnp.where(core == 0, inner, outer)
        padded[0:BAND] = jnp.where(has_left == 1, left, jnp.zeros_like(left))
        padded[BAND + blocks :] = jnp.where(has_right == 1, right, jnp.zeros_like(right))

    for i in range(STEP):
        b = step * STEP + i
        tiles = jnp.concatenate([tiles_ref[i, k] for k in range(4)], axis=1)
        near = jnp.concatenate(
            [padded[b + BAND + offsets_ref[b * 4 + k]] for k in range(4)], axis=0
        )
        out_ref[i] = dot(tiles, near)


def band_products(offsets, side, table, inner, outer, tiles):
    blocks = table.shape[0]
    whole = lambda shape: pl.BlockSpec(shape, lambda i, *_: (0,) * len(shape))
    return pl.pallas_call(
        band_kernel,
        grid_spec=pltpu.PrefetchScalarGridSpec(
            num_scalar_prefetch=2,
            grid=(blocks // STEP,),
            in_specs=[
                whole(table.shape),
                whole(inner.shape),
                whole(outer.shape),
                pl.BlockSpec((STEP, 4, BLOCK, BLOCK), lambda i, *_: (i, 0, 0, 0)),
            ],
            out_specs=pl.BlockSpec((STEP, BLOCK, BLOCK), lambda i, *_: (i, 0, 0)),
            scratch_shapes=[pltpu.VMEM((blocks + 2 * BAND, BLOCK, BLOCK), jnp.bfloat16)],
        ),
        out_shape=jax.ShapeDtypeStruct((blocks, BLOCK, BLOCK), jnp.float32),
        compiler_params=pltpu.CompilerParams(vmem_limit_bytes=24 * 2**20),
        cost_estimate=pl.CostEstimate(flops=2**29, bytes_accessed=7 * 2**20, transcendentals=0),
    )(offsets, side, table, inner, outer, tiles)


def hub_sum(i, step, place_ref, panel_ref, tiles_ref, band_ref):
    b = step * STEP + i
    tiles = jnp.concatenate([tiles_ref[i, k] for k in range(4)], axis=1)
    near = jnp.concatenate([panel_ref[place_ref[b * 4 + k]] for k in range(4)], axis=0)
    return (dot(tiles, near) + band_ref[i]).astype(jnp.bfloat16)


def hub_kernel(place_ref, ids_ref, panel_ref, tiles_ref, band_ref, out_ref, picked_ref, total):
    step = pl.program_id(0)

    @pl.when(step == 0)
    def _():
        total[...] = jnp.zeros_like(total)

    ids = ids_ref[...]
    for i in range(STEP):
        value = hub_sum(i, step, place_ref, panel_ref, tiles_ref, band_ref)
        out_ref[i] = value
        total[...] += dot(one_hot(ids, (step * STEP + i) * BLOCK, BLOCK), value)

    @pl.when(step == pl.num_programs(0) - 1)
    def _():
        picked_ref[...] = total[...].astype(jnp.bfloat16)


def last_kernel(place_ref, panel_ref, tiles_ref, band_ref, e0_ref, e1_ref, e2_ref, out_ref):
    step = pl.program_id(0)
    for i in range(STEP):
        value = hub_sum(i, step, place_ref, panel_ref, tiles_ref, band_ref)
        total = e0_ref[i].astype(jnp.float32) + e1_ref[i].astype(jnp.float32)
        total = total + e2_ref[i].astype(jnp.float32) + value.astype(jnp.float32)
        out_ref[i] = (total * 0.25).astype(jnp.bfloat16)


def rows_spec():
    return pl.BlockSpec((STEP, BLOCK, BLOCK), lambda i, *_: (i, 0, 0))


def tiles_spec():
    return pl.BlockSpec((STEP, 4, BLOCK, BLOCK), lambda i, *_: (i, 0, 0, 0))


def hub_layer(place, ids, panel, tiles, band):
    blocks = tiles.shape[0]
    return pl.pallas_call(
        hub_kernel,
        grid_spec=pltpu.PrefetchScalarGridSpec(
            num_scalar_prefetch=1,
            grid=(blocks // STEP,),
            in_specs=[
                pl.BlockSpec(ids.shape, lambda i, *_: (0, 0)),
                pl.BlockSpec(panel.shape, lambda i, *_: (0, 0, 0)),
                tiles_spec(),
                rows_spec(),
            ],
            out_specs=[rows_spec(), pl.BlockSpec((BLOCK, BLOCK), lambda i, *_: (0, 0))],
            scratch_shapes=[pltpu.VMEM((BLOCK, BLOCK), jnp.float32)],
        ),
        out_shape=[
            jax.ShapeDtypeStruct((blocks, BLOCK, BLOCK), jnp.bfloat16),
            jax.ShapeDtypeStruct((BLOCK, BLOCK), jnp.bfloat16),
        ],
        compiler_params=pltpu.CompilerParams(vmem_limit_bytes=24 * 2**20),
        cost_estimate=pl.CostEstimate(flops=2**29, bytes_accessed=8 * 2**20, transcendentals=0),
    )(place, ids, panel, tiles, band)


def last_layer(place, panel, tiles, band, e0, e1, e2):
    blocks = tiles.shape[0]
    return pl.pallas_call(
        last_kernel,
        grid_spec=pltpu.PrefetchScalarGridSpec(
            num_scalar_prefetch=1,
            grid=(blocks // STEP,),
            in_specs=[
                pl.BlockSpec(panel.shape, lambda i, *_: (0, 0, 0)),
                tiles_spec(),
            ]
            + [rows_spec()] * 4,
            out_specs=rows_spec(),
        ),
        out_shape=jax.ShapeDtypeStruct((blocks, BLOCK, BLOCK), jnp.bfloat16),
        compiler_params=pltpu.CompilerParams(vmem_limit_bytes=24 * 2**20),
        cost_estimate=pl.CostEstimate(flops=2**29, bytes_accessed=11 * 2**20, transcendentals=0),
    )(place, panel, tiles, band, e0, e1, e2)


def body(embeddings, band_tiles, band_offsets, hub_tiles, hub_blocks, hub_ids):
    rows_dev, features = embeddings.shape
    blocks = rows_dev // BLOCK
    me = lax.axis_index("row")
    core = me % 2
    side = jnp.stack([core, (me > 0).astype(jnp.int32), (me < DEVICES - 1).astype(jnp.int32)])
    offsets = band_offsets.reshape(-1)
    place = places(hub_blocks, me).reshape(-1)
    ids = (hub_ids - me * rows_dev)[:, :, None]

    def halos(table):
        start_inner = jnp.where(core == 0, blocks - BAND, 0)
        start_outer = jnp.where(core == 0, 0, blocks - BAND)
        inner = permute(lax.dynamic_slice_in_dim(table, start_inner, BAND), ACROSS_CORE)
        outer = permute(lax.dynamic_slice_in_dim(table, start_outer, BAND), ACROSS_EDGE)
        return inner, outer

    tables = [embeddings.reshape(blocks, BLOCK, features)]
    picked = pick(ids[0], embeddings)
    for level in range(LAYERS):
        table = tables[-1]
        panel = gather_rows(picked).reshape(DEVICES, BLOCK, features)
        inner, outer = halos(table)
        band = band_products(offsets, side, table, inner, outer, band_tiles)
        if level < LAYERS - 1:
            table, picked = hub_layer(place, ids[level + 1], panel, hub_tiles, band)
            tables.append(table)
        else:
            averaged = last_layer(place, panel, hub_tiles, band, *tables)
    return averaged.reshape(rows_dev, features)


def solution(mesh):
    return jax.shard_map(
        body,
        mesh=mesh,
        in_specs=(
            P(("group", "row"), None),
            P(("group", "row"), None, None, None),
            P(("group", "row"), None),
            P(("group", "row"), None, None, None),
            P(("group", "row"), None),
            P(None, ("group", "row")),
        ),
        out_specs=P(("group", "row"), None),
        check_vma=False,
    )
```

time: 246 us -> 127 us (0.52)
  waiting for transfers between devices: 147 us -> 33.9 us
  matrix products: 29.4 us -> 0 us
  Pallas kernels: 0 us -> 28.4 us
  starting transfers between devices: 18.2 us -> 44.2 us
  between operations: 13.3 us -> 0.24 us
  local copies, waits for them, and re-layouts: 28.9 us -> 16.6 us
  other arithmetic: 8.55 us -> 1.62 us
    all_gather x3 -> x0, waiting for transfers between devices: 142 us -> none  [propagate(): hub_panel = lax.all_gather(owned_hubs, 'row', axis=0, tiled=True)]
    dot_general x6 -> x0, matrix products: 29.4 us -> none  [tile_products(): jnp.einsum('bkij,bkjf->bif', tiles, operands, preferred_element_type=jnp....]
    ppermute x6 -> x24, waiting for transfers between devices: 5.23 us -> 33.9 us  [permute(): return lax.ppermute(array, 'row', pairs)]
    pallas_call x0 -> x7, Pallas kernels: none -> 28.4 us  [the longest x2 12.2 us: hub_layer(): pl.pallas_call(hub_kernel, grid_spec=pltpu.PrefetchScalarGridSpec(num_sca...]
    gather x9 -> x0, local copies, waits for them, and re-layouts: 26.6 us -> none  [the longest x3 12.8 us: propagate(): hub_near = hub_panel.reshape(-1, tile_rows, feature_count)[hub_blocks]]
    ppermute x6 -> x24, starting transfers between devices: 18.2 us -> 44.2 us  [permute(): return lax.ppermute(array, 'row', pairs)]
    unnamed x4 -> x32, local copies, waits for them, and re-layouts: 0.01 us -> 11.8 us
    select_n x5 -> x0, other arithmetic: 3.48 us -> none  [the longest x3 2.11 us: propagate(): owned_hubs = jnp.take(current, local_ids, axis=0)]
  transfers between devices with their start and end apart: 9 -> 24, of which waited for: 8 -> 18; matrix products, arithmetic and copies ran while one was open for 12% -> 5% of each run, Pallas kernels for 0% -> 7%
where the time goes in v1:
time: 127 us; the launch traced here: 125 us
  starting transfers between devices  44.2 us (35%)
  waiting for transfers between devices  33.9 us (27%)
  Pallas kernels  28.4 us (22%)
  local copies, waits for them, and re-layouts  16.6 us (13%)
  other arithmetic  1.62 us (1%)
    ppermute x24, starting transfers between devices, permute(): return lax.ppermute(array, 'row', pairs)  44.2 us
    ppermute x24, waiting for transfers between devices, permute(): return lax.ppermute(array, 'row', pairs)  33.9 us
    pallas_call x2, Pallas kernels, hub_layer(): pl.pallas_call(hub_kernel, grid_spec=pltpu.PrefetchScalarGridSpec(num_sca...  12.2 us
    unnamed x32, local copies, waits for them, and re-layouts  11.8 us
    pallas_call x3, Pallas kernels, band_products(): pl.pallas_call(band_kernel, grid_spec=pltpu.PrefetchScalarGridSpec(num_sc...  9.22 us
    pallas_call x1, Pallas kernels, last_layer(): pl.pallas_call(last_kernel, grid_spec=pltpu.PrefetchScalarGridSpec(num_sc...  4.67 us
  transfers between devices with their start and end apart: 24, of which 18 were waited for; matrix products, arithmetic and copies ran while one was open for 5% of the time, Pallas kernels for 7%

profile of v1, /device:TPU:1, one launch (start us, length us, event | category | flops | bytes accessed | tf_op | source)
XLA Modules:
  0.0 125.0 jit_solution(2520256955395196614)
XLA Ops:
  1.5 2.3 %shard_map.64 = bf16[128,128]{1,0:T(8,128)(2,1)} custom-call(s32[128,1]{1,0:T(8,128)} %copy.13.ids_ref, bf16[4096,128]{1,0:T(8,128)(2,1)} %table_ref.1), custom_call_target="tpu_custom_call" | custom-call | flops 134217728 | bytes 1048576 | tf_op jit(solution)/shard_map/pallas_call | solution.py:80
  3.9 6.8 %collective-permute-start = (bf16[128,128]{1,0:T(8,128)(2,1)}, bf16[128,128]{1,0:T(8,128)(2,1)S(1)}, u32[]{:S(2)}, u32[]{:S(2)}) collective-permute-start(bf16[128,128]{1,0:T(8,128)(2,1)} %shard_map.64), channel_id=1, source_target_pairs={{0,12},{1,13},{2,14},{3,15},{4,8},{5,9},{6,10},{7,11},{8,4},{9,5},... | collective-permute-start | bytes 98312 | tf_op jit(solution)/shard_map/ppermute | solution.py:42
  22.5 4.0 %collective-permute-done.4 = bf16[1024,128]{1,0:T(8,128)(2,1)S(1)} collective-permute-done((bf16[1024,128]{1,0:T(8,128)(2,1)S(1)}, bf16[1024,128]{1,0:T(8,128)(2,1)S(1)}, u32[]{:S(2)}, u32[]{:S(2)}) %collective-permute-start.4) | collective-permute-done | bytes 262176 | tf_op jit(solution)/shard_map/ppermute | solution.py:42
  27.3 4.1 %collective-permute-start.5 = (bf16[2048,128]{1,0:T(8,128)(2,1)}, bf16[2048,128]{1,0:T(8,128)(2,1)S(1)}, u32[]{:S(2)}, u32[]{:S(2)}) collective-permute-start(bf16[2048,128]{1,0:T(8,128)(2,1)} %get-tuple-element.23), channel_id=1, source_target_pairs={{0,1},{1,0},{2,3},{3,2},{4,5},{5,4},{6,7},{7,6},{8,9},{9,8},{10,11... | collective-permute-start | bytes 1572872 | tf_op jit(solution)/shard_map/ppermute | solution.py:42
  33.1 2.6 %collective-permute-done.7.outer_ref = bf16[3,128,128]{2,1,0:T(8,128)(2,1)S(1)} collective-permute-done((bf16[3,128,128]{2,1,0:T(8,128)(2,1)S(1)}, bf16[3,128,128]{2,1,0:T(8,128)(2,1)S(1)}, u32[]{:S(2)}, u32[]{:S(2)}) %collective-permute-start.7) | collective-permute-done | bytes 98336 | tf_op jit(solution)/shard_map/ppermute | solution.py:42
  35.7 2.2 %copy-done = bf16[32,4,128,128]{3,2,1,0:T(8,128)(2,1)S(1)} copy-done((bf16[32,4,128,128]{3,2,1,0:T(8,128)(2,1)S(1)}, bf16[32,4,128,128]{3,2,1,0:T(8,128)(2,1)}, u32[]{:S(2)}) %copy-start) | copy-done | bytes 4194328
  37.8 3.1 %shard_map.65.band_ref = f32[32,128,128]{2,1,0:T(8,128)S(1)} custom-call(s32[128]{0:T(128)S(1)} %reshape.29.offsets_ref, s32[3]{0:T(128)S(1)} %pad_add_fusion.side_ref, bf16[32,128,128]{2,1,0:T(8,128)(2,1)S(1)} %bitcast.15, bf16[3,128,128]{2,1,0:T(8,128)(2,1)S(1)} %collective-permute-done.6.inner_ref, ...), custom_call_target="tpu_custom_call" | custom-call | flops 536870912 | bytes 7340032 | tf_op jit(solution)/shard_map/pallas_call | solution.py:113
  41.0 6.1 %shard_map.66 = (bf16[32,128,128]{2,1,0:T(8,128)(2,1)S(1)}, bf16[128,128]{1,0:T(8,128)(2,1)S(1)}) custom-call(s32[128]{0:T(128)S(1)} %reshape.27.place_ref, s32[128,1]{1,0:T(8,128)S(1)} %copy.15.ids_ref, bf16[32,128,128]{2,1,0:T(8,128)(2,1)S(1)} %bitcast.18, bf16[32,4,128,128]{3,2,1,0:T(8,128)(2,1)S(1)} %copy-done.3, f32[32,128,128]{2,1,0:T(8,128)S(1)} %shard_map.65.band_ref), custom_call_target="tpu_custom_call" | custom-call | flops 536870912 | bytes 8388608 | tf_op jit(solution)/shard_map/pallas_call | solution.py:177
  47.1 3.1 %collective-permute-start.8 = (bf16[128,128]{1,0:T(8,128)(2,1)S(1)}, bf16[128,128]{1,0:T(8,128)(2,1)S(1)}, u32[]{:S(2)}, u32[]{:S(2)}) collective-permute-start(bf16[128,128]{1,0:T(8,128)(2,1)S(1)} %get-tuple-element.9), channel_id=1, source_target_pairs={{0,12},{1,13},{2,14},{3,15},{4,8},{5,9},{6,10},{7,11},{8,4},{9,5},... | collective-permute-start | bytes 98312 | tf_op jit(solution)/shard_map/ppermute | solution.py:42
  52.8 2.6 %collective-permute-start.9 = (bf16[256,128]{1,0:T(8,128)(2,1)S(1)}, bf16[256,128]{1,0:T(8,128)(2,1)S(1)}, u32[]{:S(2)}, u32[]{:S(2)}) collective-permute-start(bf16[256,128]{1,0:T(8,128)(2,1)S(1)} %get-tuple-element.63), channel_id=1, source_target_pairs={{0,2},{1,3},{2,0},{3,1},{4,6},{5,7},{6,4},{7,5},{8,10},{9,11},{10,... | collective-permute-start | bytes 196616 | tf_op jit(solution)/shard_map/ppermute | solution.py:42
  63.1 4.0 %collective-permute-done.12 = bf16[1024,128]{1,0:T(8,128)(2,1)S(1)} collective-permute-done((bf16[1024,128]{1,0:T(8,128)(2,1)S(1)}, bf16[1024,128]{1,0:T(8,128)(2,1)S(1)}, u32[]{:S(2)}, u32[]{:S(2)}) %collective-permute-start.12) | collective-permute-done | bytes 262176 | tf_op jit(solution)/shard_map/ppermute | solution.py:42
  67.9 4.6 %collective-permute-start.13 = (bf16[2048,128]{1,0:T(8,128)(2,1)}, bf16[2048,128]{1,0:T(8,128)(2,1)}, u32[]{:S(2)}, u32[]{:S(2)}) collective-permute-start(bf16[2048,128]{1,0:T(8,128)(2,1)} %get-tuple-element.21), channel_id=1, source_target_pairs={{0,1},{1,0},{2,3},{3,2},{4,5},{5,4},{6,7},{7,6},{8,9},{9,8},{10,11... | collective-permute-start | bytes 1572872 | tf_op jit(solution)/shard_map/ppermute | solution.py:42
  74.6 2.5 %collective-permute-done.15.outer_ref = bf16[3,128,128]{2,1,0:T(8,128)(2,1)S(1)} collective-permute-done((bf16[3,128,128]{2,1,0:T(8,128)(2,1)S(1)}, bf16[3,128,128]{2,1,0:T(8,128)(2,1)S(1)}, u32[]{:S(2)}, u32[]{:S(2)}) %collective-permute-start.15) | collective-permute-done | bytes 98336 | tf_op jit(solution)/shard_map/ppermute | solution.py:42
  79.4 3.1 %shard_map.67.band_ref = f32[32,128,128]{2,1,0:T(8,128)S(1)} custom-call(s32[128]{0:T(128)S(1)} %reshape.29.offsets_ref, s32[3]{0:T(128)S(1)} %pad_add_fusion.side_ref, bf16[32,128,128]{2,1,0:T(8,128)(2,1)S(1)} %get-tuple-element.10.table_ref.e1_ref, bf16[3,128,128]{2,1,0:T(8,128)(2,1)S(1)} %collective-permute-done.14.inner_ref, ...), custom_call_target="tpu_custom_call" | custom-call | flops 536870912 | bytes 7340032 | tf_op jit(solution)/shard_map/pallas_call | solution.py:113
  83.6 6.1 %shard_map.68 = (bf16[32,128,128]{2,1,0:T(8,128)(2,1)S(1)}, bf16[128,128]{1,0:T(8,128)(2,1)S(1)}) custom-call(s32[128]{0:T(128)S(1)} %reshape.27.place_ref, s32[128,1]{1,0:T(8,128)S(1)} %copy.16.ids_ref, bf16[32,128,128]{2,1,0:T(8,128)(2,1)S(1)} %bitcast.19, bf16[32,4,128,128]{3,2,1,0:T(8,128)(2,1)S(1)} %copy-done.4, f32[32,128,128]{2,1,0:T(8,128)S(1)} %shard_map.67.band_ref), custom_call_target="tpu_custom_call" | custom-call | flops 536870912 | bytes 8388608 | tf_op jit(solution)/shard_map/pallas_call | solution.py:177
  89.7 3.7 %collective-permute-start.16 = (bf16[128,128]{1,0:T(8,128)(2,1)S(1)}, bf16[128,128]{1,0:T(8,128)(2,1)S(1)}, u32[]{:S(2)}, u32[]{:S(2)}) collective-permute-start(bf16[128,128]{1,0:T(8,128)(2,1)S(1)} %get-tuple-element.11), channel_id=1, source_target_pairs={{0,12},{1,13},{2,14},{3,15},{4,8},{5,9},{6,10},{7,11},{8,4},{9,5},... | collective-permute-start | bytes 98312 | tf_op jit(solution)/shard_map/ppermute | solution.py:42
  94.9 2.2 %collective-permute-start.17 = (bf16[256,128]{1,0:T(8,128)(2,1)S(1)}, bf16[256,128]{1,0:T(8,128)(2,1)S(1)}, u32[]{:S(2)}, u32[]{:S(2)}) collective-permute-start(bf16[256,128]{1,0:T(8,128)(2,1)S(1)} %get-tuple-element.55), channel_id=1, source_target_pairs={{0,2},{1,3},{2,0},{3,1},{4,6},{5,7},{6,4},{7,5},{8,10},{9,11},{10,... | collective-permute-start | bytes 196616 | tf_op jit(solution)/shard_map/ppermute | solution.py:42
  99.3 2.3 %collective-permute-done.18 = bf16[256,128]{1,0:T(8,128)(2,1)S(1)} collective-permute-done((bf16[256,128]{1,0:T(8,128)(2,1)S(1)}, bf16[256,128]{1,0:T(8,128)(2,1)S(1)}, u32[]{:S(2)}, u32[]{:S(2)}) %collective-permute-start.18) | collective-permute-done | bytes 65568 | tf_op jit(solution)/shard_map/ppermute | solution.py:42
  101.7 2.2 %collective-permute-done.19 = bf16[256,128]{1,0:T(8,128)(2,1)S(1)} collective-permute-done((bf16[256,128]{1,0:T(8,128)(2,1)S(1)}, bf16[256,128]{1,0:T(8,128)(2,1)S(1)}, u32[]{:S(2)}, u32[]{:S(2)}) %collective-permute-start.19) | collective-permute-done | bytes 65568 | tf_op jit(solution)/shard_map/ppermute | solution.py:42
  105.2 4.3 %collective-permute-done.20 = bf16[1024,128]{1,0:T(8,128)(2,1)S(1)} collective-permute-done((bf16[1024,128]{1,0:T(8,128)(2,1)S(1)}, bf16[1024,128]{1,0:T(8,128)(2,1)S(1)}, u32[]{:S(2)}, u32[]{:S(2)}) %collective-permute-start.20) | collective-permute-done | bytes 262176 | tf_op jit(solution)/shard_map/ppermute | solution.py:42
  109.6 3.3 %collective-permute-start.21 = (bf16[2048,128]{1,0:T(8,128)(2,1)S(1)}, bf16[2048,128]{1,0:T(8,128)(2,1)S(1)}, u32[]{:S(2)}, u32[]{:S(2)}) collective-permute-start(bf16[2048,128]{1,0:T(8,128)(2,1)S(1)} %get-tuple-element.19), channel_id=1, source_target_pairs={{0,1},{1,0},{2,3},{3,2},{4,5},{5,4},{6,7},{7,6},{8,9},{9,8},{10,11... | collective-permute-start | bytes 1572872 | tf_op jit(solution)/shard_map/ppermute | solution.py:42
  114.6 2.6 %collective-permute-done.23.outer_ref = bf16[3,128,128]{2,1,0:T(8,128)(2,1)S(1)} collective-permute-done((bf16[3,128,128]{2,1,0:T(8,128)(2,1)S(1)}, bf16[3,128,128]{2,1,0:T(8,128)(2,1)S(1)}, u32[]{:S(2)}, u32[]{:S(2)}) %collective-permute-start.23) | collective-permute-done | bytes 98336 | tf_op jit(solution)/shard_map/ppermute | solution.py:42
  117.1 3.1 %shard_map.69.band_ref = f32[32,128,128]{2,1,0:T(8,128)S(1)} custom-call(s32[128]{0:T(128)S(1)} %reshape.29.offsets_ref, s32[3]{0:T(128)S(1)} %pad_add_fusion.side_ref, bf16[32,128,128]{2,1,0:T(8,128)(2,1)S(1)} %get-tuple-element.12.table_ref.e2_ref, bf16[3,128,128]{2,1,0:T(8,128)(2,1)S(1)} %collective-permute-done.22.inner_ref, ...), custom_call_target="tpu_custom_call" | custom-call | flops 536870912 | bytes 7340032 | tf_op jit(solution)/shard_map/pallas_call | solution.py:113
  120.3 4.7 %shard_map.70 = bf16[32,128,128]{2,1,0:T(8,128)(2,1)} custom-call(s32[128]{0:T(128)S(1)} %reshape.27.place_ref, bf16[32,128,128]{2,1,0:T(8,128)(2,1)S(1)} %bitcast.17, bf16[32,4,128,128]{3,2,1,0:T(8,128)(2,1)S(1)} %copy-done.4, f32[32,128,128]{2,1,0:T(8,128)S(1)} %shard_map.69.band_ref, bf16[32,128,128]{2,1,0:T(8,128)(2,1)S(1)} %bitcast.16, ...), custom_call_target="tpu_custom_call" | custom-call | flops 536870912 | bytes 11534336 | tf_op jit(solution)/shard_map/pallas_call | solution.py:202
  (83 shorter events, 39.2 us)
Async XLA Ops:
  3.9 8.4 %collective-permute-start = (bf16[128,128]{1,0:T(8,128)(2,1)}, bf16[128,128]{1,0:T(8,128)(2,1)S(1)}, u32[]{:S(2)}, u32[]{:S(2)}) collective-permute-start(bf16[128,128]{1,0:T(8,128)(2,1)} %shard_map.64), channel_id=1, source_target_pairs={{0,12},{1,13},{2,14},{3,15},{4,8},{5,9},{6,10},{7,11},{8,4},{9,5},... | collective-permute-start | bytes 98312 | tf_op jit(solution)/shard_map/ppermute | solution.py:42
  13.0 4.2 %collective-permute-start.1 = (bf16[256,128]{1,0:T(8,128)(2,1)S(1)}, bf16[256,128]{1,0:T(8,128)(2,1)S(1)}, u32[]{:S(2)}, u32[]{:S(2)}) collective-permute-start(bf16[256,128]{1,0:T(8,128)(2,1)S(1)} %pad_maximum_fusion), channel_id=1, source_target_pairs={{0,2},{1,3},{2,0},{3,1},{4,6},{5,7},{6,4},{7,5},{8,10},{9,11},{10,... | collective-permute-start | bytes 196616 | tf_op jit(solution)/shard_map/ppermute | solution.py:42
  13.7 4.7 %collective-permute-start.2 = (bf16[256,128]{1,0:T(8,128)(2,1)S(1)}, bf16[256,128]{1,0:T(8,128)(2,1)S(1)}, u32[]{:S(2)}, u32[]{:S(2)}) collective-permute-start(bf16[256,128]{1,0:T(8,128)(2,1)S(1)} %pad_maximum_fusion), channel_id=1, source_target_pairs={{0,4},{1,5},{2,6},{3,7},{4,0},{5,1},{6,2},{7,3},{8,12},{9,13},{10,... | collective-permute-start | bytes 196616 | tf_op jit(solution)/shard_map/ppermute | solution.py:42
  15.2 5.4 %collective-permute-start.3 = (bf16[256,128]{1,0:T(8,128)(2,1)S(1)}, bf16[256,128]{1,0:T(8,128)(2,1)S(1)}, u32[]{:S(2)}, u32[]{:S(2)}) collective-permute-start(bf16[256,128]{1,0:T(8,128)(2,1)S(1)} %pad_maximum_fusion), channel_id=1, source_target_pairs={{0,6},{1,7},{2,4},{3,5},{4,2},{5,3},{6,0},{7,1},{8,14},{9,15},{10,... | collective-permute-start | bytes 196616 | tf_op jit(solution)/shard_map/ppermute | solution.py:42
  21.3 5.2 %collective-permute-start.4 = (bf16[1024,128]{1,0:T(8,128)(2,1)S(1)}, bf16[1024,128]{1,0:T(8,128)(2,1)S(1)}, u32[]{:S(2)}, u32[]{:S(2)}) collective-permute-start(bf16[1024,128]{1,0:T(8,128)(2,1)S(1)} %get-tuple-element.45), channel_id=1, source_target_pairs={{0,16},{1,17},{2,18},{3,19},{4,20},{5,21},{6,22},{7,23},{8,24},{9,... | collective-permute-start | bytes 786440 | tf_op jit(solution)/shard_map/ppermute | solution.py:42
  27.3 13.7 %collective-permute-start.5 = (bf16[2048,128]{1,0:T(8,128)(2,1)}, bf16[2048,128]{1,0:T(8,128)(2,1)S(1)}, u32[]{:S(2)}, u32[]{:S(2)}) collective-permute-start(bf16[2048,128]{1,0:T(8,128)(2,1)} %get-tuple-element.23), channel_id=1, source_target_pairs={{0,1},{1,0},{2,3},{3,2},{4,5},{5,4},{6,7},{7,6},{8,9},{9,8},{10,11... | collective-permute-start | bytes 1572872 | tf_op jit(solution)/shard_map/ppermute | solution.py:42
  31.4 1.7 %collective-permute-start.6 = (bf16[3,128,128]{2,1,0:T(8,128)(2,1)S(1)}, bf16[3,128,128]{2,1,0:T(8,128)(2,1)S(1)}, u32[]{:S(2)}, u32[]{:S(2)}) collective-permute-start(bf16[3,128,128]{2,1,0:T(8,128)(2,1)S(1)} %get-tuple-element.18), channel_id=1, source_target_pairs={{0,1},{1,0},{2,3},{3,2},{4,5},{5,4},{6,7},{7,6},{8,9},{9,8},{10,11... | collective-permute-start | bytes 294920 | tf_op jit(solution)/shard_map/ppermute | solution.py:42
  31.5 4.1 %collective-permute-start.7 = (bf16[3,128,128]{2,1,0:T(8,128)(2,1)S(1)}, bf16[3,128,128]{2,1,0:T(8,128)(2,1)S(1)}, u32[]{:S(2)}, u32[]{:S(2)}) collective-permute-start(bf16[3,128,128]{2,1,0:T(8,128)(2,1)S(1)} %get-tuple-element.17), channel_id=1, source_target_pairs={{0,31},{1,2},{2,1},{3,4},{4,3},{5,6},{6,5},{7,8},{8,7},{9,10},{10,... | collective-permute-start | bytes 294920 | tf_op jit(solution)/shard_map/ppermute | solution.py:42
  47.1 5.1 %collective-permute-start.8 = (bf16[128,128]{1,0:T(8,128)(2,1)S(1)}, bf16[128,128]{1,0:T(8,128)(2,1)S(1)}, u32[]{:S(2)}, u32[]{:S(2)}) collective-permute-start(bf16[128,128]{1,0:T(8,128)(2,1)S(1)} %get-tuple-element.9), channel_id=1, source_target_pairs={{0,12},{1,13},{2,14},{3,15},{4,8},{5,9},{6,10},{7,11},{8,4},{9,5},... | collective-permute-start | bytes 98312 | tf_op jit(solution)/shard_map/ppermute | solution.py:42
  52.8 4.7 %collective-permute-start.9 = (bf16[256,128]{1,0:T(8,128)(2,1)S(1)}, bf16[256,128]{1,0:T(8,128)(2,1)S(1)}, u32[]{:S(2)}, u32[]{:S(2)}) collective-permute-start(bf16[256,128]{1,0:T(8,128)(2,1)S(1)} %get-tuple-element.63), channel_id=1, source_target_pairs={{0,2},{1,3},{2,0},{3,1},{4,6},{5,7},{6,4},{7,5},{8,10},{9,11},{10,... | collective-permute-start | bytes 196616 | tf_op jit(solution)/shard_map/ppermute | solution.py:42
  55.4 4.5 %collective-permute-start.10 = (bf16[256,128]{1,0:T(8,128)(2,1)S(1)}, bf16[256,128]{1,0:T(8,128)(2,1)S(1)}, u32[]{:S(2)}, u32[]{:S(2)}) collective-permute-start(bf16[256,128]{1,0:T(8,128)(2,1)S(1)} %get-tuple-element.63), channel_id=1, source_target_pairs={{0,4},{1,5},{2,6},{3,7},{4,0},{5,1},{6,2},{7,3},{8,12},{9,13},{10,... | collective-permute-start | bytes 196616 | tf_op jit(solution)/shard_map/ppermute | solution.py:42
  56.2 5.1 %collective-permute-start.11 = (bf16[256,128]{1,0:T(8,128)(2,1)S(1)}, bf16[256,128]{1,0:T(8,128)(2,1)S(1)}, u32[]{:S(2)}, u32[]{:S(2)}) collective-permute-start(bf16[256,128]{1,0:T(8,128)(2,1)S(1)} %get-tuple-element.63), channel_id=1, source_target_pairs={{0,6},{1,7},{2,4},{3,5},{4,2},{5,3},{6,0},{7,1},{8,14},{9,15},{10,... | collective-permute-start | bytes 196616 | tf_op jit(solution)/shard_map/ppermute | solution.py:42
  61.9 5.2 %collective-permute-start.12 = (bf16[1024,128]{1,0:T(8,128)(2,1)S(1)}, bf16[1024,128]{1,0:T(8,128)(2,1)S(1)}, u32[]{:S(2)}, u32[]{:S(2)}) collective-permute-start(bf16[1024,128]{1,0:T(8,128)(2,1)S(1)} %get-tuple-element.36), channel_id=1, source_target_pairs={{0,16},{1,17},{2,18},{3,19},{4,20},{5,21},{6,22},{7,23},{8,24},{9,... | collective-permute-start | bytes 786440 | tf_op jit(solution)/shard_map/ppermute | solution.py:42
  67.9 14.6 %collective-permute-start.13 = (bf16[2048,128]{1,0:T(8,128)(2,1)}, bf16[2048,128]{1,0:T(8,128)(2,1)}, u32[]{:S(2)}, u32[]{:S(2)}) collective-permute-start(bf16[2048,128]{1,0:T(8,128)(2,1)} %get-tuple-element.21), channel_id=1, source_target_pairs={{0,1},{1,0},{2,3},{3,2},{4,5},{5,4},{6,7},{7,6},{8,9},{9,8},{10,11... | collective-permute-start | bytes 1572872 | tf_op jit(solution)/shard_map/ppermute | solution.py:42
  73.1 1.5 %collective-permute-start.14 = (bf16[3,128,128]{2,1,0:T(8,128)(2,1)}, bf16[3,128,128]{2,1,0:T(8,128)(2,1)S(1)}, u32[]{:S(2)}, u32[]{:S(2)}) collective-permute-start(bf16[3,128,128]{2,1,0:T(8,128)(2,1)} %get-tuple-element.16), channel_id=1, source_target_pairs={{0,1},{1,0},{2,3},{3,2},{4,5},{5,4},{6,7},{7,6},{8,9},{9,8},{10,11... | collective-permute-start | bytes 294920 | tf_op jit(solution)/shard_map/ppermute | solution.py:42
  73.1 4.0 %collective-permute-start.15 = (bf16[3,128,128]{2,1,0:T(8,128)(2,1)S(1)}, bf16[3,128,128]{2,1,0:T(8,128)(2,1)S(1)}, u32[]{:S(2)}, u32[]{:S(2)}) collective-permute-start(bf16[3,128,128]{2,1,0:T(8,128)(2,1)S(1)} %get-tuple-element.15), channel_id=1, source_target_pairs={{0,31},{1,2},{2,1},{3,4},{4,3},{5,6},{6,5},{7,8},{8,7},{9,10},{10,... | collective-permute-start | bytes 294920 | tf_op jit(solution)/shard_map/ppermute | solution.py:42
  89.7 5.2 %collective-permute-start.16 = (bf16[128,128]{1,0:T(8,128)(2,1)S(1)}, bf16[128,128]{1,0:T(8,128)(2,1)S(1)}, u32[]{:S(2)}, u32[]{:S(2)}) collective-permute-start(bf16[128,128]{1,0:T(8,128)(2,1)S(1)} %get-tuple-element.11), channel_id=1, source_target_pairs={{0,12},{1,13},{2,14},{3,15},{4,8},{5,9},{6,10},{7,11},{8,4},{9,5},... | collective-permute-start | bytes 98312 | tf_op jit(solution)/shard_map/ppermute | solution.py:42
  94.9 4.4 %collective-permute-start.17 = (bf16[256,128]{1,0:T(8,128)(2,1)S(1)}, bf16[256,128]{1,0:T(8,128)(2,1)S(1)}, u32[]{:S(2)}, u32[]{:S(2)}) collective-permute-start(bf16[256,128]{1,0:T(8,128)(2,1)S(1)} %get-tuple-element.55), channel_id=1, source_target_pairs={{0,2},{1,3},{2,0},{3,1},{4,6},{5,7},{6,4},{7,5},{8,10},{9,11},{10,... | collective-permute-start | bytes 196616 | tf_op jit(solution)/shard_map/ppermute | solution.py:42
  97.1 4.5 %collective-permute-start.18 = (bf16[256,128]{1,0:T(8,128)(2,1)S(1)}, bf16[256,128]{1,0:T(8,128)(2,1)S(1)}, u32[]{:S(2)}, u32[]{:S(2)}) collective-permute-start(bf16[256,128]{1,0:T(8,128)(2,1)S(1)} %get-tuple-element.55), channel_id=1, source_target_pairs={{0,4},{1,5},{2,6},{3,7},{4,0},{5,1},{6,2},{7,3},{8,12},{9,13},{10,... | collective-permute-start | bytes 196616 | tf_op jit(solution)/shard_map/ppermute | solution.py:42
  98.9 5.0 %collective-permute-start.19 = (bf16[256,128]{1,0:T(8,128)(2,1)S(1)}, bf16[256,128]{1,0:T(8,128)(2,1)S(1)}, u32[]{:S(2)}, u32[]{:S(2)}) collective-permute-start(bf16[256,128]{1,0:T(8,128)(2,1)S(1)} %get-tuple-element.55), channel_id=1, source_target_pairs={{0,6},{1,7},{2,4},{3,5},{4,2},{5,3},{6,0},{7,1},{8,14},{9,15},{10,... | collective-permute-start | bytes 196616 | tf_op jit(solution)/shard_map/ppermute | solution.py:42
  103.9 5.6 %collective-permute-start.20 = (bf16[1024,128]{1,0:T(8,128)(2,1)S(1)}, bf16[1024,128]{1,0:T(8,128)(2,1)S(1)}, u32[]{:S(2)}, u32[]{:S(2)}) collective-permute-start(bf16[1024,128]{1,0:T(8,128)(2,1)S(1)} %get-tuple-element.27), channel_id=1, source_target_pairs={{0,16},{1,17},{2,18},{3,19},{4,20},{5,21},{6,22},{7,23},{8,24},{9,... | collective-permute-start | bytes 786440 | tf_op jit(solution)/shard_map/ppermute | solution.py:42
  109.6 10.6 %collective-permute-start.21 = (bf16[2048,128]{1,0:T(8,128)(2,1)S(1)}, bf16[2048,128]{1,0:T(8,128)(2,1)S(1)}, u32[]{:S(2)}, u32[]{:S(2)}) collective-permute-start(bf16[2048,128]{1,0:T(8,128)(2,1)S(1)} %get-tuple-element.19), channel_id=1, source_target_pairs={{0,1},{1,0},{2,3},{3,2},{4,5},{5,4},{6,7},{7,6},{8,9},{9,8},{10,11... | collective-permute-start | bytes 1572872 | tf_op jit(solution)/shard_map/ppermute | solution.py:42
  112.9 1.7 %collective-permute-start.22 = (bf16[3,128,128]{2,1,0:T(8,128)(2,1)S(1)}, bf16[3,128,128]{2,1,0:T(8,128)(2,1)S(1)}, u32[]{:S(2)}, u32[]{:S(2)}) collective-permute-start(bf16[3,128,128]{2,1,0:T(8,128)(2,1)S(1)} %get-tuple-element.14), channel_id=1, source_target_pairs={{0,1},{1,0},{2,3},{3,2},{4,5},{5,4},{6,7},{7,6},{8,9},{9,8},{10,11... | collective-permute-start | bytes 294920 | tf_op jit(solution)/shard_map/ppermute | solution.py:42
  113.0 4.1 %collective-permute-start.23 = (bf16[3,128,128]{2,1,0:T(8,128)(2,1)S(1)}, bf16[3,128,128]{2,1,0:T(8,128)(2,1)S(1)}, u32[]{:S(2)}, u32[]{:S(2)}) collective-permute-start(bf16[3,128,128]{2,1,0:T(8,128)(2,1)S(1)} %get-tuple-element.13), channel_id=1, source_target_pairs={{0,31},{1,2},{2,1},{3,4},{4,3},{5,6},{6,5},{7,8},{8,7},{9,10},{10,... | collective-permute-start | bytes 294920 | tf_op jit(solution)/shard_map/ppermute | solution.py:42
  (8 other events, 140.3 us)

commit v2 on v0

v2 whole, which is shorter than its diff:
```python
import functools

import jax
import jax.numpy as jnp
from jax import lax
from jax.experimental import pallas as pl
from jax.experimental.pallas import tpu as pltpu
from jax.sharding import PartitionSpec as P

BAND = 3
LAYERS = 3
BLOCK = 128
STEP = 4
DEVICES = 32


def index_of(x, z, c):
    return x * 16 + z * 2 + c


def permutation(move):
    return [
        (index_of(x, z, c), index_of(*move(x, z, c)))
        for x in range(2)
        for z in range(8)
        for c in range(2)
    ]


def along_z(step):
    return permutation(lambda x, z, c: (x, z ^ step, c))


ACROSS_X = permutation(lambda x, z, c: (1 - x, z, c))
ACROSS_CORE = permutation(lambda x, z, c: (x, z, 1 - c))
ACROSS_EDGE = [
    (i, (i + 1) % DEVICES if i % 2 else (i - 1) % DEVICES) for i in range(DEVICES)
]


def permute(array, pairs):
    return lax.ppermute(array, "row", pairs)


def places(hub_blocks, me):
    delta = hub_blocks ^ me
    dx, dz, dc = delta >> 4, (delta >> 1) & 7, delta & 1
    s = dz >> 2
    g = (dz & 3) ^ (2 * s)
    return 16 * dc + 8 * dx + 2 * g + s


def dot(a, b):
    return jnp.dot(a, b, preferred_element_type=jnp.float32)


def id_columns(ids_ref, level, first):
    row = ids_ref[level : level + 1, :] - first
    return jnp.transpose(jnp.broadcast_to(row, (BLOCK, BLOCK)))


def one_hot(ids, first, count):
    column = lax.broadcasted_iota(jnp.int32, (BLOCK, BLOCK), 1) + first
    parts = [(column + i * BLOCK == ids).astype(jnp.bfloat16) for i in range(count)]
    return jnp.concatenate(parts, axis=1)


def call(kernel, out_shape, scalars, arrays, flops, scratch=()):
    smem = pl.BlockSpec(memory_space=pltpu.SMEM)
    vmem = pl.BlockSpec(memory_space=pltpu.VMEM)
    moved = sum(a.size * a.dtype.itemsize for a in arrays)
    return pl.pallas_call(
        kernel,
        in_specs=[smem] * len(scalars) + [vmem] * len(arrays),
        out_specs=jax.tree.map(lambda _: vmem, out_shape),
        out_shape=out_shape,
        scratch_shapes=list(scratch),
        compiler_params=pltpu.CompilerParams(vmem_limit_bytes=40 * 2**20),
        cost_estimate=pl.CostEstimate(flops=flops, bytes_accessed=moved, transcendentals=0),
    )(*scalars, *arrays)


def f32(*shape):
    return jax.ShapeDtypeStruct(shape, jnp.float32)


def bf16(*shape):
    return jax.ShapeDtypeStruct(shape, jnp.bfloat16)


def pick_kernel(side_ref, ids_ref, table_ref, out_ref):
    ids = id_columns(ids_ref, 0, side_ref[3])
    total = jnp.zeros(out_ref.shape, jnp.float32)
    for b in range(0, table_ref.shape[0], STEP):
        table = table_ref[b : b + STEP].reshape(STEP * BLOCK, -1)
        total += dot(one_hot(ids, b * BLOCK, STEP), table)
    out_ref[...] = total.astype(out_ref.dtype)


def expand_kernel(side_ref, place_ref, ids_ref, tiles_ref, *out_refs):
    columns = [id_columns(ids_ref, level + 1, side_ref[3]) for level in range(len(out_refs))]
    for out_ref in out_refs:
        out_ref[...] = jnp.zeros_like(out_ref)

    def group(step, carry):
        for i in range(STEP):
            b = step * STEP + i
            rows = jnp.concatenate([one_hot(c, b * BLOCK, 1) for c in columns], axis=0)
            tiles = jnp.concatenate([tiles_ref[b, k] for k in range(4)], axis=1)
            taken = dot(rows, tiles).astype(jnp.bfloat16)
            for k in range(4):
                place = place_ref[b * 4 + k]
                for n, out_ref in enumerate(out_refs):
                    part = taken[n * BLOCK : (n + 1) * BLOCK, k * BLOCK : (k + 1) * BLOCK]
                    out_ref[place] += part
        return carry

    lax.fori_loop(0, tiles_ref.shape[0] // STEP, group, 0)


def tile_sum(b, tiles_ref, blocks):
    tiles = jnp.concatenate([tiles_ref[b, k] for k in range(4)], axis=1)
    return dot(tiles, jnp.concatenate(blocks, axis=0))


def band_kernel(level, offsets_ref, side_ref, table_ref, inner_ref, outer_ref, tiles_ref, ids_ref, *rest):
    out_ref, padded = rest[0], rest[-1]
    blocks = table_ref.shape[0]
    padded[BAND : BAND + blocks] = table_ref[...]
    core, has_left, has_right = side_ref[0], side_ref[1], side_ref[2]
    inner, outer = inner_ref[...], outer_ref[...]
    left = jnp.where(core == 0, outer, inner)
    right = jnp.where(core == 0, inner, outer)
    padded[0:BAND] = jnp.where(has_left == 1, left, jnp.zeros_like(left))
    padded[BAND + blocks :] = jnp.where(has_right == 1, right, jnp.zeros_like(right))
    if level is not None:
        ids = id_columns(ids_ref, level, side_ref[3])
        rest[1][...] = jnp.zeros_like(rest[1])

    def group(step, carry):
        values = []
        for i in range(STEP):
            b = step * STEP + i
            near = [padded[b + BAND + offsets_ref[b * 4 + k]] for k in range(4)]
            values.append(tile_sum(b, tiles_ref, near))
            out_ref[b] = values[-1]
        if level is not None:
            value = jnp.concatenate(values, axis=0)
            high = value.astype(jnp.bfloat16)
            low = (value - high.astype(jnp.float32)).astype(jnp.bfloat16)
            hot = one_hot(ids, step * STEP * BLOCK, STEP)
            both = dot(hot, jnp.concatenate([high, low], axis=1))
            rest[1][...] += both[:, :BLOCK] + both[:, BLOCK:]
        return carry

    lax.fori_loop(0, blocks // STEP, group, 0)


def band_products(level, offsets, side, table, inner, outer, tiles, ids):
    blocks = table.shape[0]
    return call(
        functools.partial(band_kernel, level),
        [f32(blocks, BLOCK, BLOCK)] + ([] if level is None else [f32(BLOCK, BLOCK)]),
        (offsets, side),
        (table, inner, outer, tiles, ids),
        2**29,
        [pltpu.VMEM((blocks + 2 * BAND, BLOCK, BLOCK), jnp.bfloat16)],
    )


def hub_kernel(place_ref, p0_ref, p1_ref, p2_ref, p3_ref, tiles_ref, band_ref, *rest):
    out_ref, panel = rest[-2], rest[-1]
    earlier = rest[:-2]
    for n, ref in enumerate((p0_ref, p1_ref, p2_ref, p3_ref)):
        panel[8 * n : 8 * n + 8] = ref[...].reshape(8, BLOCK, BLOCK)

    def group(step, carry):
        for i in range(STEP):
            b = step * STEP + i
            near = [panel[place_ref[b * 4 + k]] for k in range(4)]
            value = (tile_sum(b, tiles_ref, near) + band_ref[b]).astype(jnp.bfloat16)
            if earlier:
                total = value.astype(jnp.float32)
                for ref in earlier:
                    total = total + ref[b].astype(jnp.float32)
                value = (total * 0.25).astype(jnp.bfloat16)
            out_ref[b] = value
        return carry

    lax.fori_loop(0, tiles_ref.shape[0] // STEP, group, 0)


def hub_layer(place, pieces, tiles, band, earlier=()):
    blocks = tiles.shape[0]
    return call(
        hub_kernel,
        bf16(blocks, BLOCK, BLOCK),
        (place,),
        (*pieces, tiles, band, *earlier),
        2**29,
        [pltpu.VMEM((DEVICES, BLOCK, BLOCK), jnp.bfloat16)],
    )


def row_sum(spread_ref, first, piece_ref):
    spread = jnp.concatenate([spread_ref[first + i] for i in range(8)], axis=1)
    return dot(spread, piece_ref[...])


def part_kernel(near_ref, spread_ref, p0_ref, p1_ref, p2_ref, out_ref):
    total = near_ref[...]
    for n, ref in enumerate((p0_ref, p1_ref, p2_ref)):
        total += row_sum(spread_ref, 8 * n, ref)
    out_ref[...] = total


def close_kernel(part_ref, spread_ref, p3_ref, out_ref):
    out_ref[...] = (part_ref[...] + row_sum(spread_ref, 24, p3_ref)).astype(jnp.bfloat16)


def together(*arrays):
    return lax.optimization_barrier(arrays)


def body(embeddings, band_tiles, band_offsets, hub_tiles, hub_blocks, hub_ids):
    rows_dev, features = embeddings.shape
    blocks = rows_dev // BLOCK
    me = lax.axis_index("row")
    core = me % 2
    side = jnp.stack([core, (me > 0).astype(jnp.int32), (me < DEVICES - 1).astype(jnp.int32), me * rows_dev])
    offsets = band_offsets.reshape(-1)
    place = places(hub_blocks, me).reshape(-1)

    def edges(table):
        inner = lax.dynamic_slice_in_dim(table, jnp.where(core == 0, blocks - BAND, 0), BAND)
        outer = lax.dynamic_slice_in_dim(table, jnp.where(core == 0, 0, blocks - BAND), BAND)
        return inner, outer

    tables = [embeddings.reshape(blocks, BLOCK, features)]
    picked = call(pick_kernel, bf16(BLOCK, features), (side,), (hub_ids, tables[0]), 2**27)
    pieces = band = None
    for level in range(LAYERS):
        last = level == LAYERS - 1
        if level == 0:
            picked, tiles, table = together(picked, hub_tiles, tables[0])
            across = permute(picked, along_z(6))
            spreads = call(
                expand_kernel,
                [bf16(DEVICES, BLOCK, BLOCK)] * (LAYERS - 1),
                (side, place),
                (hub_ids, tiles),
                2**30,
            )
            across, *spreads = together(across, *spreads)
        else:
            picked, band, *pieces = together(picked, band, *pieces)
            across = permute(picked, along_z(6))
            table = hub_layer(place, pieces, hub_tiles, band)
            across, table = together(across, table)
            tables.append(table)
        pair, table = together(jnp.concatenate([picked, across]), table)
        inner, outer = edges(table)
        inner = permute(inner, ACROSS_CORE)
        outer = permute(outer, ACROSS_EDGE)
        near = [permute(pair, along_z(g)) for g in (1, 2, 3)]
        inner, outer, *near = together(inner, outer, *near)
        column, inner, outer = together(jnp.concatenate([pair] + near), inner, outer)
        core_column = permute(column, ACROSS_CORE)
        x_column = permute(column, ACROSS_X)
        band, *rows = band_products(
            None if last else level + 1, offsets, side, table, inner, outer, band_tiles, hub_ids
        )
        core_column, x_column, band, *rows = together(core_column, x_column, band, *rows)
        far_column = permute(x_column, ACROSS_CORE)
        pieces = [column, x_column, core_column, far_column]
        if last:
            return hub_layer(place, pieces, hub_tiles, band, tables).reshape(rows_dev, features)
        spread = spreads[level]
        part = call(
            part_kernel, f32(BLOCK, features), (), (rows[0], spread, column, x_column, core_column), 2**27
        )
        picked = call(close_kernel, bf16(BLOCK, features), (), (part, spread, far_column), 2**25)


def solution(mesh):
    return jax.shard_map(
        body,
        mesh=mesh,
        in_specs=(
            P(("group", "row"), None),
            P(("group", "row"), None, None, None),
            P(("group", "row"), None),
            P(("group", "row"), None, None, None),
            P(("group", "row"), None),
            P(None, ("group", "row")),
        ),
        out_specs=P(("group", "row"), None),
        check_vma=False,
    )
```

time: 246 us -> 98.7 us (0.40)
  waiting for transfers between devices: 147 us -> 24.7 us
  Pallas kernels: 0 us -> 30.4 us
  matrix products: 29.4 us -> 0 us
  local copies, waits for them, and re-layouts: 28.9 us -> 8.94 us
  starting transfers between devices: 18.2 us -> 33.2 us
  between operations: 13.3 us -> 0.26 us
  other arithmetic: 8.55 us -> 0.84 us
    all_gather x3 -> x0, waiting for transfers between devices: 142 us -> none  [propagate(): hub_panel = lax.all_gather(owned_hubs, 'row', axis=0, tiled=True)]
    pallas_call x0 -> x12, Pallas kernels: none -> 30.4 us  [call(): pl.pallas_call(kernel, in_specs=[smem] * len(scalars) + [vmem] * len(arra...]
    dot_general x6 -> x0, matrix products: 29.4 us -> none  [tile_products(): jnp.einsum('bkij,bkjf->bif', tiles, operands, preferred_element_type=jnp....]
    gather x9 -> x0, local copies, waits for them, and re-layouts: 26.6 us -> none  [the longest x3 12.8 us: propagate(): hub_near = hub_panel.reshape(-1, tile_rows, feature_count)[hub_blocks]]
    ppermute x6 -> x27, waiting for transfers between devices: 5.23 us -> 24.7 us  [permute(): return lax.ppermute(array, 'row', pairs)]
    ppermute x6 -> x27, starting transfers between devices: 18.2 us -> 33.2 us  [permute(): return lax.ppermute(array, 'row', pairs)]
    unnamed x4 -> x25, local copies, waits for them, and re-layouts: 0.01 us -> 8.59 us
    select_n x5 -> x0, other arithmetic: 3.48 us -> none  [the longest x3 2.11 us: propagate(): owned_hubs = jnp.take(current, local_ids, axis=0)]
  transfers between devices with their start and end apart: 9 -> 27, of which waited for: 8 -> 13; matrix products, arithmetic and copies ran while one was open for 12% -> 1% of each run, Pallas kernels for 0% -> 25%
where the time goes in v2:
time: 98.7 us; the launch traced here: 98.4 us
  starting transfers between devices  33.2 us (34%)
  Pallas kernels  30.4 us (31%)
  waiting for transfers between devices  24.7 us (25%)
  local copies, waits for them, and re-layouts  8.94 us (9%)
    ppermute x27, starting transfers between devices, permute(): return lax.ppermute(array, 'row', pairs)  33.2 us
    pallas_call x12, Pallas kernels, call(): pl.pallas_call(kernel, in_specs=[smem] * len(scalars) + [vmem] * len(arra...  30.4 us
    ppermute x27, waiting for transfers between devices, permute(): return lax.ppermute(array, 'row', pairs)  24.7 us
    unnamed x25, local copies, waits for them, and re-layouts  8.59 us
  transfers between devices with their start and end apart: 27, of which 13 were waited for; matrix products, arithmetic and copies ran while one was open for 1% of the time, Pallas kernels for 25%

profile of v2, /device:TPU:1, one launch (start us, length us, event | category | flops | bytes accessed | tf_op | source)
XLA Modules:
  0.0 98.4 jit_solution(13602691884609940003)
XLA Ops:
  3.0 6.9 %collective-permute-start = (bf16[128,128]{1,0:T(8,128)(2,1)S(1)}, bf16[128,128]{1,0:T(8,128)(2,1)S(1)}, u32[]{:S(2)}, u32[]{:S(2)}) collective-permute-start(bf16[128,128]{1,0:T(8,128)(2,1)S(1)} %shard_map.64), channel_id=1, source_target_pairs={{0,12},{1,13},{2,14},{3,15},{4,8},{5,9},{6,10},{7,11},{8,4},{9,5},... | collective-permute-start | bytes 98312 | tf_op jit(solution)/shard_map/ppermute | solution.py:42
  10.9 2.2 %copy-done = bf16[32,4,128,128]{3,2,1,0:T(8,128)(2,1)S(1)} copy-done((bf16[32,4,128,128]{3,2,1,0:T(8,128)(2,1)S(1)}, bf16[32,4,128,128]{3,2,1,0:T(8,128)(2,1)}, u32[]{:S(2)}) %copy-start) | copy-done | bytes 4194328
  13.7 4.4 %shard_map.65 = (bf16[32,128,128]{2,1,0:T(8,128)(2,1)S(1)}, bf16[32,128,128]{2,1,0:T(8,128)(2,1)S(1)}) custom-call(s32[4]{0:T(128)S(1)} %pad_add_fusion.side_ref, s32[128]{0:T(128)S(1)} %reshape.12.place_ref, s32[3,128]{1,0:T(4,128)S(1)} %copy-done.9, bf16[32,4,128,128]{3,2,1,0:T(8,128)(2,1)S(1)} %copy-done), custom_call_target="tpu_custom_call" | custom-call | flops 1073741824 | bytes 4195840 | tf_op jit(solution)/shard_map/pallas_call | solution.py:72
  18.2 1.7 %collective-permute-start.2 = (bf16[3,128,128]{2,1,0:T(8,128)(2,1)S(1)}, bf16[3,128,128]{2,1,0:T(8,128)(2,1)S(1)}, u32[]{:S(2)}, u32[]{:S(2)}) collective-permute-start(bf16[3,128,128]{2,1,0:T(8,128)(2,1)S(1)} %get-tuple-element.147), channel_id=1, source_target_pairs={{0,31},{1,2},{2,1},{3,4},{4,3},{5,6},{6,5},{7,8},{8,7},{9,10},{10,... | collective-permute-start | bytes 294920 | tf_op jit(solution)/shard_map/ppermute | solution.py:42
  21.8 1.6 %collective-permute-start.3 = (bf16[256,128]{1,0:T(8,128)(2,1)S(1)}, bf16[256,128]{1,0:T(8,128)(2,1)S(1)}, u32[]{:S(2)}, u32[]{:S(2)}) collective-permute-start(bf16[256,128]{1,0:T(8,128)(2,1)S(1)} %pad_maximum_fusion.3), channel_id=1, source_target_pairs={{0,2},{1,3},{2,0},{3,1},{4,6},{5,7},{6,4},{7,5},{8,10},{9,11},{10,... | collective-permute-start | bytes 196616 | tf_op jit(solution)/shard_map/ppermute | solution.py:42
  23.5 1.6 %collective-permute-done.5 = bf16[256,128]{1,0:T(8,128)(2,1)S(1)} collective-permute-done((bf16[256,128]{1,0:T(8,128)(2,1)S(1)}, bf16[256,128]{1,0:T(8,128)(2,1)S(1)}, u32[]{:S(2)}, u32[]{:S(2)}) %collective-permute-start.5) | collective-permute-done | bytes 65568 | tf_op jit(solution)/shard_map/ppermute | solution.py:42
  25.0 3.6 %collective-permute-done.4 = bf16[256,128]{1,0:T(8,128)(2,1)S(1)} collective-permute-done((bf16[256,128]{1,0:T(8,128)(2,1)S(1)}, bf16[256,128]{1,0:T(8,128)(2,1)S(1)}, u32[]{:S(2)}, u32[]{:S(2)}) %collective-permute-start.4) | collective-permute-done | bytes 65568 | tf_op jit(solution)/shard_map/ppermute | solution.py:42
  31.8 2.2 %copy-done.2 = bf16[32,4,128,128]{3,2,1,0:T(8,128)(2,1)S(1)} copy-done((bf16[32,4,128,128]{3,2,1,0:T(8,128)(2,1)S(1)}, bf16[32,4,128,128]{3,2,1,0:T(8,128)(2,1)}, u32[]{:S(2)}) %copy-start.2) | copy-done | bytes 4194328
  34.9 4.6 %shard_map.66 = (f32[32,128,128]{2,1,0:T(8,128)S(1)}, f32[128,128]{1,0:T(8,128)S(1)}) custom-call(s32[128]{0:T(128)S(1)} %reshape.14.offsets_ref, s32[4]{0:T(128)S(1)} %pad_add_fusion.side_ref, bf16[32,128,128]{2,1,0:T(8,128)(2,1)S(1)} %bitcast.8, bf16[3,128,128]{2,1,0:T(8,128)(2,1)S(1)} %copy-done.7, ...), custom_call_target="tpu_custom_call" | custom-call | flops 536870912 | bytes 5441024 | tf_op jit(solution)/shard_map/pallas_call | solution.py:72
  42.7 3.6 %shard_map.69.table_ref.rest_1_ = bf16[32,128,128]{2,1,0:T(8,128)(2,1)S(1)} custom-call(s32[128]{0:T(128)S(1)} %reshape.12.place_ref, bf16[1024,128]{1,0:T(8,128)(2,1)S(1)} %pad_maximum_fusion.p0_ref, bf16[1024,128]{1,0:T(8,128)(2,1)} %collective-permute-done.7.p1_ref, bf16[1024,128]{1,0:T(8,128)(2,1)} %collective-permute-done.6.p2_ref, ...), custom_call_target="tpu_custom_call" | custom-call | flops 536870912 | bytes 7340032 | tf_op jit(solution)/shard_map/pallas_call | solution.py:72
  46.6 2.0 %collective-permute-start.11 = (bf16[3,128,128]{2,1,0:T(8,128)(2,1)S(1)}, bf16[3,128,128]{2,1,0:T(8,128)(2,1)S(1)}, u32[]{:S(2)}, u32[]{:S(2)}) collective-permute-start(bf16[3,128,128]{2,1,0:T(8,128)(2,1)S(1)} %get-tuple-element.145), channel_id=1, source_target_pairs={{0,31},{1,2},{2,1},{3,4},{4,3},{5,6},{6,5},{7,8},{8,7},{9,10},{10,... | collective-permute-start | bytes 294920 | tf_op jit(solution)/shard_map/ppermute | solution.py:42
  49.0 1.6 %collective-permute-start.14 = (bf16[256,128]{1,0:T(8,128)(2,1)S(1)}, bf16[256,128]{1,0:T(8,128)(2,1)S(1)}, u32[]{:S(2)}, u32[]{:S(2)}) collective-permute-start(bf16[256,128]{1,0:T(8,128)(2,1)S(1)} %pad_maximum_fusion.4), channel_id=1, source_target_pairs={{0,6},{1,7},{2,4},{3,5},{4,2},{5,3},{6,0},{7,1},{8,14},{9,15},{10,... | collective-permute-start | bytes 196616 | tf_op jit(solution)/shard_map/ppermute | solution.py:42
  50.7 1.9 %collective-permute-start.12 = (bf16[256,128]{1,0:T(8,128)(2,1)S(1)}, bf16[256,128]{1,0:T(8,128)(2,1)S(1)}, u32[]{:S(2)}, u32[]{:S(2)}) collective-permute-start(bf16[256,128]{1,0:T(8,128)(2,1)S(1)} %pad_maximum_fusion.4), channel_id=1, source_target_pairs={{0,2},{1,3},{2,0},{3,1},{4,6},{5,7},{6,4},{7,5},{8,10},{9,11},{10,... | collective-permute-start | bytes 196616 | tf_op jit(solution)/shard_map/ppermute | solution.py:42
  52.6 2.0 %collective-permute-done.14 = bf16[256,128]{1,0:T(8,128)(2,1)S(1)} collective-permute-done((bf16[256,128]{1,0:T(8,128)(2,1)S(1)}, bf16[256,128]{1,0:T(8,128)(2,1)S(1)}, u32[]{:S(2)}, u32[]{:S(2)}) %collective-permute-start.14) | collective-permute-done | bytes 65568 | tf_op jit(solution)/shard_map/ppermute | solution.py:42
  54.6 3.2 %collective-permute-done.13 = bf16[256,128]{1,0:T(8,128)(2,1)S(1)} collective-permute-done((bf16[256,128]{1,0:T(8,128)(2,1)S(1)}, bf16[256,128]{1,0:T(8,128)(2,1)S(1)}, u32[]{:S(2)}, u32[]{:S(2)}) %collective-permute-start.13) | collective-permute-done | bytes 65568 | tf_op jit(solution)/shard_map/ppermute | solution.py:42
  59.4 4.6 %shard_map.70 = (f32[32,128,128]{2,1,0:T(8,128)S(1)}, f32[128,128]{1,0:T(8,128)S(1)}) custom-call(s32[128]{0:T(128)S(1)} %reshape.14.offsets_ref, s32[4]{0:T(128)S(1)} %pad_add_fusion.side_ref, bf16[32,128,128]{2,1,0:T(8,128)(2,1)S(1)} %shard_map.69.table_ref.rest_1_, bf16[3,128,128]{2,1,0:T(8,128)(2,1)S(1)} %collective-permute-done.10.inner_ref, ...), custom_call_target="tpu_custom_call" | custom-call | flops 536870912 | bytes 5441024 | tf_op jit(solution)/shard_map/pallas_call | solution.py:72
  68.2 2.9 %shard_map.73.table_ref.rest_2_ = bf16[32,128,128]{2,1,0:T(8,128)(2,1)S(1)} custom-call(s32[128]{0:T(128)S(1)} %reshape.12.place_ref, bf16[1024,128]{1,0:T(8,128)(2,1)S(1)} %pad_maximum_fusion.1.p0_ref, bf16[1024,128]{1,0:T(8,128)(2,1)S(1)} %collective-permute-done.16.p1_ref, bf16[1024,128]{1,0:T(8,128)(2,1)S(1)} %collective-permute-done.15.p2_ref, ...), custom_call_target="tpu_custom_call" | custom-call | flops 536870912 | bytes 7340032 | tf_op jit(solution)/shard_map/pallas_call | solution.py:72
  71.1 1.9 %collective-permute-done.18 = bf16[128,128]{1,0:T(8,128)(2,1)S(1)} collective-permute-done((bf16[128,128]{1,0:T(8,128)(2,1)S(1)}, bf16[128,128]{1,0:T(8,128)(2,1)S(1)}, u32[]{:S(2)}, u32[]{:S(2)}) %collective-permute-start.18) | collective-permute-done | bytes 32800 | tf_op jit(solution)/shard_map/ppermute | solution.py:42
  77.0 2.3 %collective-permute-start.21 = (bf16[256,128]{1,0:T(8,128)(2,1)S(1)}, bf16[256,128]{1,0:T(8,128)(2,1)S(1)}, u32[]{:S(2)}, u32[]{:S(2)}) collective-permute-start(bf16[256,128]{1,0:T(8,128)(2,1)S(1)} %pad_maximum_fusion.5), channel_id=1, source_target_pairs={{0,2},{1,3},{2,0},{3,1},{4,6},{5,7},{6,4},{7,5},{8,10},{9,11},{10,... | collective-permute-start | bytes 196616 | tf_op jit(solution)/shard_map/ppermute | solution.py:42
  79.3 2.0 %collective-permute-done.23 = bf16[256,128]{1,0:T(8,128)(2,1)S(1)} collective-permute-done((bf16[256,128]{1,0:T(8,128)(2,1)S(1)}, bf16[256,128]{1,0:T(8,128)(2,1)S(1)}, u32[]{:S(2)}, u32[]{:S(2)}) %collective-permute-start.23) | collective-permute-done | bytes 65568 | tf_op jit(solution)/shard_map/ppermute | solution.py:42
  81.3 3.1 %collective-permute-done.22 = bf16[256,128]{1,0:T(8,128)(2,1)S(1)} collective-permute-done((bf16[256,128]{1,0:T(8,128)(2,1)S(1)}, bf16[256,128]{1,0:T(8,128)(2,1)S(1)}, u32[]{:S(2)}, u32[]{:S(2)}) %collective-permute-start.22) | collective-permute-done | bytes 65568 | tf_op jit(solution)/shard_map/ppermute | solution.py:42
  85.5 3.0 %shard_map.74.band_ref = f32[32,128,128]{2,1,0:T(8,128)S(1)} custom-call(s32[128]{0:T(128)S(1)} %reshape.14.offsets_ref, s32[4]{0:T(128)S(1)} %pad_add_fusion.side_ref, bf16[32,128,128]{2,1,0:T(8,128)(2,1)S(1)} %shard_map.73.table_ref.rest_2_, bf16[3,128,128]{2,1,0:T(8,128)(2,1)S(1)} %collective-permute-done.19.inner_ref, ...), custom_call_target="tpu_custom_call" | custom-call | flops 536870912 | bytes 5441024 | tf_op jit(solution)/shard_map/pallas_call | solution.py:72
  88.5 3.3 %collective-permute-done.25.p1_ref = bf16[1024,128]{1,0:T(8,128)(2,1)S(1)} collective-permute-done((bf16[1024,128]{1,0:T(8,128)(2,1)S(1)}, bf16[1024,128]{1,0:T(8,128)(2,1)S(1)}, u32[]{:S(2)}, u32[]{:S(2)}) %collective-permute-start.25) | collective-permute-done | bytes 262176 | tf_op jit(solution)/shard_map/ppermute | solution.py:42
  94.4 4.0 %shard_map.75 = bf16[32,128,128]{2,1,0:T(8,128)(2,1)} custom-call(s32[128]{0:T(128)S(1)} %reshape.12.place_ref, bf16[1024,128]{1,0:T(8,128)(2,1)S(1)} %pad_maximum_fusion.2.p0_ref, bf16[1024,128]{1,0:T(8,128)(2,1)S(1)} %collective-permute-done.25.p1_ref, bf16[1024,128]{1,0:T(8,128)(2,1)S(1)} %collective-permute-done.24.p2_ref, ...), custom_call_target="tpu_custom_call" | custom-call | flops 536870912 | bytes 10485760 | tf_op jit(solution)/shard_map/pallas_call | solution.py:72
  (81 shorter events, 27.8 us)
Async XLA Ops:
  3.0 15.2 %collective-permute-start = (bf16[128,128]{1,0:T(8,128)(2,1)S(1)}, bf16[128,128]{1,0:T(8,128)(2,1)S(1)}, u32[]{:S(2)}, u32[]{:S(2)}) collective-permute-start(bf16[128,128]{1,0:T(8,128)(2,1)S(1)} %shard_map.64), channel_id=1, source_target_pairs={{0,12},{1,13},{2,14},{3,15},{4,8},{5,9},{6,10},{7,11},{8,4},{9,5},... | collective-permute-start | bytes 98312 | tf_op jit(solution)/shard_map/ppermute | solution.py:42
  18.2 10.5 %collective-permute-start.2 = (bf16[3,128,128]{2,1,0:T(8,128)(2,1)S(1)}, bf16[3,128,128]{2,1,0:T(8,128)(2,1)S(1)}, u32[]{:S(2)}, u32[]{:S(2)}) collective-permute-start(bf16[3,128,128]{2,1,0:T(8,128)(2,1)S(1)} %get-tuple-element.147), channel_id=1, source_target_pairs={{0,31},{1,2},{2,1},{3,4},{4,3},{5,6},{6,5},{7,8},{8,7},{9,10},{10,... | collective-permute-start | bytes 294920 | tf_op jit(solution)/shard_map/ppermute | solution.py:42
  19.9 8.8 %collective-permute-start.1 = (bf16[3,128,128]{2,1,0:T(8,128)(2,1)S(1)}, bf16[3,128,128]{2,1,0:T(8,128)(2,1)S(1)}, u32[]{:S(2)}, u32[]{:S(2)}) collective-permute-start(bf16[3,128,128]{2,1,0:T(8,128)(2,1)S(1)} %get-tuple-element.148), channel_id=1, source_target_pairs={{0,1},{1,0},{2,3},{3,2},{4,5},{5,4},{6,7},{7,6},{8,9},{9,8},{10,11... | collective-permute-start | bytes 294920 | tf_op jit(solution)/shard_map/ppermute | solution.py:42
  19.9 5.1 %collective-permute-start.5 = (bf16[256,128]{1,0:T(8,128)(2,1)S(1)}, bf16[256,128]{1,0:T(8,128)(2,1)S(1)}, u32[]{:S(2)}, u32[]{:S(2)}) collective-permute-start(bf16[256,128]{1,0:T(8,128)(2,1)S(1)} %pad_maximum_fusion.3), channel_id=1, source_target_pairs={{0,6},{1,7},{2,4},{3,5},{4,2},{5,3},{6,0},{7,1},{8,14},{9,15},{10,... | collective-permute-start | bytes 196616 | tf_op jit(solution)/shard_map/ppermute | solution.py:42
  21.1 7.6 %collective-permute-start.4 = (bf16[256,128]{1,0:T(8,128)(2,1)S(1)}, bf16[256,128]{1,0:T(8,128)(2,1)S(1)}, u32[]{:S(2)}, u32[]{:S(2)}) collective-permute-start(bf16[256,128]{1,0:T(8,128)(2,1)S(1)} %pad_maximum_fusion.3), channel_id=1, source_target_pairs={{0,4},{1,5},{2,6},{3,7},{4,0},{5,1},{6,2},{7,3},{8,12},{9,13},{10,... | collective-permute-start | bytes 196616 | tf_op jit(solution)/shard_map/ppermute | solution.py:42
  21.8 6.9 %collective-permute-start.3 = (bf16[256,128]{1,0:T(8,128)(2,1)S(1)}, bf16[256,128]{1,0:T(8,128)(2,1)S(1)}, u32[]{:S(2)}, u32[]{:S(2)}) collective-permute-start(bf16[256,128]{1,0:T(8,128)(2,1)S(1)} %pad_maximum_fusion.3), channel_id=1, source_target_pairs={{0,2},{1,3},{2,0},{3,1},{4,6},{5,7},{6,4},{7,5},{8,10},{9,11},{10,... | collective-permute-start | bytes 196616 | tf_op jit(solution)/shard_map/ppermute | solution.py:42
  29.4 10.1 %collective-permute-start.7 = (bf16[1024,128]{1,0:T(8,128)(2,1)S(1)}, bf16[1024,128]{1,0:T(8,128)(2,1)}, u32[]{:S(2)}, u32[]{:S(2)}) collective-permute-start(bf16[1024,128]{1,0:T(8,128)(2,1)S(1)} %pad_maximum_fusion.p0_ref), channel_id=1, source_target_pairs={{0,16},{1,17},{2,18},{3,19},{4,20},{5,21},{6,22},{7,23},{8,24},{9,... | collective-permute-start | bytes 786440 | tf_op jit(solution)/shard_map/ppermute | solution.py:42
  30.6 8.9 %collective-permute-start.6 = (bf16[1024,128]{1,0:T(8,128)(2,1)S(1)}, bf16[1024,128]{1,0:T(8,128)(2,1)}, u32[]{:S(2)}, u32[]{:S(2)}) collective-permute-start(bf16[1024,128]{1,0:T(8,128)(2,1)S(1)} %pad_maximum_fusion.p0_ref), channel_id=1, source_target_pairs={{0,1},{1,0},{2,3},{3,2},{4,5},{5,4},{6,7},{7,6},{8,9},{9,8},{10,11... | collective-permute-start | bytes 786440 | tf_op jit(solution)/shard_map/ppermute | solution.py:42
  41.6 5.0 %collective-permute-start.9 = (bf16[128,128]{1,0:T(8,128)(2,1)S(1)}, bf16[128,128]{1,0:T(8,128)(2,1)S(1)}, u32[]{:S(2)}, u32[]{:S(2)}) collective-permute-start(bf16[128,128]{1,0:T(8,128)(2,1)S(1)} %shard_map.68), channel_id=1, source_target_pairs={{0,12},{1,13},{2,14},{3,15},{4,8},{5,9},{6,10},{7,11},{8,4},{9,5},... | collective-permute-start | bytes 98312 | tf_op jit(solution)/shard_map/ppermute | solution.py:42
  46.6 11.3 %collective-permute-start.11 = (bf16[3,128,128]{2,1,0:T(8,128)(2,1)S(1)}, bf16[3,128,128]{2,1,0:T(8,128)(2,1)S(1)}, u32[]{:S(2)}, u32[]{:S(2)}) collective-permute-start(bf16[3,128,128]{2,1,0:T(8,128)(2,1)S(1)} %get-tuple-element.145), channel_id=1, source_target_pairs={{0,31},{1,2},{2,1},{3,4},{4,3},{5,6},{6,5},{7,8},{8,7},{9,10},{10,... | collective-permute-start | bytes 294920 | tf_op jit(solution)/shard_map/ppermute | solution.py:42
  48.5 9.3 %collective-permute-start.10 = (bf16[3,128,128]{2,1,0:T(8,128)(2,1)S(1)}, bf16[3,128,128]{2,1,0:T(8,128)(2,1)S(1)}, u32[]{:S(2)}, u32[]{:S(2)}) collective-permute-start(bf16[3,128,128]{2,1,0:T(8,128)(2,1)S(1)} %get-tuple-element.146), channel_id=1, source_target_pairs={{0,1},{1,0},{2,3},{3,2},{4,5},{5,4},{6,7},{7,6},{8,9},{9,8},{10,11... | collective-permute-start | bytes 294920 | tf_op jit(solution)/shard_map/ppermute | solution.py:42
  49.0 5.6 %collective-permute-start.14 = (bf16[256,128]{1,0:T(8,128)(2,1)S(1)}, bf16[256,128]{1,0:T(8,128)(2,1)S(1)}, u32[]{:S(2)}, u32[]{:S(2)}) collective-permute-start(bf16[256,128]{1,0:T(8,128)(2,1)S(1)} %pad_maximum_fusion.4), channel_id=1, source_target_pairs={{0,6},{1,7},{2,4},{3,5},{4,2},{5,3},{6,0},{7,1},{8,14},{9,15},{10,... | collective-permute-start | bytes 196616 | tf_op jit(solution)/shard_map/ppermute | solution.py:42
  50.7 7.1 %collective-permute-start.13 = (bf16[256,128]{1,0:T(8,128)(2,1)S(1)}, bf16[256,128]{1,0:T(8,128)(2,1)S(1)}, u32[]{:S(2)}, u32[]{:S(2)}) collective-permute-start(bf16[256,128]{1,0:T(8,128)(2,1)S(1)} %pad_maximum_fusion.4), channel_id=1, source_target_pairs={{0,4},{1,5},{2,6},{3,7},{4,0},{5,1},{6,2},{7,3},{8,12},{9,13},{10,... | collective-permute-start | bytes 196616 | tf_op jit(solution)/shard_map/ppermute | solution.py:42
  50.7 7.1 %collective-permute-start.12 = (bf16[256,128]{1,0:T(8,128)(2,1)S(1)}, bf16[256,128]{1,0:T(8,128)(2,1)S(1)}, u32[]{:S(2)}, u32[]{:S(2)}) collective-permute-start(bf16[256,128]{1,0:T(8,128)(2,1)S(1)} %pad_maximum_fusion.4), channel_id=1, source_target_pairs={{0,2},{1,3},{2,0},{3,1},{4,6},{5,7},{6,4},{7,5},{8,10},{9,11},{10,... | collective-permute-start | bytes 196616 | tf_op jit(solution)/shard_map/ppermute | solution.py:42
  57.9 7.6 %collective-permute-start.16 = (bf16[1024,128]{1,0:T(8,128)(2,1)S(1)}, bf16[1024,128]{1,0:T(8,128)(2,1)S(1)}, u32[]{:S(2)}, u32[]{:S(2)}) collective-permute-start(bf16[1024,128]{1,0:T(8,128)(2,1)S(1)} %pad_maximum_fusion.1.p0_ref), channel_id=1, source_target_pairs={{0,16},{1,17},{2,18},{3,19},{4,20},{5,21},{6,22},{7,23},{8,24},{9,... | collective-permute-start | bytes 786440 | tf_op jit(solution)/shard_map/ppermute | solution.py:42
  58.6 6.9 %collective-permute-start.15 = (bf16[1024,128]{1,0:T(8,128)(2,1)S(1)}, bf16[1024,128]{1,0:T(8,128)(2,1)S(1)}, u32[]{:S(2)}, u32[]{:S(2)}) collective-permute-start(bf16[1024,128]{1,0:T(8,128)(2,1)S(1)} %pad_maximum_fusion.1.p0_ref), channel_id=1, source_target_pairs={{0,1},{1,0},{2,3},{3,2},{4,5},{5,4},{6,7},{7,6},{8,9},{9,8},{10,11... | collective-permute-start | bytes 786440 | tf_op jit(solution)/shard_map/ppermute | solution.py:42
  68.1 5.0 %collective-permute-start.18 = (bf16[128,128]{1,0:T(8,128)(2,1)S(1)}, bf16[128,128]{1,0:T(8,128)(2,1)S(1)}, u32[]{:S(2)}, u32[]{:S(2)}) collective-permute-start(bf16[128,128]{1,0:T(8,128)(2,1)S(1)} %shard_map.72), channel_id=1, source_target_pairs={{0,12},{1,13},{2,14},{3,15},{4,8},{5,9},{6,10},{7,11},{8,4},{9,5},... | collective-permute-start | bytes 98312 | tf_op jit(solution)/shard_map/ppermute | solution.py:42
  73.0 11.3 %collective-permute-start.20 = (bf16[3,128,128]{2,1,0:T(8,128)(2,1)S(1)}, bf16[3,128,128]{2,1,0:T(8,128)(2,1)S(1)}, u32[]{:S(2)}, u32[]{:S(2)}) collective-permute-start(bf16[3,128,128]{2,1,0:T(8,128)(2,1)S(1)} %get-tuple-element.143), channel_id=1, source_target_pairs={{0,31},{1,2},{2,1},{3,4},{4,3},{5,6},{6,5},{7,8},{8,7},{9,10},{10,... | collective-permute-start | bytes 294920 | tf_op jit(solution)/shard_map/ppermute | solution.py:42
  74.3 10.1 %collective-permute-start.19 = (bf16[3,128,128]{2,1,0:T(8,128)(2,1)S(1)}, bf16[3,128,128]{2,1,0:T(8,128)(2,1)S(1)}, u32[]{:S(2)}, u32[]{:S(2)}) collective-permute-start(bf16[3,128,128]{2,1,0:T(8,128)(2,1)S(1)} %get-tuple-element.144), channel_id=1, source_target_pairs={{0,1},{1,0},{2,3},{3,2},{4,5},{5,4},{6,7},{7,6},{8,9},{9,8},{10,11... | collective-permute-start | bytes 294920 | tf_op jit(solution)/shard_map/ppermute | solution.py:42
  75.7 5.5 %collective-permute-start.23 = (bf16[256,128]{1,0:T(8,128)(2,1)S(1)}, bf16[256,128]{1,0:T(8,128)(2,1)S(1)}, u32[]{:S(2)}, u32[]{:S(2)}) collective-permute-start(bf16[256,128]{1,0:T(8,128)(2,1)S(1)} %pad_maximum_fusion.5), channel_id=1, source_target_pairs={{0,6},{1,7},{2,4},{3,5},{4,2},{5,3},{6,0},{7,1},{8,14},{9,15},{10,... | collective-permute-start | bytes 196616 | tf_op jit(solution)/shard_map/ppermute | solution.py:42
  77.0 7.4 %collective-permute-start.22 = (bf16[256,128]{1,0:T(8,128)(2,1)S(1)}, bf16[256,128]{1,0:T(8,128)(2,1)S(1)}, u32[]{:S(2)}, u32[]{:S(2)}) collective-permute-start(bf16[256,128]{1,0:T(8,128)(2,1)S(1)} %pad_maximum_fusion.5), channel_id=1, source_target_pairs={{0,4},{1,5},{2,6},{3,7},{4,0},{5,1},{6,2},{7,3},{8,12},{9,13},{10,... | collective-permute-start | bytes 196616 | tf_op jit(solution)/shard_map/ppermute | solution.py:42
  77.0 7.4 %collective-permute-start.21 = (bf16[256,128]{1,0:T(8,128)(2,1)S(1)}, bf16[256,128]{1,0:T(8,128)(2,1)S(1)}, u32[]{:S(2)}, u32[]{:S(2)}) collective-permute-start(bf16[256,128]{1,0:T(8,128)(2,1)S(1)} %pad_maximum_fusion.5), channel_id=1, source_target_pairs={{0,2},{1,3},{2,0},{3,1},{4,6},{5,7},{6,4},{7,5},{8,10},{9,11},{10,... | collective-permute-start | bytes 196616 | tf_op jit(solution)/shard_map/ppermute | solution.py:42
  84.4 7.5 %collective-permute-start.25 = (bf16[1024,128]{1,0:T(8,128)(2,1)S(1)}, bf16[1024,128]{1,0:T(8,128)(2,1)S(1)}, u32[]{:S(2)}, u32[]{:S(2)}) collective-permute-start(bf16[1024,128]{1,0:T(8,128)(2,1)S(1)} %pad_maximum_fusion.2.p0_ref), channel_id=1, source_target_pairs={{0,16},{1,17},{2,18},{3,19},{4,20},{5,21},{6,22},{7,23},{8,24},{9,... | collective-permute-start | bytes 786440 | tf_op jit(solution)/shard_map/ppermute | solution.py:42
  84.8 7.1 %collective-permute-start.24 = (bf16[1024,128]{1,0:T(8,128)(2,1)S(1)}, bf16[1024,128]{1,0:T(8,128)(2,1)S(1)}, u32[]{:S(2)}, u32[]{:S(2)}) collective-permute-start(bf16[1024,128]{1,0:T(8,128)(2,1)S(1)} %pad_maximum_fusion.2.p0_ref), channel_id=1, source_target_pairs={{0,1},{1,0},{2,3},{3,2},{4,5},{5,4},{6,7},{7,6},{8,9},{9,8},{10,11... | collective-permute-start | bytes 786440 | tf_op jit(solution)/shard_map/ppermute | solution.py:42
  (15 other events, 80.1 us)

commit v3 on v2

v3 whole, which is shorter than its diff:
```python
import functools

import jax
import jax.numpy as jnp
from jax import lax
from jax.experimental import pallas as pl
from jax.experimental.pallas import tpu as pltpu
from jax.sharding import PartitionSpec as P

BAND = 3
LAYERS = 3
BLOCK = 128
STEP = 16
CHUNK = 8
DEVICES = 32


def index_of(x, z, c):
    return x * 16 + z * 2 + c


def permutation(move):
    return [
        (index_of(x, z, c), index_of(*move(x, z, c)))
        for x in range(2)
        for z in range(8)
        for c in range(2)
    ]


def along_z(step):
    return permutation(lambda x, z, c: (x, z ^ step, c))


ACROSS_X = permutation(lambda x, z, c: (1 - x, z, c))
ACROSS_CORE = permutation(lambda x, z, c: (x, z, 1 - c))
ACROSS_EDGE = [
    (i, (i + 1) % DEVICES if i % 2 else (i - 1) % DEVICES) for i in range(DEVICES)
]


def permute(array, pairs):
    return lax.ppermute(array, "row", pairs)


def places(hub_blocks, me):
    delta = hub_blocks ^ me
    dx, dz, dc = delta >> 4, (delta >> 1) & 7, delta & 1
    s = dz >> 2
    g = (dz & 3) ^ (2 * s)
    return 16 * dc + 8 * dx + 2 * g + s


def dot(a, b):
    return jnp.dot(a, b, preferred_element_type=jnp.float32)


def id_columns(ids_ref, level, first):
    row = ids_ref[level : level + 1, :] - first
    return jnp.transpose(jnp.broadcast_to(row, (BLOCK, BLOCK)))


def one_hot(ids, first, count):
    column = lax.broadcasted_iota(jnp.int32, (BLOCK, BLOCK), 1) + first
    parts = [(column + i * BLOCK == ids).astype(jnp.bfloat16) for i in range(count)]
    return jnp.concatenate(parts, axis=1)


def call(kernel, out_shape, scalars, arrays, flops, scratch=()):
    smem = pl.BlockSpec(memory_space=pltpu.SMEM)
    vmem = pl.BlockSpec(memory_space=pltpu.VMEM)
    moved = sum(a.size * a.dtype.itemsize for a in arrays)
    return pl.pallas_call(
        kernel,
        in_specs=[smem] * len(scalars) + [vmem] * len(arrays),
        out_specs=jax.tree.map(lambda _: vmem, out_shape),
        out_shape=out_shape,
        scratch_shapes=list(scratch),
        compiler_params=pltpu.CompilerParams(vmem_limit_bytes=8 * 2**20),
        cost_estimate=pl.CostEstimate(flops=1, bytes_accessed=1, transcendentals=0),
    )(*scalars, *arrays)


def f32(*shape):
    return jax.ShapeDtypeStruct(shape, jnp.float32)


def bf16(*shape):
    return jax.ShapeDtypeStruct(shape, jnp.bfloat16)


def pick_kernel(side_ref, ids_ref, table_ref, out_ref, columns_ref):
    ids = id_columns(ids_ref, 0, side_ref[3])
    for level in range(1, LAYERS):
        columns_ref[level - 1] = id_columns(ids_ref, level, side_ref[3])
    total = jnp.zeros(out_ref.shape, jnp.float32)
    for b in range(0, table_ref.shape[0], CHUNK):
        table = table_ref[b : b + CHUNK].reshape(CHUNK * BLOCK, -1)
        total += dot(one_hot(ids, b * BLOCK, CHUNK), table)
    out_ref[...] = total.astype(out_ref.dtype)


def touch_kernel(*refs):
    refs[-1][...] = jnp.zeros_like(refs[-1])


def expand_kernel(level, place_ref, columns_ref, tiles_ref, out_ref):
    column = columns_ref[level]
    out_ref[...] = jnp.zeros_like(out_ref)

    def group(step, carry):
        for i in range(STEP):
            b = step * STEP + i
            tiles = jnp.concatenate([tiles_ref[b, k] for k in range(4)], axis=1)
            taken = dot(one_hot(column, b * BLOCK, 1), tiles).astype(jnp.bfloat16)
            for k in range(4):
                out_ref[place_ref[b * 4 + k]] += taken[:, k * BLOCK : (k + 1) * BLOCK]
        return carry

    lax.fori_loop(0, tiles_ref.shape[0] // STEP, group, 0)


def tile_sum(b, tiles_ref, blocks):
    tiles = jnp.concatenate([tiles_ref[b, k] for k in range(4)], axis=1)
    return dot(tiles, jnp.concatenate(blocks, axis=0))


def band_kernel(level, offsets_ref, side_ref, table_ref, inner_ref, outer_ref, tiles_ref, *rest):
    outs = 2 if level == 0 else 3
    extra, (out_ref, *more_refs, padded) = rest[:-outs], rest[-outs:]
    blocks = table_ref.shape[0]
    padded[BAND : BAND + blocks] = table_ref[...]
    core, has_left, has_right = side_ref[0], side_ref[1], side_ref[2]
    inner, outer = inner_ref[...], outer_ref[...]
    left = jnp.where(core == 0, outer, inner)
    right = jnp.where(core == 0, inner, outer)
    padded[0:BAND] = jnp.where(has_left == 1, left, jnp.zeros_like(left))
    padded[BAND + blocks :] = jnp.where(has_right == 1, right, jnp.zeros_like(right))
    pick_rows = 0 < level < LAYERS - 1
    more_ref = more_refs[0] if more_refs else None
    if pick_rows:
        ids = extra[0][level]
        more_ref[...] = jnp.zeros_like(more_ref)

    def group(step, carry):
        values = []
        for i in range(STEP):
            b = step * STEP + i
            near = [padded[b + BAND + offsets_ref[b * 4 + k]] for k in range(4)]
            values.append(tile_sum(b, tiles_ref, near))
            out_ref[b] = values[-1]
            if level == LAYERS - 1:
                total = table_ref[b].astype(jnp.float32)
                for ref in extra:
                    total = total + ref[b].astype(jnp.float32)
                more_ref[b] = total
        if pick_rows:
            value = jnp.concatenate(values, axis=0)
            high = value.astype(jnp.bfloat16)
            low = (value - high.astype(jnp.float32)).astype(jnp.bfloat16)
            hot = one_hot(ids, step * STEP * BLOCK, STEP)
            both = dot(hot, jnp.concatenate([high, low], axis=1))
            more_ref[...] += both[:, :BLOCK] + both[:, BLOCK:]
        return carry

    lax.fori_loop(0, blocks // STEP, group, 0)


def band_products(level, offsets, side, table, inner, outer, tiles, extra):
    blocks = table.shape[0]
    more = {0: [], LAYERS - 1: [f32(blocks, BLOCK, BLOCK)]}.get(level, [f32(BLOCK, BLOCK)])
    return call(
        functools.partial(band_kernel, level),
        [f32(blocks, BLOCK, BLOCK)] + more,
        (offsets, side),
        (table, inner, outer, tiles, *extra),
        2**29,
        [pltpu.VMEM((blocks + 2 * BAND, BLOCK, BLOCK), jnp.bfloat16)],
    )


def hub_kernel(mode, place_ref, tiles_ref, band_ref, *rest):
    panel = rest[-1]
    if mode == "pick":
        extra_ref, *pieces, out_ref, picked_ref, panel = rest
    elif mode == "mean":
        extra_ref, *pieces, out_ref, panel = rest
    else:
        *pieces, out_ref, panel = rest
    start = 0
    for ref in pieces:
        count = ref.shape[0] // BLOCK
        panel[start : start + count] = ref[...].reshape(count, BLOCK, BLOCK)
        start += count

    def group(step, total):
        values = []
        for i in range(STEP):
            b = step * STEP + i
            near = [panel[place_ref[b * 4 + k]] for k in range(4)]
            value = (tile_sum(b, tiles_ref, near) + band_ref[b]).astype(jnp.bfloat16)
            if mode == "mean":
                value = ((extra_ref[b] + value.astype(jnp.float32)) * 0.25).astype(jnp.bfloat16)
            out_ref[b] = value
            values.append(value)
        if mode == "pick":
            hot = one_hot(extra_ref[0], step * STEP * BLOCK, STEP)
            total = total + dot(hot, jnp.concatenate(values, axis=0))
        return total

    total = jnp.zeros((BLOCK, BLOCK), jnp.float32) if mode == "pick" else 0
    total = lax.fori_loop(0, tiles_ref.shape[0] // STEP, group, total)
    if mode == "pick":
        picked_ref[...] = total.astype(jnp.bfloat16)


def hub_layer(mode, place, pieces, tiles, band, *extra):
    out_shape = [bf16(tiles.shape[0], BLOCK, BLOCK)]
    if mode == "pick":
        out_shape.append(bf16(BLOCK, BLOCK))
    return call(
        functools.partial(hub_kernel, mode),
        out_shape,
        (place,),
        (tiles, band, *extra, *pieces),
        2**29,
        [pltpu.VMEM((DEVICES, BLOCK, BLOCK), jnp.bfloat16)],
    )


def row_sums(spread_ref, first, refs):
    total = None
    for ref in refs:
        count = ref.shape[0] // BLOCK
        spread = jnp.concatenate([spread_ref[first + i] for i in range(count)], axis=1)
        part = dot(spread, ref[...])
        total = part if total is None else total + part
        first += count
    return total


def part_kernel(near_ref, spread_ref, *rest):
    rest[-1][...] = near_ref[...] + row_sums(spread_ref, 0, rest[:-1])


def close_kernel(part_ref, spread_ref, piece_ref, out_ref):
    first = DEVICES - piece_ref.shape[0] // BLOCK
    out_ref[...] = (part_ref[...] + row_sums(spread_ref, first, [piece_ref])).astype(jnp.bfloat16)


def together(*arrays):
    return lax.optimization_barrier(arrays)


def body(embeddings, band_tiles, band_offsets, hub_tiles, hub_blocks, hub_ids):
    rows_dev, features = embeddings.shape
    blocks = rows_dev // BLOCK
    me = lax.axis_index("row")
    core = me % 2
    side = jnp.stack([core, (me > 0).astype(jnp.int32), (me < DEVICES - 1).astype(jnp.int32), me * rows_dev])
    offsets = band_offsets.reshape(-1)
    place = places(hub_blocks, me).reshape(-1)

    def edges(table):
        inner = lax.dynamic_slice_in_dim(table, jnp.where(core == 0, blocks - BAND, 0), BAND)
        outer = lax.dynamic_slice_in_dim(table, jnp.where(core == 0, 0, blocks - BAND), BAND)
        return inner, outer

    def exchange(rims):
        return [permute(rim, pairs) for rim, pairs in zip(rims, (ACROSS_CORE, ACROSS_EDGE))]

    table = embeddings.reshape(blocks, BLOCK, features)
    picked, columns = call(
        pick_kernel,
        [bf16(BLOCK, features), jax.ShapeDtypeStruct((LAYERS - 1, BLOCK, BLOCK), jnp.int32)],
        (side,),
        (hub_ids, table),
        2**27,
    )
    tables = [table]
    pieces = band = spread = None
    for level in range(LAYERS):
        if level == 1:
            picked, table = together(picked, table)
            across = permute(picked, along_z(6))
            halos = exchange(edges(table))
            across, *halos = together(across, *halos)
        elif level == 0:
            across = permute(picked, along_z(6))
        else:
            across = permute(picked, along_z(6))
            (table,) = hub_layer("", place, pieces, hub_tiles, band)
            across, table = together(across, table)
            tables.append(table)
        if level == 0:
            across, place, offsets = together(across, place, offsets)
        pair, columns = together(jnp.concatenate([picked, across]), columns)
        near = [permute(pair, along_z(g)) for g in (1, 2, 3)]
        if level == 0:
            held = call(touch_kernel, f32(8, BLOCK), (), (columns, hub_tiles, band_tiles), 2**20)
            near[1], held = together(near[1], held)
        elif level == 1:
            spread = call(
                functools.partial(expand_kernel, level),
                bf16(DEVICES, BLOCK, BLOCK),
                (place,),
                (columns, hub_tiles),
                2**29,
            )
            near[1], spread = together(near[1], spread)
        if level != 1:
            rims = edges(table)
            *near, rim_inner, rim_outer = together(*near, *rims)
            halos = exchange((rim_inner, rim_outer))
            (column,) = together(jnp.concatenate([pair] + near))
        else:
            column, *halos = together(jnp.concatenate([pair] + near), *halos)
        inner, outer = halos
        x_column = permute(column, ACROSS_X)
        core_column = permute(column, ACROSS_CORE)
        extra = ([held], [columns], tables[:-1])[level]
        band, *more = band_products(level, offsets, side, table, inner, outer, band_tiles, extra)
        x_column, core_column, band, *more = together(x_column, core_column, band, *more)
        far = permute(x_column, ACROSS_CORE)
        pieces = [column, x_column, core_column, far]
        if level == 0:
            table, picked = hub_layer("pick", place, pieces, hub_tiles, band, columns)
            tables.append(table)
            picked, columns, table = together(picked, columns, table)
        elif level == 1:
            part = call(part_kernel, f32(BLOCK, features), (), (more[0], spread, *pieces[:3]), 2**27)
            picked = call(close_kernel, bf16(BLOCK, features), (), (part, spread, far), 2**25)
            picked, band, *pieces = together(picked, band, *pieces)
    (averaged,) = hub_layer("mean", place, pieces, hub_tiles, band, more[0])
    return averaged.reshape(rows_dev, features)


def solution(mesh):
    return jax.shard_map(
        body,
        mesh=mesh,
        in_specs=(
            P(("group", "row"), None),
            P(("group", "row"), None, None, None),
            P(("group", "row"), None),
            P(("group", "row"), None, None, None),
            P(("group", "row"), None),
            P(None, ("group", "row")),
        ),
        out_specs=P(("group", "row"), None),
        check_vma=False,
    )
```

time: 98.7 us -> 93.5 us (0.947)
  starting transfers between devices: 33.2 us -> 46.7 us
  Pallas kernels: 30.4 us -> 18.6 us
  waiting for transfers between devices: 24.7 us -> 18.5 us
    ppermute x27, starting transfers between devices: 33.2 us -> 46.7 us  [permute(): return lax.ppermute(array, 'row', pairs)]
    pallas_call x12 -> x11, Pallas kernels: 30.4 us -> 18.6 us  [call(): pl.pallas_call(kernel, in_specs=[smem] * len(scalars) + [vmem] * len(arra...]
    ppermute x27, waiting for transfers between devices: 24.7 us -> 18.5 us  [permute(): return lax.ppermute(array, 'row', pairs)]
    unnamed x25 -> x15, local copies, waits for them, and re-layouts: 8.59 us -> 7.06 us
  transfers between devices with their start and end apart: 27 -> 27, of which waited for: 13 -> 11; matrix products, arithmetic and copies ran while one was open for 1% -> 3% of each run, Pallas kernels for 25% -> 13%
where the time goes in v3:
time: 93.5 us; the launch traced here: 93.2 us
  starting transfers between devices  46.7 us (50%)
  Pallas kernels  18.6 us (20%)
  waiting for transfers between devices  18.5 us (20%)
  local copies, waits for them, and re-layouts  8.34 us (9%)
    ppermute x27, starting transfers between devices, permute(): return lax.ppermute(array, 'row', pairs)  46.7 us
    pallas_call x11, Pallas kernels, call(): pl.pallas_call(kernel, in_specs=[smem] * len(scalars) + [vmem] * len(arra...  18.6 us
    ppermute x27, waiting for transfers between devices, permute(): return lax.ppermute(array, 'row', pairs)  18.5 us
    unnamed x15, local copies, waits for them, and re-layouts  7.06 us
  transfers between devices with their start and end apart: 27, of which 11 were waited for; matrix products, arithmetic and copies ran while one was open for 3% of the time, Pallas kernels for 13%

profile of v3, /device:TPU:1, one launch (start us, length us, event | category | flops | bytes accessed | tf_op | source)
XLA Modules:
  0.0 93.2 jit_solution(14935255195501545582)
XLA Ops:
  3.0 6.9 %collective-permute-start = (bf16[128,128]{1,0:T(8,128)(2,1)S(1)}, bf16[128,128]{1,0:T(8,128)(2,1)S(1)}, u32[]{:S(2)}, u32[]{:S(2)}) collective-permute-start(bf16[128,128]{1,0:T(8,128)(2,1)S(1)} %get-tuple-element.65), channel_id=1, source_target_pairs={{0,12},{1,13},{2,14},{3,15},{4,8},{5,9},{6,10},{7,11},{8,4},{9,5},... | collective-permute-start | bytes 98312 | tf_op jit(solution)/shard_map/ppermute | solution.py:43
  16.3 2.2 %copy-done = bf16[32,4,128,128]{3,2,1,0:T(8,128)(2,1)S(1)} copy-done((bf16[32,4,128,128]{3,2,1,0:T(8,128)(2,1)S(1)}, bf16[32,4,128,128]{3,2,1,0:T(8,128)(2,1)}, u32[]{:S(2)}) %copy-start) | copy-done | bytes 4194328
  18.5 2.2 %copy-done.2 = bf16[32,4,128,128]{3,2,1,0:T(8,128)(2,1)S(1)} copy-done((bf16[32,4,128,128]{3,2,1,0:T(8,128)(2,1)S(1)}, bf16[32,4,128,128]{3,2,1,0:T(8,128)(2,1)}, u32[]{:S(2)}) %copy-start.2) | copy-done | bytes 4194328
  22.1 2.1 %collective-permute-start.5 = (bf16[1024,128]{1,0:T(8,128)(2,1)S(1)}, bf16[1024,128]{1,0:T(8,128)(2,1)S(1)}, u32[]{:S(2)}, u32[]{:S(2)}) collective-permute-start(bf16[1024,128]{1,0:T(8,128)(2,1)S(1)} %pad_maximum_fusion.rest_1_), channel_id=1, source_target_pairs={{0,1},{1,0},{2,3},{3,2},{4,5},{5,4},{6,7},{7,6},{8,9},{9,8},{10,11... | collective-permute-start | bytes 786440 | tf_op jit(solution)/shard_map/ppermute | solution.py:43
  25.5 3.0 %collective-permute-done.7.outer_ref = bf16[3,128,128]{2,1,0:T(8,128)(2,1)S(1)} collective-permute-done((bf16[3,128,128]{2,1,0:T(8,128)(2,1)S(1)}, bf16[3,128,128]{2,1,0:T(8,128)(2,1)S(1)}, u32[]{:S(2)}, u32[]{:S(2)}) %collective-permute-start.7) | collective-permute-done | bytes 98336 | tf_op jit(solution)/shard_map/ppermute | solution.py:43
  28.5 2.1 %shard_map.66.band_ref = f32[32,128,128]{2,1,0:T(8,128)S(1)} custom-call(s32[128]{0:T(128)S(1)} %reshape.14.offsets_ref, s32[4]{0:T(128)S(1)} %pad_add_fusion.side_ref, bf16[32,128,128]{2,1,0:T(8,128)(2,1)S(1)} %bitcast.8, bf16[3,128,128]{2,1,0:T(8,128)(2,1)S(1)} %collective-permute-done.6.inner_ref, ...), custom_call_target="tpu_custom_call" | custom-call | flops 1 | bytes 1 | tf_op jit(solution)/shard_map/pallas_call | solution.py:73
  30.6 2.4 %collective-permute-start.8 = (bf16[1024,128]{1,0:T(8,128)(2,1)S(1)}, bf16[1024,128]{1,0:T(8,128)(2,1)S(1)}, u32[]{:S(2)}, u32[]{:S(2)}) collective-permute-start(bf16[1024,128]{1,0:T(8,128)(2,1)S(1)} %collective-permute-done.4.rest_2_), channel_id=1, source_target_pairs={{0,1},{1,0},{2,3},{3,2},{4,5},{5,4},{6,7},{7,6},{8,9},{9,8},{10,11... | collective-permute-start | bytes 786440 | tf_op jit(solution)/shard_map/ppermute | solution.py:43
  34.2 2.4 %shard_map.67 = (bf16[32,128,128]{2,1,0:T(8,128)(2,1)S(1)}, bf16[128,128]{1,0:T(8,128)(2,1)S(1)}) custom-call(s32[128]{0:T(128)S(1)} %reshape.13.place_ref, bf16[32,4,128,128]{3,2,1,0:T(8,128)(2,1)S(1)} %copy-done.1, f32[32,128,128]{2,1,0:T(8,128)S(1)} %shard_map.66.band_ref, s32[2,128,128]{2,1,0:T(8,128)S(1)} %get-tuple-element.91.refs_0_.rest_0_.columns_ref, ...), custom_call_target="tpu_custom_call" | custom-call | flops 1 | bytes 1 | tf_op jit(solution)/shard_map/pallas_call | solution.py:73
  37.1 4.5 %collective-permute-start.9 = (bf16[128,128]{1,0:T(8,128)(2,1)S(1)}, bf16[128,128]{1,0:T(8,128)(2,1)S(1)}, u32[]{:S(2)}, u32[]{:S(2)}) collective-permute-start(bf16[128,128]{1,0:T(8,128)(2,1)S(1)} %get-tuple-element.86), channel_id=1, source_target_pairs={{0,12},{1,13},{2,14},{3,15},{4,8},{5,9},{6,10},{7,11},{8,4},{9,5},... | collective-permute-start | bytes 98312 | tf_op jit(solution)/shard_map/ppermute | solution.py:43
  41.6 2.4 %collective-permute-done.9 = bf16[128,128]{1,0:T(8,128)(2,1)S(1)} collective-permute-done((bf16[128,128]{1,0:T(8,128)(2,1)S(1)}, bf16[128,128]{1,0:T(8,128)(2,1)S(1)}, u32[]{:S(2)}, u32[]{:S(2)}) %collective-permute-start.9) | collective-permute-done | bytes 32800 | tf_op jit(solution)/shard_map/ppermute | solution.py:43
  44.5 2.1 %collective-permute-start.12 = (bf16[256,128]{1,0:T(8,128)(2,1)S(1)}, bf16[256,128]{1,0:T(8,128)(2,1)S(1)}, u32[]{:S(2)}, u32[]{:S(2)}) collective-permute-start(bf16[256,128]{1,0:T(8,128)(2,1)S(1)} %pad_maximum_fusion.4), channel_id=1, source_target_pairs={{0,2},{1,3},{2,0},{3,1},{4,6},{5,7},{6,4},{7,5},{8,10},{9,11},{10,... | collective-permute-start | bytes 196616 | tf_op jit(solution)/shard_map/ppermute | solution.py:43
  47.6 2.3 %shard_map.68.spread_ref = bf16[32,128,128]{2,1,0:T(8,128)(2,1)S(1)} custom-call(s32[128]{0:T(128)S(1)} %reshape.13.place_ref, s32[2,128,128]{2,1,0:T(8,128)S(1)} %get-tuple-element.91.refs_0_.rest_0_.columns_ref, bf16[32,4,128,128]{3,2,1,0:T(8,128)(2,1)S(1)} %copy-done.1), custom_call_target="tpu_custom_call" | custom-call | flops 1 | bytes 1 | tf_op jit(solution)/shard_map/pallas_call | solution.py:73
  52.1 3.7 %collective-permute-start.16 = (bf16[1024,128]{1,0:T(8,128)(2,1)S(1)}, bf16[1024,128]{1,0:T(8,128)(2,1)S(1)}, u32[]{:S(2)}, u32[]{:S(2)}) collective-permute-start(bf16[1024,128]{1,0:T(8,128)(2,1)S(1)} %pad_maximum_fusion.1.rest_0_), channel_id=1, source_target_pairs={{0,1},{1,0},{2,3},{3,2},{4,5},{5,4},{6,7},{7,6},{8,9},{9,8},{10,11... | collective-permute-start | bytes 786440 | tf_op jit(solution)/shard_map/ppermute | solution.py:43
  55.8 2.7 %shard_map.69 = (f32[32,128,128]{2,1,0:T(8,128)S(1)}, f32[128,128]{1,0:T(8,128)S(1)}) custom-call(s32[128]{0:T(128)S(1)} %reshape.14.offsets_ref, s32[4]{0:T(128)S(1)} %pad_add_fusion.side_ref, bf16[32,128,128]{2,1,0:T(8,128)(2,1)S(1)} %get-tuple-element.87.table_ref.rest_1_, bf16[3,128,128]{2,1,0:T(8,128)(2,1)S(1)} %collective-permute-done.10.inner_ref, ...), custom_call_target="tpu_custom_call" | custom-call | flops 1 | bytes 1 | tf_op jit(solution)/shard_map/pallas_call | solution.py:73
  58.5 2.2 %collective-permute-start.17 = (bf16[1024,128]{1,0:T(8,128)(2,1)S(1)}, bf16[1024,128]{1,0:T(8,128)(2,1)S(1)}, u32[]{:S(2)}, u32[]{:S(2)}) collective-permute-start(bf16[1024,128]{1,0:T(8,128)(2,1)S(1)} %collective-permute-done.15.rest_1_), channel_id=1, source_target_pairs={{0,1},{1,0},{2,3},{3,2},{4,5},{5,4},{6,7},{7,6},{8,9},{9,8},{10,11... | collective-permute-start | bytes 786440 | tf_op jit(solution)/shard_map/ppermute | solution.py:43
  62.1 4.7 %collective-permute-start.18 = (bf16[128,128]{1,0:T(8,128)(2,1)S(1)}, bf16[128,128]{1,0:T(8,128)(2,1)S(1)}, u32[]{:S(2)}, u32[]{:S(2)}) collective-permute-start(bf16[128,128]{1,0:T(8,128)(2,1)S(1)} %shard_map.71), channel_id=1, source_target_pairs={{0,12},{1,13},{2,14},{3,15},{4,8},{5,9},{6,10},{7,11},{8,4},{9,5},... | collective-permute-start | bytes 98312 | tf_op jit(solution)/shard_map/ppermute | solution.py:43
  66.8 2.1 %shard_map.72.table_ref = bf16[32,128,128]{2,1,0:T(8,128)(2,1)S(1)} custom-call(s32[128]{0:T(128)S(1)} %reshape.13.place_ref, bf16[32,4,128,128]{3,2,1,0:T(8,128)(2,1)S(1)} %copy-done.1, f32[32,128,128]{2,1,0:T(8,128)S(1)} %get-tuple-element.106.band_ref, bf16[1024,128]{1,0:T(8,128)(2,1)S(1)} %pad_maximum_fusion.1.rest_0_, ...), custom_call_target="tpu_custom_call" | custom-call | flops 1 | bytes 1 | tf_op jit(solution)/shard_map/pallas_call | solution.py:73
  70.2 2.3 %collective-permute-start.21 = (bf16[256,128]{1,0:T(8,128)(2,1)S(1)}, bf16[256,128]{1,0:T(8,128)(2,1)S(1)}, u32[]{:S(2)}, u32[]{:S(2)}) collective-permute-start(bf16[256,128]{1,0:T(8,128)(2,1)S(1)} %pad_maximum_fusion.5), channel_id=1, source_target_pairs={{0,6},{1,7},{2,4},{3,5},{4,2},{5,3},{6,0},{7,1},{8,14},{9,15},{10,... | collective-permute-start | bytes 196616 | tf_op jit(solution)/shard_map/ppermute | solution.py:43
  73.2 2.3 %collective-permute-done.21 = bf16[256,128]{1,0:T(8,128)(2,1)S(1)} collective-permute-done((bf16[256,128]{1,0:T(8,128)(2,1)S(1)}, bf16[256,128]{1,0:T(8,128)(2,1)S(1)}, u32[]{:S(2)}, u32[]{:S(2)}) %collective-permute-start.21) | collective-permute-done | bytes 65568 | tf_op jit(solution)/shard_map/ppermute | solution.py:43
  76.9 3.0 %collective-permute-start.23 = (bf16[1024,128]{1,0:T(8,128)(2,1)S(1)}, bf16[1024,128]{1,0:T(8,128)(2,1)S(1)}, u32[]{:S(2)}, u32[]{:S(2)}) collective-permute-start(bf16[1024,128]{1,0:T(8,128)(2,1)S(1)} %pad_maximum_fusion.2.rest_1_), channel_id=1, source_target_pairs={{0,1},{1,0},{2,3},{3,2},{4,5},{5,4},{6,7},{7,6},{8,9},{9,8},{10,11... | collective-permute-start | bytes 786440 | tf_op jit(solution)/shard_map/ppermute | solution.py:43
  81.2 3.0 %collective-permute-done.25.outer_ref = bf16[3,128,128]{2,1,0:T(8,128)(2,1)S(1)} collective-permute-done((bf16[3,128,128]{2,1,0:T(8,128)(2,1)S(1)}, bf16[3,128,128]{2,1,0:T(8,128)(2,1)S(1)}, u32[]{:S(2)}, u32[]{:S(2)}) %collective-permute-start.25) | collective-permute-done | bytes 98336 | tf_op jit(solution)/shard_map/ppermute | solution.py:43
  84.2 2.2 %shard_map.73 = (f32[32,128,128]{2,1,0:T(8,128)S(1)}, f32[32,128,128]{2,1,0:T(8,128)S(1)}) custom-call(s32[128]{0:T(128)S(1)} %reshape.14.offsets_ref, s32[4]{0:T(128)S(1)} %pad_add_fusion.side_ref, bf16[32,128,128]{2,1,0:T(8,128)(2,1)S(1)} %shard_map.72.table_ref, bf16[3,128,128]{2,1,0:T(8,128)(2,1)S(1)} %collective-permute-done.24.inner_ref, ...), custom_call_target="tpu_custom_call" | custom-call | flops 1 | bytes 1 | tf_op jit(solution)/shard_map/pallas_call | solution.py:73
  86.5 2.4 %collective-permute-start.26 = (bf16[1024,128]{1,0:T(8,128)(2,1)S(1)}, bf16[1024,128]{1,0:T(8,128)(2,1)S(1)}, u32[]{:S(2)}, u32[]{:S(2)}) collective-permute-start(bf16[1024,128]{1,0:T(8,128)(2,1)S(1)} %collective-permute-done.22.rest_2_), channel_id=1, source_target_pairs={{0,1},{1,0},{2,3},{3,2},{4,5},{5,4},{6,7},{7,6},{8,9},{9,8},{10,11... | collective-permute-start | bytes 786440 | tf_op jit(solution)/shard_map/ppermute | solution.py:43
  90.0 3.2 %shard_map.74 = bf16[32,128,128]{2,1,0:T(8,128)(2,1)} custom-call(s32[128]{0:T(128)S(1)} %reshape.13.place_ref, bf16[32,4,128,128]{3,2,1,0:T(8,128)(2,1)S(1)} %copy-done.1, f32[32,128,128]{2,1,0:T(8,128)S(1)} %get-tuple-element.121.band_ref, f32[32,128,128]{2,1,0:T(8,128)S(1)} %get-tuple-element.122.rest_0_, ...), custom_call_target="tpu_custom_call" | custom-call | flops 1 | bytes 1 | tf_op jit(solution)/shard_map/pallas_call | solution.py:73
  (70 shorter events, 24.7 us)
Async XLA Ops:
  3.0 8.7 %collective-permute-start = (bf16[128,128]{1,0:T(8,128)(2,1)S(1)}, bf16[128,128]{1,0:T(8,128)(2,1)S(1)}, u32[]{:S(2)}, u32[]{:S(2)}) collective-permute-start(bf16[128,128]{1,0:T(8,128)(2,1)S(1)} %get-tuple-element.65), channel_id=1, source_target_pairs={{0,12},{1,13},{2,14},{3,15},{4,8},{5,9},{6,10},{7,11},{8,4},{9,5},... | collective-permute-start | bytes 98312 | tf_op jit(solution)/shard_map/ppermute | solution.py:43
  11.7 9.0 %collective-permute-start.2 = (bf16[256,128]{1,0:T(8,128)(2,1)S(1)}, bf16[256,128]{1,0:T(8,128)(2,1)S(1)}, u32[]{:S(2)}, u32[]{:S(2)}) collective-permute-start(bf16[256,128]{1,0:T(8,128)(2,1)S(1)} %pad_maximum_fusion.3), channel_id=1, source_target_pairs={{0,4},{1,5},{2,6},{3,7},{4,0},{5,1},{6,2},{7,3},{8,12},{9,13},{10,... | collective-permute-start | bytes 196616 | tf_op jit(solution)/shard_map/ppermute | solution.py:43
  13.0 7.7 %collective-permute-start.1 = (bf16[256,128]{1,0:T(8,128)(2,1)S(1)}, bf16[256,128]{1,0:T(8,128)(2,1)S(1)}, u32[]{:S(2)}, u32[]{:S(2)}) collective-permute-start(bf16[256,128]{1,0:T(8,128)(2,1)S(1)} %pad_maximum_fusion.3), channel_id=1, source_target_pairs={{0,2},{1,3},{2,0},{3,1},{4,6},{5,7},{6,4},{7,5},{8,10},{9,11},{10,... | collective-permute-start | bytes 196616 | tf_op jit(solution)/shard_map/ppermute | solution.py:43
  13.7 7.0 %collective-permute-start.3 = (bf16[256,128]{1,0:T(8,128)(2,1)S(1)}, bf16[256,128]{1,0:T(8,128)(2,1)S(1)}, u32[]{:S(2)}, u32[]{:S(2)}) collective-permute-start(bf16[256,128]{1,0:T(8,128)(2,1)S(1)} %pad_maximum_fusion.3), channel_id=1, source_target_pairs={{0,6},{1,7},{2,4},{3,5},{4,2},{5,3},{6,0},{7,1},{8,14},{9,15},{10,... | collective-permute-start | bytes 196616 | tf_op jit(solution)/shard_map/ppermute | solution.py:43
  20.8 9.8 %collective-permute-start.4 = (bf16[1024,128]{1,0:T(8,128)(2,1)S(1)}, bf16[1024,128]{1,0:T(8,128)(2,1)S(1)}, u32[]{:S(2)}, u32[]{:S(2)}) collective-permute-start(bf16[1024,128]{1,0:T(8,128)(2,1)S(1)} %pad_maximum_fusion.rest_1_), channel_id=1, source_target_pairs={{0,16},{1,17},{2,18},{3,19},{4,20},{5,21},{6,22},{7,23},{8,24},{9,... | collective-permute-start | bytes 786440 | tf_op jit(solution)/shard_map/ppermute | solution.py:43
  22.1 8.5 %collective-permute-start.5 = (bf16[1024,128]{1,0:T(8,128)(2,1)S(1)}, bf16[1024,128]{1,0:T(8,128)(2,1)S(1)}, u32[]{:S(2)}, u32[]{:S(2)}) collective-permute-start(bf16[1024,128]{1,0:T(8,128)(2,1)S(1)} %pad_maximum_fusion.rest_1_), channel_id=1, source_target_pairs={{0,1},{1,0},{2,3},{3,2},{4,5},{5,4},{6,7},{7,6},{8,9},{9,8},{10,11... | collective-permute-start | bytes 786440 | tf_op jit(solution)/shard_map/ppermute | solution.py:43
  24.2 4.3 %collective-permute-start.7 = (bf16[3,128,128]{2,1,0:T(8,128)(2,1)S(1)}, bf16[3,128,128]{2,1,0:T(8,128)(2,1)S(1)}, u32[]{:S(2)}, u32[]{:S(2)}) collective-permute-start(bf16[3,128,128]{2,1,0:T(8,128)(2,1)S(1)} %get-tuple-element.77), channel_id=1, source_target_pairs={{0,31},{1,2},{2,1},{3,4},{4,3},{5,6},{6,5},{7,8},{8,7},{9,10},{10,... | collective-permute-start | bytes 294920 | tf_op jit(solution)/shard_map/ppermute | solution.py:43
  30.6 3.6 %collective-permute-start.8 = (bf16[1024,128]{1,0:T(8,128)(2,1)S(1)}, bf16[1024,128]{1,0:T(8,128)(2,1)S(1)}, u32[]{:S(2)}, u32[]{:S(2)}) collective-permute-start(bf16[1024,128]{1,0:T(8,128)(2,1)S(1)} %collective-permute-done.4.rest_2_), channel_id=1, source_target_pairs={{0,1},{1,0},{2,3},{3,2},{4,5},{5,4},{6,7},{7,6},{8,9},{9,8},{10,11... | collective-permute-start | bytes 786440 | tf_op jit(solution)/shard_map/ppermute | solution.py:43
  36.7 7.3 %collective-permute-start.10 = (bf16[3,128,128]{2,1,0:T(8,128)(2,1)S(1)}, bf16[3,128,128]{2,1,0:T(8,128)(2,1)S(1)}, u32[]{:S(2)}, u32[]{:S(2)}) collective-permute-start(bf16[3,128,128]{2,1,0:T(8,128)(2,1)S(1)} %get-tuple-element.128), channel_id=1, source_target_pairs={{0,1},{1,0},{2,3},{3,2},{4,5},{5,4},{6,7},{7,6},{8,9},{9,8},{10,11... | collective-permute-start | bytes 294920 | tf_op jit(solution)/shard_map/ppermute | solution.py:43
  37.1 6.8 %collective-permute-start.11 = (bf16[3,128,128]{2,1,0:T(8,128)(2,1)S(1)}, bf16[3,128,128]{2,1,0:T(8,128)(2,1)S(1)}, u32[]{:S(2)}, u32[]{:S(2)}) collective-permute-start(bf16[3,128,128]{2,1,0:T(8,128)(2,1)S(1)} %get-tuple-element.127), channel_id=1, source_target_pairs={{0,31},{1,2},{2,1},{3,4},{4,3},{5,6},{6,5},{7,8},{8,7},{9,10},{10,... | collective-permute-start | bytes 294920 | tf_op jit(solution)/shard_map/ppermute | solution.py:43
  37.1 6.8 %collective-permute-start.9 = (bf16[128,128]{1,0:T(8,128)(2,1)S(1)}, bf16[128,128]{1,0:T(8,128)(2,1)S(1)}, u32[]{:S(2)}, u32[]{:S(2)}) collective-permute-start(bf16[128,128]{1,0:T(8,128)(2,1)S(1)} %get-tuple-element.86), channel_id=1, source_target_pairs={{0,12},{1,13},{2,14},{3,15},{4,8},{5,9},{6,10},{7,11},{8,4},{9,5},... | collective-permute-start | bytes 98312 | tf_op jit(solution)/shard_map/ppermute | solution.py:43
  44.0 5.9 %collective-permute-start.13 = (bf16[256,128]{1,0:T(8,128)(2,1)S(1)}, bf16[256,128]{1,0:T(8,128)(2,1)S(1)}, u32[]{:S(2)}, u32[]{:S(2)}) collective-permute-start(bf16[256,128]{1,0:T(8,128)(2,1)S(1)} %pad_maximum_fusion.4), channel_id=1, source_target_pairs={{0,4},{1,5},{2,6},{3,7},{4,0},{5,1},{6,2},{7,3},{8,12},{9,13},{10,... | collective-permute-start | bytes 196616 | tf_op jit(solution)/shard_map/ppermute | solution.py:43
  44.5 5.5 %collective-permute-start.12 = (bf16[256,128]{1,0:T(8,128)(2,1)S(1)}, bf16[256,128]{1,0:T(8,128)(2,1)S(1)}, u32[]{:S(2)}, u32[]{:S(2)}) collective-permute-start(bf16[256,128]{1,0:T(8,128)(2,1)S(1)} %pad_maximum_fusion.4), channel_id=1, source_target_pairs={{0,2},{1,3},{2,0},{3,1},{4,6},{5,7},{6,4},{7,5},{8,10},{9,11},{10,... | collective-permute-start | bytes 196616 | tf_op jit(solution)/shard_map/ppermute | solution.py:43
  46.5 5.0 %collective-permute-start.14 = (bf16[256,128]{1,0:T(8,128)(2,1)S(1)}, bf16[256,128]{1,0:T(8,128)(2,1)S(1)}, u32[]{:S(2)}, u32[]{:S(2)}) collective-permute-start(bf16[256,128]{1,0:T(8,128)(2,1)S(1)} %pad_maximum_fusion.4), channel_id=1, source_target_pairs={{0,6},{1,7},{2,4},{3,5},{4,2},{5,3},{6,0},{7,1},{8,14},{9,15},{10,... | collective-permute-start | bytes 196616 | tf_op jit(solution)/shard_map/ppermute | solution.py:43
  51.6 6.9 %collective-permute-start.15 = (bf16[1024,128]{1,0:T(8,128)(2,1)S(1)}, bf16[1024,128]{1,0:T(8,128)(2,1)S(1)}, u32[]{:S(2)}, u32[]{:S(2)}) collective-permute-start(bf16[1024,128]{1,0:T(8,128)(2,1)S(1)} %pad_maximum_fusion.1.rest_0_), channel_id=1, source_target_pairs={{0,16},{1,17},{2,18},{3,19},{4,20},{5,21},{6,22},{7,23},{8,24},{9,... | collective-permute-start | bytes 786440 | tf_op jit(solution)/shard_map/ppermute | solution.py:43
  52.1 6.4 %collective-permute-start.16 = (bf16[1024,128]{1,0:T(8,128)(2,1)S(1)}, bf16[1024,128]{1,0:T(8,128)(2,1)S(1)}, u32[]{:S(2)}, u32[]{:S(2)}) collective-permute-start(bf16[1024,128]{1,0:T(8,128)(2,1)S(1)} %pad_maximum_fusion.1.rest_0_), channel_id=1, source_target_pairs={{0,1},{1,0},{2,3},{3,2},{4,5},{5,4},{6,7},{7,6},{8,9},{9,8},{10,11... | collective-permute-start | bytes 786440 | tf_op jit(solution)/shard_map/ppermute | solution.py:43
  62.1 6.8 %collective-permute-start.18 = (bf16[128,128]{1,0:T(8,128)(2,1)S(1)}, bf16[128,128]{1,0:T(8,128)(2,1)S(1)}, u32[]{:S(2)}, u32[]{:S(2)}) collective-permute-start(bf16[128,128]{1,0:T(8,128)(2,1)S(1)} %shard_map.71), channel_id=1, source_target_pairs={{0,12},{1,13},{2,14},{3,15},{4,8},{5,9},{6,10},{7,11},{8,4},{9,5},... | collective-permute-start | bytes 98312 | tf_op jit(solution)/shard_map/ppermute | solution.py:43
  68.9 3.7 %collective-permute-start.19 = (bf16[256,128]{1,0:T(8,128)(2,1)S(1)}, bf16[256,128]{1,0:T(8,128)(2,1)S(1)}, u32[]{:S(2)}, u32[]{:S(2)}) collective-permute-start(bf16[256,128]{1,0:T(8,128)(2,1)S(1)} %pad_maximum_fusion.5), channel_id=1, source_target_pairs={{0,2},{1,3},{2,0},{3,1},{4,6},{5,7},{6,4},{7,5},{8,10},{9,11},{10,... | collective-permute-start | bytes 196616 | tf_op jit(solution)/shard_map/ppermute | solution.py:43
  69.0 4.2 %collective-permute-start.20 = (bf16[256,128]{1,0:T(8,128)(2,1)S(1)}, bf16[256,128]{1,0:T(8,128)(2,1)S(1)}, u32[]{:S(2)}, u32[]{:S(2)}) collective-permute-start(bf16[256,128]{1,0:T(8,128)(2,1)S(1)} %pad_maximum_fusion.5), channel_id=1, source_target_pairs={{0,4},{1,5},{2,6},{3,7},{4,0},{5,1},{6,2},{7,3},{8,12},{9,13},{10,... | collective-permute-start | bytes 196616 | tf_op jit(solution)/shard_map/ppermute | solution.py:43
  70.2 5.2 %collective-permute-start.21 = (bf16[256,128]{1,0:T(8,128)(2,1)S(1)}, bf16[256,128]{1,0:T(8,128)(2,1)S(1)}, u32[]{:S(2)}, u32[]{:S(2)}) collective-permute-start(bf16[256,128]{1,0:T(8,128)(2,1)S(1)} %pad_maximum_fusion.5), channel_id=1, source_target_pairs={{0,6},{1,7},{2,4},{3,5},{4,2},{5,3},{6,0},{7,1},{8,14},{9,15},{10,... | collective-permute-start | bytes 196616 | tf_op jit(solution)/shard_map/ppermute | solution.py:43
  75.5 11.0 %collective-permute-start.22 = (bf16[1024,128]{1,0:T(8,128)(2,1)S(1)}, bf16[1024,128]{1,0:T(8,128)(2,1)S(1)}, u32[]{:S(2)}, u32[]{:S(2)}) collective-permute-start(bf16[1024,128]{1,0:T(8,128)(2,1)S(1)} %pad_maximum_fusion.2.rest_1_), channel_id=1, source_target_pairs={{0,16},{1,17},{2,18},{3,19},{4,20},{5,21},{6,22},{7,23},{8,24},{9,... | collective-permute-start | bytes 786440 | tf_op jit(solution)/shard_map/ppermute | solution.py:43
  76.9 9.5 %collective-permute-start.23 = (bf16[1024,128]{1,0:T(8,128)(2,1)S(1)}, bf16[1024,128]{1,0:T(8,128)(2,1)S(1)}, u32[]{:S(2)}, u32[]{:S(2)}) collective-permute-start(bf16[1024,128]{1,0:T(8,128)(2,1)S(1)} %pad_maximum_fusion.2.rest_1_), channel_id=1, source_target_pairs={{0,1},{1,0},{2,3},{3,2},{4,5},{5,4},{6,7},{7,6},{8,9},{9,8},{10,11... | collective-permute-start | bytes 786440 | tf_op jit(solution)/shard_map/ppermute | solution.py:43
  79.9 4.3 %collective-permute-start.25 = (bf16[3,128,128]{2,1,0:T(8,128)(2,1)S(1)}, bf16[3,128,128]{2,1,0:T(8,128)(2,1)S(1)}, u32[]{:S(2)}, u32[]{:S(2)}) collective-permute-start(bf16[3,128,128]{2,1,0:T(8,128)(2,1)S(1)} %get-tuple-element.118), channel_id=1, source_target_pairs={{0,31},{1,2},{2,1},{3,4},{4,3},{5,6},{6,5},{7,8},{8,7},{9,10},{10,... | collective-permute-start | bytes 294920 | tf_op jit(solution)/shard_map/ppermute | solution.py:43
  86.5 3.6 %collective-permute-start.26 = (bf16[1024,128]{1,0:T(8,128)(2,1)S(1)}, bf16[1024,128]{1,0:T(8,128)(2,1)S(1)}, u32[]{:S(2)}, u32[]{:S(2)}) collective-permute-start(bf16[1024,128]{1,0:T(8,128)(2,1)S(1)} %collective-permute-done.22.rest_2_), channel_id=1, source_target_pairs={{0,1},{1,0},{2,3},{3,2},{4,5},{5,4},{6,7},{7,6},{8,9},{9,8},{10,11... | collective-permute-start | bytes 786440 | tf_op jit(solution)/shard_map/ppermute | solution.py:43
  (10 other events, 41.3 us)

commit v4 on v3

--- a/solution.py
+++ b/solution.py
@@ -55,8 +55,8 @@
     return jnp.dot(a, b, preferred_element_type=jnp.float32)
 
 
-def id_columns(ids_ref, level, first):
-    row = ids_ref[level : level + 1, :] - first
+def id_columns(ids_ref, level):
+    row = ids_ref[level : level + 1, :]
     return jnp.transpose(jnp.broadcast_to(row, (BLOCK, BLOCK)))
 
 
@@ -66,7 +66,7 @@
     return jnp.concatenate(parts, axis=1)
 
 
-def call(kernel, out_shape, scalars, arrays, flops, scratch=()):
+def call(kernel, out_shape, scalars, arrays, flops, scratch=(), aliases=None):
     smem = pl.BlockSpec(memory_space=pltpu.SMEM)
     vmem = pl.BlockSpec(memory_space=pltpu.VMEM)
     moved = sum(a.size * a.dtype.itemsize for a in arrays)
@@ -76,6 +76,7 @@
         out_specs=jax.tree.map(lambda _: vmem, out_shape),
         out_shape=out_shape,
         scratch_shapes=list(scratch),
+        input_output_aliases=aliases or {},
         compiler_params=pltpu.CompilerParams(vmem_limit_bytes=8 * 2**20),
         cost_estimate=pl.CostEstimate(flops=1, bytes_accessed=1, transcendentals=0),
     )(*scalars, *arrays)
@@ -89,10 +90,10 @@
     return jax.ShapeDtypeStruct(shape, jnp.bfloat16)
 
 
-def pick_kernel(side_ref, ids_ref, table_ref, out_ref, columns_ref):
-    ids = id_columns(ids_ref, 0, side_ref[3])
+def pick_kernel(ids_ref, table_ref, out_ref, columns_ref):
+    ids = id_columns(ids_ref, 0)
     for level in range(1, LAYERS):
-        columns_ref[level - 1] = id_columns(ids_ref, level, side_ref[3])
+        columns_ref[level - 1] = id_columns(ids_ref, level)
     total = jnp.zeros(out_ref.shape, jnp.float32)
     for b in range(0, table_ref.shape[0], CHUNK):
         table = table_ref[b : b + CHUNK].reshape(CHUNK * BLOCK, -1)
@@ -125,57 +126,83 @@
     return dot(tiles, jnp.concatenate(blocks, axis=0))
 
 
-def band_kernel(level, offsets_ref, side_ref, table_ref, inner_ref, outer_ref, tiles_ref, *rest):
-    outs = 2 if level == 0 else 3
-    extra, (out_ref, *more_refs, padded) = rest[:-outs], rest[-outs:]
+def inner_kernel(level, offsets_ref, table_ref, tiles_ref, *rest):
+    more = 1 if level == LAYERS - 1 else 0
+    extra, outs = rest[: len(rest) - 1 - more], rest[len(rest) - 1 - more :]
     blocks = table_ref.shape[0]
-    padded[BAND : BAND + blocks] = table_ref[...]
+    half = (blocks - 2 * BAND) // 2
+
+    def group(step, carry):
+        for i in range(half):
+            b = BAND + step * half + i
+            near = [table_ref[b + offsets_ref[b * 4 + k]] for k in range(4)]
+            outs[0][b] = tile_sum(b, tiles_ref, near)
+        if more:
+            for i in range(blocks // 2):
+                b = step * (blocks // 2) + i
+                total = table_ref[b].astype(jnp.float32)
+                for ref in extra:
+                    total = total + ref[b].astype(jnp.float32)
+                outs[1][b] = total
+        return carry
+
+    lax.fori_loop(0, 2, group, 0)
+
+
+def inner_products(level, offsets, table, tiles, extra):
+    blocks = table.shape[0]
+    shape = f32(blocks, BLOCK, BLOCK)
+    return call(
+        functools.partial(inner_kernel, level),
+        [shape, shape] if level == LAYERS - 1 else [shape],
+        (offsets,),
+        (table, tiles, *extra),
+        2**29,
+    )
+
+
+def rim_kernel(level, offsets_ref, side_ref, band_ref, table_ref, inner_ref, outer_ref, tiles_ref, *rest):
+    del band_ref
+    pick_rows = level == 1
+    if pick_rows:
+        columns_ref, out_ref, more_ref, window = rest
+    else:
+        out_ref, window = rest
+    blocks = table_ref.shape[0]
     core, has_left, has_right = side_ref[0], side_ref[1], side_ref[2]
     inner, outer = inner_ref[...], outer_ref[...]
     left = jnp.where(core == 0, outer, inner)
     right = jnp.where(core == 0, inner, outer)
-    padded[0:BAND] = jnp.where(has_left == 1, left, jnp.zeros_like(left))
-    padded[BAND + blocks :] = jnp.where(has_right == 1, right, jnp.zeros_like(right))
-    pick_rows = 0 < level < LAYERS - 1
-    more_ref = more_refs[0] if more_refs else None
+    window[0:BAND] = jnp.where(has_left == 1, left, jnp.zeros_like(left))
+    window[BAND : 3 * BAND] = table_ref[0 : 2 * BAND]
+    window[3 * BAND : 5 * BAND] = table_ref[blocks - 2 * BAND :]
+    window[5 * BAND :] = jnp.where(has_right == 1, right, jnp.zeros_like(right))
+    for i in range(2 * BAND):
+        b = i if i < BAND else blocks - 2 * BAND + i
+        at = i + BAND if i < BAND else i + 3 * BAND
+        near = [window[at + offsets_ref[b * 4 + k]] for k in range(4)]
+        out_ref[b] = tile_sum(b, tiles_ref, near)
     if pick_rows:
-        ids = extra[0][level]
-        more_ref[...] = jnp.zeros_like(more_ref)
-
-    def group(step, carry):
-        values = []
-        for i in range(STEP):
-            b = step * STEP + i
-            near = [padded[b + BAND + offsets_ref[b * 4 + k]] for k in range(4)]
-            values.append(tile_sum(b, tiles_ref, near))
-            out_ref[b] = values[-1]
-            if level == LAYERS - 1:
-                total = table_ref[b].astype(jnp.float32)
-                for ref in extra:
-                    total = total + ref[b].astype(jnp.float32)
-                more_ref[b] = total
-        if pick_rows:
-            value = jnp.concatenate(values, axis=0)
+        total = jnp.zeros((BLOCK, 2 * BLOCK), jnp.float32)
+        for first in range(0, blocks, STEP):
+            value = out_ref[first : first + STEP].reshape(STEP * BLOCK, BLOCK)
             high = value.astype(jnp.bfloat16)
             low = (value - high.astype(jnp.float32)).astype(jnp.bfloat16)
-            hot = one_hot(ids, step * STEP * BLOCK, STEP)
-            both = dot(hot, jnp.concatenate([high, low], axis=1))
-            more_ref[...] += both[:, :BLOCK] + both[:, BLOCK:]
-        return carry
-
-    lax.fori_loop(0, blocks // STEP, group, 0)
-
-
-def band_products(level, offsets, side, table, inner, outer, tiles, extra):
+            hot = one_hot(columns_ref[level], first * BLOCK, STEP)
+            total += dot(hot, jnp.concatenate([high, low], axis=1))
+        more_ref[...] = total[:, :BLOCK] + total[:, BLOCK:]
+
+
+def rim_products(level, offsets, side, band, table, halos, tiles, extra):
     blocks = table.shape[0]
-    more = {0: [], LAYERS - 1: [f32(blocks, BLOCK, BLOCK)]}.get(level, [f32(BLOCK, BLOCK)])
     return call(
-        functools.partial(band_kernel, level),
-        [f32(blocks, BLOCK, BLOCK)] + more,
+        functools.partial(rim_kernel, level),
+        [f32(blocks, BLOCK, BLOCK)] + ([f32(BLOCK, BLOCK)] if level == 1 else []),
         (offsets, side),
-        (table, inner, outer, tiles, *extra),
+        (band, table, *halos, tiles, *extra),
         2**29,
-        [pltpu.VMEM((blocks + 2 * BAND, BLOCK, BLOCK), jnp.bfloat16)],
+        [pltpu.VMEM((6 * BAND, BLOCK, BLOCK), jnp.bfloat16)],
+        {2: 0},
     )
 
 
@@ -257,7 +284,7 @@
     blocks = rows_dev // BLOCK
     me = lax.axis_index("row")
     core = me % 2
-    side = jnp.stack([core, (me > 0).astype(jnp.int32), (me < DEVICES - 1).astype(jnp.int32), me * rows_dev])
+    side = jnp.stack([core, (me > 0).astype(jnp.int32), (me < DEVICES - 1).astype(jnp.int32)])
     offsets = band_offsets.reshape(-1)
     place = places(hub_blocks, me).reshape(-1)
 
@@ -273,32 +300,16 @@
     picked, columns = call(
         pick_kernel,
         [bf16(BLOCK, features), jax.ShapeDtypeStruct((LAYERS - 1, BLOCK, BLOCK), jnp.int32)],
-        (side,),
-        (hub_ids, table),
+        (),
+        (hub_ids - me * rows_dev, table),
         2**27,
     )
     tables = [table]
     pieces = band = spread = None
     for level in range(LAYERS):
-        if level == 1:
-            picked, table = together(picked, table)
-            across = permute(picked, along_z(6))
-            halos = exchange(edges(table))
-            across, *halos = together(across, *halos)
-        elif level == 0:
-            across = permute(picked, along_z(6))
-        else:
-            across = permute(picked, along_z(6))
-            (table,) = hub_layer("", place, pieces, hub_tiles, band)
-            across, table = together(across, table)
-            tables.append(table)
+        across = permute(picked, along_z(6))
         if level == 0:
             across, place, offsets = together(across, place, offsets)
-        pair, columns = together(jnp.concatenate([picked, across]), columns)
-        near = [permute(pair, along_z(g)) for g in (1, 2, 3)]
-        if level == 0:
-            held = call(touch_kernel, f32(8, BLOCK), (), (columns, hub_tiles, band_tiles), 2**20)
-            near[1], held = together(near[1], held)
         elif level == 1:
             spread = call(
                 functools.partial(expand_kernel, level),
@@ -307,19 +318,26 @@
                 (columns, hub_tiles),
                 2**29,
             )
-            near[1], spread = together(near[1], spread)
-        if level != 1:
-            rims = edges(table)
-            *near, rim_inner, rim_outer = together(*near, *rims)
-            halos = exchange((rim_inner, rim_outer))
-            (column,) = together(jnp.concatenate([pair] + near))
+            across, spread = together(across, spread)
         else:
-            column, *halos = together(jnp.concatenate([pair] + near), *halos)
-        inner, outer = halos
+            (table,) = hub_layer("", place, pieces, hub_tiles, band)
+            across, table = together(across, table)
+            tables.append(table)
+        pair, columns = together(jnp.concatenate([picked, across]), columns)
+        near = [permute(pair, along_z(g)) for g in (1, 2, 3)]
+        if level == 0:
+            held = call(touch_kernel, f32(8, BLOCK), (), (columns, hub_tiles, band_tiles), 2**20)
+            near[1], held = together(near[1], held)
+        *near, rim_inner, rim_outer, table = together(*near, *edges(table), table)
+        column, table = together(jnp.concatenate([pair] + near), table)
         x_column = permute(column, ACROSS_X)
         core_column = permute(column, ACROSS_CORE)
-        extra = ([held], [columns], tables[:-1])[level]
-        band, *more = band_products(level, offsets, side, table, inner, outer, band_tiles, extra)
+        halos = exchange((rim_inner, rim_outer))
+        extra = ([held], [], tables[:-1])[level]
+        band, *base = inner_products(level, offsets, table, band_tiles, extra)
+        *halos, band = together(*halos, band)
+        extra = [columns] if level == 1 else []
+        band, *more = rim_products(level, offsets, side, band, table, halos, band_tiles, extra)
         x_column, core_column, band, *more = together(x_column, core_column, band, *more)
         far = permute(x_column, ACROSS_CORE)
         pieces = [column, x_column, core_column, far]
@@ -328,10 +346,10 @@
             tables.append(table)
             picked, columns, table = together(picked, columns, table)
         elif level == 1:
-            part = call(part_kernel, f32(BLOCK, features), (), (more[0], spread, *pieces[:3]), 2**27)
+            part = call(part_kernel, f32(BLOCK, features), (), (more[0], spread, *pieces[:-1]), 2**27)
             picked = call(close_kernel, bf16(BLOCK, features), (), (part, spread, far), 2**25)
             picked, band, *pieces = together(picked, band, *pieces)
-    (averaged,) = hub_layer("mean", place, pieces, hub_tiles, band, more[0])
+    (averaged,) = hub_layer("mean", place, pieces, hub_tiles, band, base[0])
     return averaged.reshape(rows_dev, features)
 
 

time: 93.5 us -> 89.7 us (0.959)
  starting transfers between devices: 46.7 us -> 41.2 us
  waiting for transfers between devices: 18.5 us -> 16.5 us
  local copies, waits for them, and re-layouts: 8.34 us -> 9.84 us
  Pallas kernels: 18.6 us -> 20 us
    ppermute x27, starting transfers between devices: 46.7 us -> 41.2 us  [permute(): return lax.ppermute(array, 'row', pairs)]
    ppermute x27, waiting for transfers between devices: 18.5 us -> 16.5 us  [permute(): return lax.ppermute(array, 'row', pairs)]
    unnamed x15, local copies, waits for them, and re-layouts: 7.06 us -> 8.56 us
    pallas_call x11 -> x14, Pallas kernels: 18.6 us -> 20 us  [call(): pl.pallas_call(kernel, in_specs=[smem] * len(scalars) + [vmem] * len(arra...]
  transfers between devices with their start and end apart: 27 -> 27, of which waited for: 11 -> 12; matrix products, arithmetic and copies ran while one was open for 3% -> 3% of each run, Pallas kernels for 13% -> 15%
where the time goes in v4:
time: 89.7 us; the launch traced here: 89.4 us
  starting transfers between devices  41.2 us (46%)
  Pallas kernels  20 us (22%)
  waiting for transfers between devices  16.5 us (18%)
  local copies, waits for them, and re-layouts  9.84 us (11%)
  other arithmetic  1.52 us (2%)
    ppermute x27, starting transfers between devices, permute(): return lax.ppermute(array, 'row', pairs)  41.2 us
    pallas_call x14, Pallas kernels, call(): pl.pallas_call(kernel, in_specs=[smem] * len(scalars) + [vmem] * len(arra...  20 us
    ppermute x27, waiting for transfers between devices, permute(): return lax.ppermute(array, 'row', pairs)  16.5 us
    unnamed x15, local copies, waits for them, and re-layouts  8.56 us
  transfers between devices with their start and end apart: 27, of which 12 were waited for; matrix products, arithmetic and copies ran while one was open for 3% of the time, Pallas kernels for 15%

profile of v4, /device:TPU:1, one launch (start us, length us, event | category | flops | bytes accessed | tf_op | source)
XLA Modules:
  0.0 89.4 jit_solution(6302636005896566636)
XLA Ops:
  2.4 6.9 %collective-permute-start = (bf16[128,128]{1,0:T(8,128)(2,1)S(1)}, bf16[128,128]{1,0:T(8,128)(2,1)S(1)}, u32[]{:S(2)}, u32[]{:S(2)}) collective-permute-start(bf16[128,128]{1,0:T(8,128)(2,1)S(1)} %get-tuple-element.79), channel_id=1, source_target_pairs={{0,12},{1,13},{2,14},{3,15},{4,8},{5,9},{6,10},{7,11},{8,4},{9,5},... | collective-permute-start | bytes 98312 | tf_op jit(solution)/shard_map/ppermute | solution.py:43
  13.1 1.6 %collective-permute-start.3 = (bf16[256,128]{1,0:T(8,128)(2,1)S(1)}, bf16[256,128]{1,0:T(8,128)(2,1)S(1)}, u32[]{:S(2)}, u32[]{:S(2)}) collective-permute-start(bf16[256,128]{1,0:T(8,128)(2,1)S(1)} %pad_maximum_fusion.3), channel_id=1, source_target_pairs={{0,6},{1,7},{2,4},{3,5},{4,2},{5,3},{6,0},{7,1},{8,14},{9,15},{10,... | collective-permute-start | bytes 196616 | tf_op jit(solution)/shard_map/ppermute | solution.py:43
  15.7 2.2 %copy-done = bf16[32,4,128,128]{3,2,1,0:T(8,128)(2,1)S(1)} copy-done((bf16[32,4,128,128]{3,2,1,0:T(8,128)(2,1)S(1)}, bf16[32,4,128,128]{3,2,1,0:T(8,128)(2,1)}, u32[]{:S(2)}) %copy-start) | copy-done | bytes 4194328
  17.9 2.2 %copy-done.3 = bf16[32,4,128,128]{3,2,1,0:T(8,128)(2,1)S(1)} copy-done((bf16[32,4,128,128]{3,2,1,0:T(8,128)(2,1)S(1)}, bf16[32,4,128,128]{3,2,1,0:T(8,128)(2,1)}, u32[]{:S(2)}) %copy-start.3) | copy-done | bytes 4194328
  21.4 2.1 %collective-permute-start.5 = (bf16[1024,128]{1,0:T(8,128)(2,1)S(1)}, bf16[1024,128]{1,0:T(8,128)(2,1)S(1)}, u32[]{:S(2)}, u32[]{:S(2)}) collective-permute-start(bf16[1024,128]{1,0:T(8,128)(2,1)S(1)} %pad_maximum_fusion.rest_1_), channel_id=1, source_target_pairs={{0,1},{1,0},{2,3},{3,2},{4,5},{5,4},{6,7},{7,6},{8,9},{9,8},{10,11... | collective-permute-start | bytes 786440 | tf_op jit(solution)/shard_map/ppermute | solution.py:43
  23.9 2.2 %copy-done.1 = bf16[32,4,128,128]{3,2,1,0:T(8,128)(2,1)S(1)} copy-done((bf16[32,4,128,128]{3,2,1,0:T(8,128)(2,1)S(1)}, bf16[32,4,128,128]{3,2,1,0:T(8,128)(2,1)}, u32[]{:S(2)}) %copy-start.1) | copy-done | bytes 4194328
  26.0 1.7 %shard_map.66.band_ref = f32[32,128,128]{2,1,0:T(8,128)S(1)} custom-call(s32[128]{0:T(128)S(1)} %reshape.14.offsets_ref, bf16[32,128,128]{2,1,0:T(8,128)(2,1)S(1)} %bitcast.7, bf16[32,4,128,128]{3,2,1,0:T(8,128)(2,1)S(1)} %copy-done.1, f32[8,128]{1,0:T(8,128)S(1)} %shard_map.65.rest_0_), custom_call_target="tpu_custom_call" | custom-call | flops 1 | bytes 1 | tf_op jit(solution)/shard_map/pallas_call | solution.py:73
  28.9 3.6 %collective-permute-start.8 = (bf16[1024,128]{1,0:T(8,128)(2,1)S(1)}, bf16[1024,128]{1,0:T(8,128)(2,1)S(1)}, u32[]{:S(2)}, u32[]{:S(2)}) collective-permute-start(bf16[1024,128]{1,0:T(8,128)(2,1)S(1)} %collective-permute-done.4.rest_2_), channel_id=1, source_target_pairs={{0,1},{1,0},{2,3},{3,2},{4,5},{5,4},{6,7},{7,6},{8,9},{9,8},{10,11... | collective-permute-start | bytes 786440 | tf_op jit(solution)/shard_map/ppermute | solution.py:43
  33.6 2.4 %shard_map.68 = (bf16[32,128,128]{2,1,0:T(8,128)(2,1)S(1)}, bf16[128,128]{1,0:T(8,128)(2,1)S(1)}) custom-call(s32[128]{0:T(128)S(1)} %reshape.13.place_ref, bf16[32,4,128,128]{3,2,1,0:T(8,128)(2,1)S(1)} %copy-done.4, f32[32,128,128]{2,1,0:T(8,128)S(1)} %shard_map.67.band_ref, s32[2,128,128]{2,1,0:T(8,128)S(1)} %get-tuple-element.120.refs_0_.rest_0_.columns_ref, ...), custom_call_target="tpu_custom_call" | custom-call | flops 1 | bytes 1 | tf_op jit(solution)/shard_map/pallas_call | solution.py:73
  36.1 1.7 %collective-permute-start.9 = (bf16[128,128]{1,0:T(8,128)(2,1)S(1)}, bf16[128,128]{1,0:T(8,128)(2,1)S(1)}, u32[]{:S(2)}, u32[]{:S(2)}) collective-permute-start(bf16[128,128]{1,0:T(8,128)(2,1)S(1)} %get-tuple-element.104), channel_id=1, source_target_pairs={{0,12},{1,13},{2,14},{3,15},{4,8},{5,9},{6,10},{7,11},{8,4},{9,5},... | collective-permute-start | bytes 98312 | tf_op jit(solution)/shard_map/ppermute | solution.py:43
  37.7 2.3 %shard_map.69.spread_ref = bf16[32,128,128]{2,1,0:T(8,128)(2,1)S(1)} custom-call(s32[128]{0:T(128)S(1)} %reshape.13.place_ref, s32[2,128,128]{2,1,0:T(8,128)S(1)} %get-tuple-element.120.refs_0_.rest_0_.columns_ref, bf16[32,4,128,128]{3,2,1,0:T(8,128)(2,1)S(1)} %copy-done.4), custom_call_target="tpu_custom_call" | custom-call | flops 1 | bytes 1 | tf_op jit(solution)/shard_map/pallas_call | solution.py:73
  46.1 2.6 %collective-permute-done.12 = bf16[256,128]{1,0:T(8,128)(2,1)S(1)} collective-permute-done((bf16[256,128]{1,0:T(8,128)(2,1)S(1)}, bf16[256,128]{1,0:T(8,128)(2,1)S(1)}, u32[]{:S(2)}, u32[]{:S(2)}) %collective-permute-start.12) | collective-permute-done | bytes 65568 | tf_op jit(solution)/shard_map/ppermute | solution.py:43
  48.9 3.0 %collective-permute-start.14 = (bf16[1024,128]{1,0:T(8,128)(2,1)S(1)}, bf16[1024,128]{1,0:T(8,128)(2,1)S(1)}, u32[]{:S(2)}, u32[]{:S(2)}) collective-permute-start(bf16[1024,128]{1,0:T(8,128)(2,1)S(1)} %pad_maximum_fusion.1.rest_0_), channel_id=1, source_target_pairs={{0,1},{1,0},{2,3},{3,2},{4,5},{5,4},{6,7},{7,6},{8,9},{9,8},{10,11... | collective-permute-start | bytes 786440 | tf_op jit(solution)/shard_map/ppermute | solution.py:43
  53.0 1.7 %shard_map.70.band_ref = f32[32,128,128]{2,1,0:T(8,128)S(1)} custom-call(s32[128]{0:T(128)S(1)} %reshape.14.offsets_ref, bf16[32,128,128]{2,1,0:T(8,128)(2,1)S(1)} %get-tuple-element.116.table_ref.rest_1_, bf16[32,4,128,128]{3,2,1,0:T(8,128)(2,1)S(1)} %copy-done.2), custom_call_target="tpu_custom_call" | custom-call | flops 1 | bytes 1 | tf_op jit(solution)/shard_map/pallas_call | solution.py:73
  56.3 1.6 %shard_map.71 = (f32[32,128,128]{2,1,0:T(8,128)S(1)}, f32[128,128]{1,0:T(8,128)S(1)}) custom-call(s32[128]{0:T(128)S(1)} %reshape.14.offsets_ref, s32[3]{0:T(128)S(1)} %pad_add_fusion.side_ref, f32[32,128,128]{2,1,0:T(8,128)S(1)} %shard_map.70.band_ref, ...), custom_call_target="tpu_custom_call", output_to_operand_aliasing={{0}: (2, {})} | custom-call | flops 1 | bytes 1 | tf_op jit(solution)/shard_map/pallas_call | solution.py:73
  57.9 2.5 %collective-permute-start.17 = (bf16[1024,128]{1,0:T(8,128)(2,1)S(1)}, bf16[1024,128]{1,0:T(8,128)(2,1)S(1)}, u32[]{:S(2)}, u32[]{:S(2)}) collective-permute-start(bf16[1024,128]{1,0:T(8,128)(2,1)S(1)} %collective-permute-done.13.rest_1_), channel_id=1, source_target_pairs={{0,1},{1,0},{2,3},{3,2},{4,5},{5,4},{6,7},{7,6},{8,9},{9,8},{10,11... | collective-permute-start | bytes 786440 | tf_op jit(solution)/shard_map/ppermute | solution.py:43
  61.9 2.1 %shard_map.74.table_ref = bf16[32,128,128]{2,1,0:T(8,128)(2,1)S(1)} custom-call(s32[128]{0:T(128)S(1)} %reshape.13.place_ref, bf16[32,4,128,128]{3,2,1,0:T(8,128)(2,1)S(1)} %copy-done.4, f32[32,128,128]{2,1,0:T(8,128)S(1)} %get-tuple-element.129.band_ref, bf16[1024,128]{1,0:T(8,128)(2,1)S(1)} %pad_maximum_fusion.1.rest_0_, ...), custom_call_target="tpu_custom_call" | custom-call | flops 1 | bytes 1 | tf_op jit(solution)/shard_map/pallas_call | solution.py:73
  64.0 2.7 %collective-permute-done.18 = bf16[128,128]{1,0:T(8,128)(2,1)S(1)} collective-permute-done((bf16[128,128]{1,0:T(8,128)(2,1)S(1)}, bf16[128,128]{1,0:T(8,128)(2,1)S(1)}, u32[]{:S(2)}, u32[]{:S(2)}) %collective-permute-start.18) | collective-permute-done | bytes 32800 | tf_op jit(solution)/shard_map/ppermute | solution.py:43
  68.3 2.0 %collective-permute-start.21 = (bf16[256,128]{1,0:T(8,128)(2,1)S(1)}, bf16[256,128]{1,0:T(8,128)(2,1)S(1)}, u32[]{:S(2)}, u32[]{:S(2)}) collective-permute-start(bf16[256,128]{1,0:T(8,128)(2,1)S(1)} %pad_maximum_fusion.5), channel_id=1, source_target_pairs={{0,6},{1,7},{2,4},{3,5},{4,2},{5,3},{6,0},{7,1},{8,14},{9,15},{10,... | collective-permute-start | bytes 196616 | tf_op jit(solution)/shard_map/ppermute | solution.py:43
  70.9 2.3 %collective-permute-done.21 = bf16[256,128]{1,0:T(8,128)(2,1)S(1)} collective-permute-done((bf16[256,128]{1,0:T(8,128)(2,1)S(1)}, bf16[256,128]{1,0:T(8,128)(2,1)S(1)}, u32[]{:S(2)}, u32[]{:S(2)}) %collective-permute-start.21) | collective-permute-done | bytes 65568 | tf_op jit(solution)/shard_map/ppermute | solution.py:43
  74.0 3.3 %collective-permute-start.23 = (bf16[1024,128]{1,0:T(8,128)(2,1)S(1)}, bf16[1024,128]{1,0:T(8,128)(2,1)S(1)}, u32[]{:S(2)}, u32[]{:S(2)}) collective-permute-start(bf16[1024,128]{1,0:T(8,128)(2,1)S(1)} %pad_maximum_fusion.2.rest_1_), channel_id=1, source_target_pairs={{0,1},{1,0},{2,3},{3,2},{4,5},{5,4},{6,7},{7,6},{8,9},{9,8},{10,11... | collective-permute-start | bytes 786440 | tf_op jit(solution)/shard_map/ppermute | solution.py:43
  78.7 2.0 %shard_map.75 = (f32[32,128,128]{2,1,0:T(8,128)S(1)}, f32[32,128,128]{2,1,0:T(8,128)S(1)}) custom-call(s32[128]{0:T(128)S(1)} %reshape.14.offsets_ref, bf16[32,128,128]{2,1,0:T(8,128)(2,1)S(1)} %shard_map.74.table_ref, bf16[32,4,128,128]{3,2,1,0:T(8,128)(2,1)S(1)} %copy-done.2, bf16[32,128,128]{2,1,0:T(8,128)(2,1)S(1)} %bitcast.9, ...), custom_call_target="tpu_custom_call" | custom-call | flops 1 | bytes 1 | tf_op jit(solution)/shard_map/pallas_call | solution.py:73
  82.7 2.4 %collective-permute-start.26 = (bf16[1024,128]{1,0:T(8,128)(2,1)S(1)}, bf16[1024,128]{1,0:T(8,128)(2,1)S(1)}, u32[]{:S(2)}, u32[]{:S(2)}) collective-permute-start(bf16[1024,128]{1,0:T(8,128)(2,1)S(1)} %collective-permute-done.22.rest_2_), channel_id=1, source_target_pairs={{0,1},{1,0},{2,3},{3,2},{4,5},{5,4},{6,7},{7,6},{8,9},{9,8},{10,11... | collective-permute-start | bytes 786440 | tf_op jit(solution)/shard_map/ppermute | solution.py:43
  86.2 3.1 %shard_map.77 = bf16[32,128,128]{2,1,0:T(8,128)(2,1)} custom-call(s32[128]{0:T(128)S(1)} %reshape.13.place_ref, bf16[32,4,128,128]{3,2,1,0:T(8,128)(2,1)S(1)} %copy-done.4, f32[32,128,128]{2,1,0:T(8,128)S(1)} %shard_map.76.band_ref, f32[32,128,128]{2,1,0:T(8,128)S(1)} %get-tuple-element.150.rest_0_, bf16[1024,128]{1,0:T(8,128)(2,1)S(1)} %pad_maximum_fusion.2.rest_1_, ...), custom_call_target="tpu_custom_call" | custom-call | flops 1 | bytes 1 | tf_op jit(solution)/shard_map/pallas_call | solution.py:73
  (74 shorter events, 28.7 us)
Async XLA Ops:
  2.4 8.7 %collective-permute-start = (bf16[128,128]{1,0:T(8,128)(2,1)S(1)}, bf16[128,128]{1,0:T(8,128)(2,1)S(1)}, u32[]{:S(2)}, u32[]{:S(2)}) collective-permute-start(bf16[128,128]{1,0:T(8,128)(2,1)S(1)} %get-tuple-element.79), channel_id=1, source_target_pairs={{0,12},{1,13},{2,14},{3,15},{4,8},{5,9},{6,10},{7,11},{8,4},{9,5},... | collective-permute-start | bytes 98312 | tf_op jit(solution)/shard_map/ppermute | solution.py:43
  11.1 9.0 %collective-permute-start.2 = (bf16[256,128]{1,0:T(8,128)(2,1)S(1)}, bf16[256,128]{1,0:T(8,128)(2,1)S(1)}, u32[]{:S(2)}, u32[]{:S(2)}) collective-permute-start(bf16[256,128]{1,0:T(8,128)(2,1)S(1)} %pad_maximum_fusion.3), channel_id=1, source_target_pairs={{0,4},{1,5},{2,6},{3,7},{4,0},{5,1},{6,2},{7,3},{8,12},{9,13},{10,... | collective-permute-start | bytes 196616 | tf_op jit(solution)/shard_map/ppermute | solution.py:43
  12.4 7.7 %collective-permute-start.1 = (bf16[256,128]{1,0:T(8,128)(2,1)S(1)}, bf16[256,128]{1,0:T(8,128)(2,1)S(1)}, u32[]{:S(2)}, u32[]{:S(2)}) collective-permute-start(bf16[256,128]{1,0:T(8,128)(2,1)S(1)} %pad_maximum_fusion.3), channel_id=1, source_target_pairs={{0,2},{1,3},{2,0},{3,1},{4,6},{5,7},{6,4},{7,5},{8,10},{9,11},{10,... | collective-permute-start | bytes 196616 | tf_op jit(solution)/shard_map/ppermute | solution.py:43
  13.1 7.0 %collective-permute-start.3 = (bf16[256,128]{1,0:T(8,128)(2,1)S(1)}, bf16[256,128]{1,0:T(8,128)(2,1)S(1)}, u32[]{:S(2)}, u32[]{:S(2)}) collective-permute-start(bf16[256,128]{1,0:T(8,128)(2,1)S(1)} %pad_maximum_fusion.3), channel_id=1, source_target_pairs={{0,6},{1,7},{2,4},{3,5},{4,2},{5,3},{6,0},{7,1},{8,14},{9,15},{10,... | collective-permute-start | bytes 196616 | tf_op jit(solution)/shard_map/ppermute | solution.py:43
  20.1 8.7 %collective-permute-start.4 = (bf16[1024,128]{1,0:T(8,128)(2,1)S(1)}, bf16[1024,128]{1,0:T(8,128)(2,1)S(1)}, u32[]{:S(2)}, u32[]{:S(2)}) collective-permute-start(bf16[1024,128]{1,0:T(8,128)(2,1)S(1)} %pad_maximum_fusion.rest_1_), channel_id=1, source_target_pairs={{0,16},{1,17},{2,18},{3,19},{4,20},{5,21},{6,22},{7,23},{8,24},{9,... | collective-permute-start | bytes 786440 | tf_op jit(solution)/shard_map/ppermute | solution.py:43
  21.4 7.5 %collective-permute-start.5 = (bf16[1024,128]{1,0:T(8,128)(2,1)S(1)}, bf16[1024,128]{1,0:T(8,128)(2,1)S(1)}, u32[]{:S(2)}, u32[]{:S(2)}) collective-permute-start(bf16[1024,128]{1,0:T(8,128)(2,1)S(1)} %pad_maximum_fusion.rest_1_), channel_id=1, source_target_pairs={{0,1},{1,0},{2,3},{3,2},{4,5},{5,4},{6,7},{7,6},{8,9},{9,8},{10,11... | collective-permute-start | bytes 786440 | tf_op jit(solution)/shard_map/ppermute | solution.py:43
  23.5 4.3 %collective-permute-start.6 = (bf16[3,128,128]{2,1,0:T(8,128)(2,1)S(1)}, bf16[3,128,128]{2,1,0:T(8,128)(2,1)S(1)}, u32[]{:S(2)}, u32[]{:S(2)}) collective-permute-start(bf16[3,128,128]{2,1,0:T(8,128)(2,1)S(1)} %get-tuple-element.92), channel_id=1, source_target_pairs={{0,1},{1,0},{2,3},{3,2},{4,5},{5,4},{6,7},{7,6},{8,9},{9,8},{10,11... | collective-permute-start | bytes 294920 | tf_op jit(solution)/shard_map/ppermute | solution.py:43
  23.5 4.3 %collective-permute-start.7 = (bf16[3,128,128]{2,1,0:T(8,128)(2,1)S(1)}, bf16[3,128,128]{2,1,0:T(8,128)(2,1)S(1)}, u32[]{:S(2)}, u32[]{:S(2)}) collective-permute-start(bf16[3,128,128]{2,1,0:T(8,128)(2,1)S(1)} %get-tuple-element.93), channel_id=1, source_target_pairs={{0,31},{1,2},{2,1},{3,4},{4,3},{5,6},{6,5},{7,8},{8,7},{9,10},{10,... | collective-permute-start | bytes 294920 | tf_op jit(solution)/shard_map/ppermute | solution.py:43
  28.9 4.7 %collective-permute-start.8 = (bf16[1024,128]{1,0:T(8,128)(2,1)S(1)}, bf16[1024,128]{1,0:T(8,128)(2,1)S(1)}, u32[]{:S(2)}, u32[]{:S(2)}) collective-permute-start(bf16[1024,128]{1,0:T(8,128)(2,1)S(1)} %collective-permute-done.4.rest_2_), channel_id=1, source_target_pairs={{0,1},{1,0},{2,3},{3,2},{4,5},{5,4},{6,7},{7,6},{8,9},{9,8},{10,11... | collective-permute-start | bytes 786440 | tf_op jit(solution)/shard_map/ppermute | solution.py:43
  36.1 5.0 %collective-permute-start.9 = (bf16[128,128]{1,0:T(8,128)(2,1)S(1)}, bf16[128,128]{1,0:T(8,128)(2,1)S(1)}, u32[]{:S(2)}, u32[]{:S(2)}) collective-permute-start(bf16[128,128]{1,0:T(8,128)(2,1)S(1)} %get-tuple-element.104), channel_id=1, source_target_pairs={{0,12},{1,13},{2,14},{3,15},{4,8},{5,9},{6,10},{7,11},{8,4},{9,5},... | collective-permute-start | bytes 98312 | tf_op jit(solution)/shard_map/ppermute | solution.py:43
  41.8 4.3 %collective-permute-start.11 = (bf16[256,128]{1,0:T(8,128)(2,1)S(1)}, bf16[256,128]{1,0:T(8,128)(2,1)S(1)}, u32[]{:S(2)}, u32[]{:S(2)}) collective-permute-start(bf16[256,128]{1,0:T(8,128)(2,1)S(1)} %pad_maximum_fusion.4), channel_id=1, source_target_pairs={{0,4},{1,5},{2,6},{3,7},{4,0},{5,1},{6,2},{7,3},{8,12},{9,13},{10,... | collective-permute-start | bytes 196616 | tf_op jit(solution)/shard_map/ppermute | solution.py:43
  43.3 5.5 %collective-permute-start.12 = (bf16[256,128]{1,0:T(8,128)(2,1)S(1)}, bf16[256,128]{1,0:T(8,128)(2,1)S(1)}, u32[]{:S(2)}, u32[]{:S(2)}) collective-permute-start(bf16[256,128]{1,0:T(8,128)(2,1)S(1)} %pad_maximum_fusion.4), channel_id=1, source_target_pairs={{0,6},{1,7},{2,4},{3,5},{4,2},{5,3},{6,0},{7,1},{8,14},{9,15},{10,... | collective-permute-start | bytes 196616 | tf_op jit(solution)/shard_map/ppermute | solution.py:43
  48.8 9.1 %collective-permute-start.13 = (bf16[1024,128]{1,0:T(8,128)(2,1)S(1)}, bf16[1024,128]{1,0:T(8,128)(2,1)S(1)}, u32[]{:S(2)}, u32[]{:S(2)}) collective-permute-start(bf16[1024,128]{1,0:T(8,128)(2,1)S(1)} %pad_maximum_fusion.1.rest_0_), channel_id=1, source_target_pairs={{0,16},{1,17},{2,18},{3,19},{4,20},{5,21},{6,22},{7,23},{8,24},{9,... | collective-permute-start | bytes 786440 | tf_op jit(solution)/shard_map/ppermute | solution.py:43
  48.9 9.0 %collective-permute-start.14 = (bf16[1024,128]{1,0:T(8,128)(2,1)S(1)}, bf16[1024,128]{1,0:T(8,128)(2,1)S(1)}, u32[]{:S(2)}, u32[]{:S(2)}) collective-permute-start(bf16[1024,128]{1,0:T(8,128)(2,1)S(1)} %pad_maximum_fusion.1.rest_0_), channel_id=1, source_target_pairs={{0,1},{1,0},{2,3},{3,2},{4,5},{5,4},{6,7},{7,6},{8,9},{9,8},{10,11... | collective-permute-start | bytes 786440 | tf_op jit(solution)/shard_map/ppermute | solution.py:43
  52.0 4.3 %collective-permute-start.16 = (bf16[3,128,128]{2,1,0:T(8,128)(2,1)S(1)}, bf16[3,128,128]{2,1,0:T(8,128)(2,1)S(1)}, u32[]{:S(2)}, u32[]{:S(2)}) collective-permute-start(bf16[3,128,128]{2,1,0:T(8,128)(2,1)S(1)} %get-tuple-element.115), channel_id=1, source_target_pairs={{0,31},{1,2},{2,1},{3,4},{4,3},{5,6},{6,5},{7,8},{8,7},{9,10},{10,... | collective-permute-start | bytes 294920 | tf_op jit(solution)/shard_map/ppermute | solution.py:43
  57.9 3.7 %collective-permute-start.17 = (bf16[1024,128]{1,0:T(8,128)(2,1)S(1)}, bf16[1024,128]{1,0:T(8,128)(2,1)S(1)}, u32[]{:S(2)}, u32[]{:S(2)}) collective-permute-start(bf16[1024,128]{1,0:T(8,128)(2,1)S(1)} %collective-permute-done.13.rest_1_), channel_id=1, source_target_pairs={{0,1},{1,0},{2,3},{3,2},{4,5},{5,4},{6,7},{7,6},{8,9},{9,8},{10,11... | collective-permute-start | bytes 786440 | tf_op jit(solution)/shard_map/ppermute | solution.py:43
  61.8 5.0 %collective-permute-start.18 = (bf16[128,128]{1,0:T(8,128)(2,1)S(1)}, bf16[128,128]{1,0:T(8,128)(2,1)S(1)}, u32[]{:S(2)}, u32[]{:S(2)}) collective-permute-start(bf16[128,128]{1,0:T(8,128)(2,1)S(1)} %shard_map.73), channel_id=1, source_target_pairs={{0,12},{1,13},{2,14},{3,15},{4,8},{5,9},{6,10},{7,11},{8,4},{9,5},... | collective-permute-start | bytes 98312 | tf_op jit(solution)/shard_map/ppermute | solution.py:43
  66.8 3.6 %collective-permute-start.19 = (bf16[256,128]{1,0:T(8,128)(2,1)S(1)}, bf16[256,128]{1,0:T(8,128)(2,1)S(1)}, u32[]{:S(2)}, u32[]{:S(2)}) collective-permute-start(bf16[256,128]{1,0:T(8,128)(2,1)S(1)} %pad_maximum_fusion.5), channel_id=1, source_target_pairs={{0,2},{1,3},{2,0},{3,1},{4,6},{5,7},{6,4},{7,5},{8,10},{9,11},{10,... | collective-permute-start | bytes 196616 | tf_op jit(solution)/shard_map/ppermute | solution.py:43
  66.8 4.1 %collective-permute-start.20 = (bf16[256,128]{1,0:T(8,128)(2,1)S(1)}, bf16[256,128]{1,0:T(8,128)(2,1)S(1)}, u32[]{:S(2)}, u32[]{:S(2)}) collective-permute-start(bf16[256,128]{1,0:T(8,128)(2,1)S(1)} %pad_maximum_fusion.5), channel_id=1, source_target_pairs={{0,4},{1,5},{2,6},{3,7},{4,0},{5,1},{6,2},{7,3},{8,12},{9,13},{10,... | collective-permute-start | bytes 196616 | tf_op jit(solution)/shard_map/ppermute | solution.py:43
  68.3 4.9 %collective-permute-start.21 = (bf16[256,128]{1,0:T(8,128)(2,1)S(1)}, bf16[256,128]{1,0:T(8,128)(2,1)S(1)}, u32[]{:S(2)}, u32[]{:S(2)}) collective-permute-start(bf16[256,128]{1,0:T(8,128)(2,1)S(1)} %pad_maximum_fusion.5), channel_id=1, source_target_pairs={{0,6},{1,7},{2,4},{3,5},{4,2},{5,3},{6,0},{7,1},{8,14},{9,15},{10,... | collective-permute-start | bytes 196616 | tf_op jit(solution)/shard_map/ppermute | solution.py:43
  73.2 9.4 %collective-permute-start.22 = (bf16[1024,128]{1,0:T(8,128)(2,1)S(1)}, bf16[1024,128]{1,0:T(8,128)(2,1)S(1)}, u32[]{:S(2)}, u32[]{:S(2)}) collective-permute-start(bf16[1024,128]{1,0:T(8,128)(2,1)S(1)} %pad_maximum_fusion.2.rest_1_), channel_id=1, source_target_pairs={{0,16},{1,17},{2,18},{3,19},{4,20},{5,21},{6,22},{7,23},{8,24},{9,... | collective-permute-start | bytes 786440 | tf_op jit(solution)/shard_map/ppermute | solution.py:43
  74.0 8.6 %collective-permute-start.23 = (bf16[1024,128]{1,0:T(8,128)(2,1)S(1)}, bf16[1024,128]{1,0:T(8,128)(2,1)S(1)}, u32[]{:S(2)}, u32[]{:S(2)}) collective-permute-start(bf16[1024,128]{1,0:T(8,128)(2,1)S(1)} %pad_maximum_fusion.2.rest_1_), channel_id=1, source_target_pairs={{0,1},{1,0},{2,3},{3,2},{4,5},{5,4},{6,7},{7,6},{8,9},{9,8},{10,11... | collective-permute-start | bytes 786440 | tf_op jit(solution)/shard_map/ppermute | solution.py:43
  77.3 4.3 %collective-permute-start.25 = (bf16[3,128,128]{2,1,0:T(8,128)(2,1)S(1)}, bf16[3,128,128]{2,1,0:T(8,128)(2,1)S(1)}, u32[]{:S(2)}, u32[]{:S(2)}) collective-permute-start(bf16[3,128,128]{2,1,0:T(8,128)(2,1)S(1)} %get-tuple-element.143), channel_id=1, source_target_pairs={{0,31},{1,2},{2,1},{3,4},{4,3},{5,6},{6,5},{7,8},{8,7},{9,10},{10,... | collective-permute-start | bytes 294920 | tf_op jit(solution)/shard_map/ppermute | solution.py:43
  82.7 3.6 %collective-permute-start.26 = (bf16[1024,128]{1,0:T(8,128)(2,1)S(1)}, bf16[1024,128]{1,0:T(8,128)(2,1)S(1)}, u32[]{:S(2)}, u32[]{:S(2)}) collective-permute-start(bf16[1024,128]{1,0:T(8,128)(2,1)S(1)} %collective-permute-done.22.rest_2_), channel_id=1, source_target_pairs={{0,1},{1,0},{2,3},{3,2},{4,5},{5,4},{6,7},{7,6},{8,9},{9,8},{10,11... | collective-permute-start | bytes 786440 | tf_op jit(solution)/shard_map/ppermute | solution.py:43
  (10 other events, 44.0 us)

commit v5 on v4

--- a/solution.py
+++ b/solution.py
@@ -99,10 +99,6 @@
         table = table_ref[b : b + CHUNK].reshape(CHUNK * BLOCK, -1)
         total += dot(one_hot(ids, b * BLOCK, CHUNK), table)
     out_ref[...] = total.astype(out_ref.dtype)
-
-
-def touch_kernel(*refs):
-    refs[-1][...] = jnp.zeros_like(refs[-1])
 
 
 def expand_kernel(level, place_ref, columns_ref, tiles_ref, out_ref):
@@ -325,20 +321,17 @@
             tables.append(table)
         pair, columns = together(jnp.concatenate([picked, across]), columns)
         near = [permute(pair, along_z(g)) for g in (1, 2, 3)]
-        if level == 0:
-            held = call(touch_kernel, f32(8, BLOCK), (), (columns, hub_tiles, band_tiles), 2**20)
-            near[1], held = together(near[1], held)
         *near, rim_inner, rim_outer, table = together(*near, *edges(table), table)
         column, table = together(jnp.concatenate([pair] + near), table)
         x_column = permute(column, ACROSS_X)
-        core_column = permute(column, ACROSS_CORE)
         halos = exchange((rim_inner, rim_outer))
-        extra = ([held], [], tables[:-1])[level]
+        extra = ([], [], tables[:-1])[level]
         band, *base = inner_products(level, offsets, table, band_tiles, extra)
         *halos, band = together(*halos, band)
         extra = [columns] if level == 1 else []
         band, *more = rim_products(level, offsets, side, band, table, halos, band_tiles, extra)
-        x_column, core_column, band, *more = together(x_column, core_column, band, *more)
+        core_in, band, *more = together(column, band, *more)
+        core_column = permute(core_in, ACROSS_CORE)
         far = permute(x_column, ACROSS_CORE)
         pieces = [column, x_column, core_column, far]
         if level == 0:

time: 89.7 us -> 88.9 us (level)
  waiting for transfers between devices: 16.5 us -> 22.2 us
  local copies, waits for them, and re-layouts: 9.84 us -> 5.47 us
  starting transfers between devices: 41.2 us -> 39.3 us
    ppermute x27, waiting for transfers between devices: 16.5 us -> 22.2 us  [permute(): return lax.ppermute(array, 'row', pairs)]
    unnamed x15 -> x11, local copies, waits for them, and re-layouts: 8.56 us -> 4.2 us
    ppermute x27, starting transfers between devices: 41.2 us -> 39.3 us  [permute(): return lax.ppermute(array, 'row', pairs)]
    pallas_call x14 -> x13, Pallas kernels: 20 us -> 19.9 us  [call(): pl.pallas_call(kernel, in_specs=[smem] * len(scalars) + [vmem] * len(arra...]
  transfers between devices with their start and end apart: 27 -> 27, of which waited for: 12 -> 15; matrix products, arithmetic and copies ran while one was open for 3% -> 3% of each run, Pallas kernels for 15% -> 15%
where the time goes in v5:
time: 88.9 us; the launch traced here: 88.7 us
  starting transfers between devices  39.3 us (44%)
  waiting for transfers between devices  22.2 us (25%)
  Pallas kernels  19.9 us (22%)
  local copies, waits for them, and re-layouts  5.47 us (6%)
  other arithmetic  1.52 us (2%)
    ppermute x27, starting transfers between devices, permute(): return lax.ppermute(array, 'row', pairs)  39.3 us
    ppermute x27, waiting for transfers between devices, permute(): return lax.ppermute(array, 'row', pairs)  22.2 us
    pallas_call x13, Pallas kernels, call(): pl.pallas_call(kernel, in_specs=[smem] * len(scalars) + [vmem] * len(arra...  19.9 us
    unnamed x11, local copies, waits for them, and re-layouts  4.2 us
  transfers between devices with their start and end apart: 27, of which 15 were waited for; matrix products, arithmetic and copies ran while one was open for 3% of the time, Pallas kernels for 15%

profile of v5, /device:TPU:1, one launch (start us, length us, event | category | flops | bytes accessed | tf_op | source)
XLA Modules:
  0.0 88.7 jit_solution(9808897466330998238)
XLA Ops:
  2.4 6.9 %collective-permute-start = (bf16[128,128]{1,0:T(8,128)(2,1)S(1)}, bf16[128,128]{1,0:T(8,128)(2,1)S(1)}, u32[]{:S(2)}, u32[]{:S(2)}) collective-permute-start(bf16[128,128]{1,0:T(8,128)(2,1)S(1)} %get-tuple-element.74), channel_id=1, source_target_pairs={{0,12},{1,13},{2,14},{3,15},{4,8},{5,9},{6,10},{7,11},{8,4},{9,5},... | collective-permute-start | bytes 98312 | tf_op jit(solution)/shard_map/ppermute | solution.py:43
  13.1 1.6 %collective-permute-start.3 = (bf16[256,128]{1,0:T(8,128)(2,1)S(1)}, bf16[256,128]{1,0:T(8,128)(2,1)S(1)}, u32[]{:S(2)}, u32[]{:S(2)}) collective-permute-start(bf16[256,128]{1,0:T(8,128)(2,1)S(1)} %pad_maximum_fusion.3), channel_id=1, source_target_pairs={{0,6},{1,7},{2,4},{3,5},{4,2},{5,3},{6,0},{7,1},{8,14},{9,15},{10,... | collective-permute-start | bytes 196616 | tf_op jit(solution)/shard_map/ppermute | solution.py:43
  16.6 2.1 %collective-permute-done.3 = bf16[256,128]{1,0:T(8,128)(2,1)S(1)} collective-permute-done((bf16[256,128]{1,0:T(8,128)(2,1)S(1)}, bf16[256,128]{1,0:T(8,128)(2,1)S(1)}, u32[]{:S(2)}, u32[]{:S(2)}) %collective-permute-start.3) | collective-permute-done | bytes 65568 | tf_op jit(solution)/shard_map/ppermute | solution.py:43
  20.1 2.9 %collective-permute-start.4 = (bf16[3,128,128]{2,1,0:T(8,128)(2,1)S(1)}, bf16[3,128,128]{2,1,0:T(8,128)(2,1)S(1)}, u32[]{:S(2)}, u32[]{:S(2)}) collective-permute-start(bf16[3,128,128]{2,1,0:T(8,128)(2,1)S(1)} %get-tuple-element.85), channel_id=1, source_target_pairs={{0,1},{1,0},{2,3},{3,2},{4,5},{5,4},{6,7},{7,6},{8,9},{9,8},{10,11... | collective-permute-start | bytes 294920 | tf_op jit(solution)/shard_map/ppermute | solution.py:43
  23.4 2.2 %copy-done = bf16[32,4,128,128]{3,2,1,0:T(8,128)(2,1)S(1)} copy-done((bf16[32,4,128,128]{3,2,1,0:T(8,128)(2,1)S(1)}, bf16[32,4,128,128]{3,2,1,0:T(8,128)(2,1)}, u32[]{:S(2)}) %copy-start) | copy-done | bytes 4194328
  25.6 1.7 %shard_map.65.band_ref = f32[32,128,128]{2,1,0:T(8,128)S(1)} custom-call(s32[128]{0:T(128)S(1)} %reshape.14.offsets_ref, bf16[32,128,128]{2,1,0:T(8,128)(2,1)S(1)} %bitcast.7, bf16[32,4,128,128]{3,2,1,0:T(8,128)(2,1)S(1)} %copy-done), custom_call_target="tpu_custom_call" | custom-call | flops 1 | bytes 1 | tf_op jit(solution)/shard_map/pallas_call | solution.py:73
  28.4 2.9 %collective-permute-start.7 = (bf16[1024,128]{1,0:T(8,128)(2,1)S(1)}, bf16[1024,128]{1,0:T(8,128)(2,1)S(1)}, u32[]{:S(2)}, u32[]{:S(2)}) collective-permute-start(bf16[1024,128]{1,0:T(8,128)(2,1)S(1)} %pad_maximum_fusion.rest_1_), channel_id=1, source_target_pairs={{0,1},{1,0},{2,3},{3,2},{4,5},{5,4},{6,7},{7,6},{8,9},{9,8},{10,11... | collective-permute-start | bytes 786440 | tf_op jit(solution)/shard_map/ppermute | solution.py:43
  32.9 2.4 %shard_map.67 = (bf16[32,128,128]{2,1,0:T(8,128)(2,1)S(1)}, bf16[128,128]{1,0:T(8,128)(2,1)S(1)}) custom-call(s32[128]{0:T(128)S(1)} %reshape.13.place_ref, bf16[32,4,128,128]{3,2,1,0:T(8,128)(2,1)S(1)} %copy-done.2, f32[32,128,128]{2,1,0:T(8,128)S(1)} %shard_map.66.band_ref, s32[2,128,128]{2,1,0:T(8,128)S(1)} %get-tuple-element.112.rest_0_.columns_ref, ...), custom_call_target="tpu_custom_call" | custom-call | flops 1 | bytes 1 | tf_op jit(solution)/shard_map/pallas_call | solution.py:73
  36.4 2.3 %shard_map.68.spread_ref = bf16[32,128,128]{2,1,0:T(8,128)(2,1)S(1)} custom-call(s32[128]{0:T(128)S(1)} %reshape.13.place_ref, s32[2,128,128]{2,1,0:T(8,128)S(1)} %get-tuple-element.112.rest_0_.columns_ref, bf16[32,4,128,128]{3,2,1,0:T(8,128)(2,1)S(1)} %copy-done.2), custom_call_target="tpu_custom_call" | custom-call | flops 1 | bytes 1 | tf_op jit(solution)/shard_map/pallas_call | solution.py:73
  42.1 1.7 %collective-permute-start.12 = (bf16[256,128]{1,0:T(8,128)(2,1)S(1)}, bf16[256,128]{1,0:T(8,128)(2,1)S(1)}, u32[]{:S(2)}, u32[]{:S(2)}) collective-permute-start(bf16[256,128]{1,0:T(8,128)(2,1)S(1)} %pad_maximum_fusion.4), channel_id=1, source_target_pairs={{0,6},{1,7},{2,4},{3,5},{4,2},{5,3},{6,0},{7,1},{8,14},{9,15},{10,... | collective-permute-start | bytes 196616 | tf_op jit(solution)/shard_map/ppermute | solution.py:43
  43.8 2.3 %collective-permute-done.11 = bf16[256,128]{1,0:T(8,128)(2,1)S(1)} collective-permute-done((bf16[256,128]{1,0:T(8,128)(2,1)S(1)}, bf16[256,128]{1,0:T(8,128)(2,1)S(1)}, u32[]{:S(2)}, u32[]{:S(2)}) %collective-permute-start.11) | collective-permute-done | bytes 65568 | tf_op jit(solution)/shard_map/ppermute | solution.py:43
  47.6 3.3 %collective-permute-start.13 = (bf16[3,128,128]{2,1,0:T(8,128)(2,1)S(1)}, bf16[3,128,128]{2,1,0:T(8,128)(2,1)S(1)}, u32[]{:S(2)}, u32[]{:S(2)}) collective-permute-start(bf16[3,128,128]{2,1,0:T(8,128)(2,1)S(1)} %get-tuple-element.106), channel_id=1, source_target_pairs={{0,1},{1,0},{2,3},{3,2},{4,5},{5,4},{6,7},{7,6},{8,9},{9,8},{10,11... | collective-permute-start | bytes 294920 | tf_op jit(solution)/shard_map/ppermute | solution.py:43
  51.7 1.7 %shard_map.69.band_ref = f32[32,128,128]{2,1,0:T(8,128)S(1)} custom-call(s32[128]{0:T(128)S(1)} %reshape.14.offsets_ref, bf16[32,128,128]{2,1,0:T(8,128)(2,1)S(1)} %get-tuple-element.108.table_ref.rest_1_, bf16[32,4,128,128]{3,2,1,0:T(8,128)(2,1)S(1)} %copy-done.1), custom_call_target="tpu_custom_call" | custom-call | flops 1 | bytes 1 | tf_op jit(solution)/shard_map/pallas_call | solution.py:73
  53.5 1.7 %collective-permute-done.14.outer_ref = bf16[3,128,128]{2,1,0:T(8,128)(2,1)S(1)} collective-permute-done((bf16[3,128,128]{2,1,0:T(8,128)(2,1)S(1)}, bf16[3,128,128]{2,1,0:T(8,128)(2,1)S(1)}, u32[]{:S(2)}, u32[]{:S(2)}) %collective-permute-start.14) | collective-permute-done | bytes 98336 | tf_op jit(solution)/shard_map/ppermute | solution.py:43
  56.8 2.0 %collective-permute-start.16 = (bf16[1024,128]{1,0:T(8,128)(2,1)S(1)}, bf16[1024,128]{1,0:T(8,128)(2,1)S(1)}, u32[]{:S(2)}, u32[]{:S(2)}) collective-permute-start(bf16[1024,128]{1,0:T(8,128)(2,1)S(1)} %pad_maximum_fusion.1.rest_0_), channel_id=1, source_target_pairs={{0,1},{1,0},{2,3},{3,2},{4,5},{5,4},{6,7},{7,6},{8,9},{9,8},{10,11... | collective-permute-start | bytes 786440 | tf_op jit(solution)/shard_map/ppermute | solution.py:43
  61.1 2.1 %shard_map.73.table_ref = bf16[32,128,128]{2,1,0:T(8,128)(2,1)S(1)} custom-call(s32[128]{0:T(128)S(1)} %reshape.13.place_ref, bf16[32,4,128,128]{3,2,1,0:T(8,128)(2,1)S(1)} %copy-done.2, f32[32,128,128]{2,1,0:T(8,128)S(1)} %get-tuple-element.120.band_ref, bf16[1024,128]{1,0:T(8,128)(2,1)S(1)} %pad_maximum_fusion.1.rest_0_, ...), custom_call_target="tpu_custom_call" | custom-call | flops 1 | bytes 1 | tf_op jit(solution)/shard_map/pallas_call | solution.py:73
  63.2 2.4 %collective-permute-done.18 = bf16[128,128]{1,0:T(8,128)(2,1)S(1)} collective-permute-done((bf16[128,128]{1,0:T(8,128)(2,1)S(1)}, bf16[128,128]{1,0:T(8,128)(2,1)S(1)}, u32[]{:S(2)}, u32[]{:S(2)}) %collective-permute-start.18) | collective-permute-done | bytes 32800 | tf_op jit(solution)/shard_map/ppermute | solution.py:43
  65.6 2.3 %collective-permute-start.20 = (bf16[256,128]{1,0:T(8,128)(2,1)S(1)}, bf16[256,128]{1,0:T(8,128)(2,1)S(1)}, u32[]{:S(2)}, u32[]{:S(2)}) collective-permute-start(bf16[256,128]{1,0:T(8,128)(2,1)S(1)} %pad_maximum_fusion.5), channel_id=1, source_target_pairs={{0,4},{1,5},{2,6},{3,7},{4,0},{5,1},{6,2},{7,3},{8,12},{9,13},{10,... | collective-permute-start | bytes 196616 | tf_op jit(solution)/shard_map/ppermute | solution.py:43
  69.6 3.7 %collective-permute-done.21 = bf16[256,128]{1,0:T(8,128)(2,1)S(1)} collective-permute-done((bf16[256,128]{1,0:T(8,128)(2,1)S(1)}, bf16[256,128]{1,0:T(8,128)(2,1)S(1)}, u32[]{:S(2)}, u32[]{:S(2)}) %collective-permute-start.21) | collective-permute-done | bytes 65568 | tf_op jit(solution)/shard_map/ppermute | solution.py:43
  73.5 3.2 %collective-permute-start.22 = (bf16[3,128,128]{2,1,0:T(8,128)(2,1)S(1)}, bf16[3,128,128]{2,1,0:T(8,128)(2,1)S(1)}, u32[]{:S(2)}, u32[]{:S(2)}) collective-permute-start(bf16[3,128,128]{2,1,0:T(8,128)(2,1)S(1)} %get-tuple-element.133), channel_id=1, source_target_pairs={{0,1},{1,0},{2,3},{3,2},{4,5},{5,4},{6,7},{7,6},{8,9},{9,8},{10,11... | collective-permute-start | bytes 294920 | tf_op jit(solution)/shard_map/ppermute | solution.py:43
  76.9 2.0 %shard_map.74 = (f32[32,128,128]{2,1,0:T(8,128)S(1)}, f32[32,128,128]{2,1,0:T(8,128)S(1)}) custom-call(s32[128]{0:T(128)S(1)} %reshape.14.offsets_ref, bf16[32,128,128]{2,1,0:T(8,128)(2,1)S(1)} %shard_map.73.table_ref, bf16[32,4,128,128]{3,2,1,0:T(8,128)(2,1)S(1)} %copy-done.1, bf16[32,128,128]{2,1,0:T(8,128)(2,1)S(1)} %bitcast.9, ...), custom_call_target="tpu_custom_call" | custom-call | flops 1 | bytes 1 | tf_op jit(solution)/shard_map/pallas_call | solution.py:73
  78.8 2.1 %collective-permute-done.23.outer_ref = bf16[3,128,128]{2,1,0:T(8,128)(2,1)S(1)} collective-permute-done((bf16[3,128,128]{2,1,0:T(8,128)(2,1)S(1)}, bf16[3,128,128]{2,1,0:T(8,128)(2,1)S(1)}, u32[]{:S(2)}, u32[]{:S(2)}) %collective-permute-start.23) | collective-permute-done | bytes 98336 | tf_op jit(solution)/shard_map/ppermute | solution.py:43
  82.0 2.0 %collective-permute-start.25 = (bf16[1024,128]{1,0:T(8,128)(2,1)S(1)}, bf16[1024,128]{1,0:T(8,128)(2,1)S(1)}, u32[]{:S(2)}, u32[]{:S(2)}) collective-permute-start(bf16[1024,128]{1,0:T(8,128)(2,1)S(1)} %pad_maximum_fusion.2.rest_1_), channel_id=1, source_target_pairs={{0,1},{1,0},{2,3},{3,2},{4,5},{5,4},{6,7},{7,6},{8,9},{9,8},{10,11... | collective-permute-start | bytes 786440 | tf_op jit(solution)/shard_map/ppermute | solution.py:43
  85.5 3.1 %shard_map.76 = bf16[32,128,128]{2,1,0:T(8,128)(2,1)} custom-call(s32[128]{0:T(128)S(1)} %reshape.13.place_ref, bf16[32,4,128,128]{3,2,1,0:T(8,128)(2,1)S(1)} %copy-done.2, f32[32,128,128]{2,1,0:T(8,128)S(1)} %shard_map.75.band_ref, f32[32,128,128]{2,1,0:T(8,128)S(1)} %get-tuple-element.141.rest_0_, bf16[1024,128]{1,0:T(8,128)(2,1)S(1)} %pad_maximum_fusion.2.rest_1_, ...), custom_call_target="tpu_custom_call" | custom-call | flops 1 | bytes 1 | tf_op jit(solution)/shard_map/pallas_call | solution.py:73
  (69 shorter events, 27.6 us)
Async XLA Ops:
  2.4 8.7 %collective-permute-start = (bf16[128,128]{1,0:T(8,128)(2,1)S(1)}, bf16[128,128]{1,0:T(8,128)(2,1)S(1)}, u32[]{:S(2)}, u32[]{:S(2)}) collective-permute-start(bf16[128,128]{1,0:T(8,128)(2,1)S(1)} %get-tuple-element.74), channel_id=1, source_target_pairs={{0,12},{1,13},{2,14},{3,15},{4,8},{5,9},{6,10},{7,11},{8,4},{9,5},... | collective-permute-start | bytes 98312 | tf_op jit(solution)/shard_map/ppermute | solution.py:43
  11.1 4.6 %collective-permute-start.1 = (bf16[256,128]{1,0:T(8,128)(2,1)S(1)}, bf16[256,128]{1,0:T(8,128)(2,1)S(1)}, u32[]{:S(2)}, u32[]{:S(2)}) collective-permute-start(bf16[256,128]{1,0:T(8,128)(2,1)S(1)} %pad_maximum_fusion.3), channel_id=1, source_target_pairs={{0,2},{1,3},{2,0},{3,1},{4,6},{5,7},{6,4},{7,5},{8,10},{9,11},{10,... | collective-permute-start | bytes 196616 | tf_op jit(solution)/shard_map/ppermute | solution.py:43
  11.9 4.7 %collective-permute-start.2 = (bf16[256,128]{1,0:T(8,128)(2,1)S(1)}, bf16[256,128]{1,0:T(8,128)(2,1)S(1)}, u32[]{:S(2)}, u32[]{:S(2)}) collective-permute-start(bf16[256,128]{1,0:T(8,128)(2,1)S(1)} %pad_maximum_fusion.3), channel_id=1, source_target_pairs={{0,4},{1,5},{2,6},{3,7},{4,0},{5,1},{6,2},{7,3},{8,12},{9,13},{10,... | collective-permute-start | bytes 196616 | tf_op jit(solution)/shard_map/ppermute | solution.py:43
  13.1 5.6 %collective-permute-start.3 = (bf16[256,128]{1,0:T(8,128)(2,1)S(1)}, bf16[256,128]{1,0:T(8,128)(2,1)S(1)}, u32[]{:S(2)}, u32[]{:S(2)}) collective-permute-start(bf16[256,128]{1,0:T(8,128)(2,1)S(1)} %pad_maximum_fusion.3), channel_id=1, source_target_pairs={{0,6},{1,7},{2,4},{3,5},{4,2},{5,3},{6,0},{7,1},{8,14},{9,15},{10,... | collective-permute-start | bytes 196616 | tf_op jit(solution)/shard_map/ppermute | solution.py:43
  18.8 12.6 %collective-permute-start.6 = (bf16[1024,128]{1,0:T(8,128)(2,1)S(1)}, bf16[1024,128]{1,0:T(8,128)(2,1)S(1)}, u32[]{:S(2)}, u32[]{:S(2)}) collective-permute-start(bf16[1024,128]{1,0:T(8,128)(2,1)S(1)} %pad_maximum_fusion.rest_1_), channel_id=1, source_target_pairs={{0,16},{1,17},{2,18},{3,19},{4,20},{5,21},{6,22},{7,23},{8,24},{9,... | collective-permute-start | bytes 786440 | tf_op jit(solution)/shard_map/ppermute | solution.py:43
  20.1 7.3 %collective-permute-start.4 = (bf16[3,128,128]{2,1,0:T(8,128)(2,1)S(1)}, bf16[3,128,128]{2,1,0:T(8,128)(2,1)S(1)}, u32[]{:S(2)}, u32[]{:S(2)}) collective-permute-start(bf16[3,128,128]{2,1,0:T(8,128)(2,1)S(1)} %get-tuple-element.85), channel_id=1, source_target_pairs={{0,1},{1,0},{2,3},{3,2},{4,5},{5,4},{6,7},{7,6},{8,9},{9,8},{10,11... | collective-permute-start | bytes 294920 | tf_op jit(solution)/shard_map/ppermute | solution.py:43
  23.0 4.4 %collective-permute-start.5 = (bf16[3,128,128]{2,1,0:T(8,128)(2,1)S(1)}, bf16[3,128,128]{2,1,0:T(8,128)(2,1)S(1)}, u32[]{:S(2)}, u32[]{:S(2)}) collective-permute-start(bf16[3,128,128]{2,1,0:T(8,128)(2,1)S(1)} %get-tuple-element.86), channel_id=1, source_target_pairs={{0,31},{1,2},{2,1},{3,4},{4,3},{5,6},{6,5},{7,8},{8,7},{9,10},{10,... | collective-permute-start | bytes 294920 | tf_op jit(solution)/shard_map/ppermute | solution.py:43
  28.4 4.1 %collective-permute-start.7 = (bf16[1024,128]{1,0:T(8,128)(2,1)S(1)}, bf16[1024,128]{1,0:T(8,128)(2,1)S(1)}, u32[]{:S(2)}, u32[]{:S(2)}) collective-permute-start(bf16[1024,128]{1,0:T(8,128)(2,1)S(1)} %pad_maximum_fusion.rest_1_), channel_id=1, source_target_pairs={{0,1},{1,0},{2,3},{3,2},{4,5},{5,4},{6,7},{7,6},{8,9},{9,8},{10,11... | collective-permute-start | bytes 786440 | tf_op jit(solution)/shard_map/ppermute | solution.py:43
  35.3 5.0 %collective-permute-start.9 = (bf16[128,128]{1,0:T(8,128)(2,1)S(1)}, bf16[128,128]{1,0:T(8,128)(2,1)S(1)}, u32[]{:S(2)}, u32[]{:S(2)}) collective-permute-start(bf16[128,128]{1,0:T(8,128)(2,1)S(1)} %get-tuple-element.96), channel_id=1, source_target_pairs={{0,12},{1,13},{2,14},{3,15},{4,8},{5,9},{6,10},{7,11},{8,4},{9,5},... | collective-permute-start | bytes 98312 | tf_op jit(solution)/shard_map/ppermute | solution.py:43
  40.3 3.6 %collective-permute-start.10 = (bf16[256,128]{1,0:T(8,128)(2,1)S(1)}, bf16[256,128]{1,0:T(8,128)(2,1)S(1)}, u32[]{:S(2)}, u32[]{:S(2)}) collective-permute-start(bf16[256,128]{1,0:T(8,128)(2,1)S(1)} %pad_maximum_fusion.4), channel_id=1, source_target_pairs={{0,2},{1,3},{2,0},{3,1},{4,6},{5,7},{6,4},{7,5},{8,10},{9,11},{10,... | collective-permute-start | bytes 196616 | tf_op jit(solution)/shard_map/ppermute | solution.py:43
  41.1 5.1 %collective-permute-start.11 = (bf16[256,128]{1,0:T(8,128)(2,1)S(1)}, bf16[256,128]{1,0:T(8,128)(2,1)S(1)}, u32[]{:S(2)}, u32[]{:S(2)}) collective-permute-start(bf16[256,128]{1,0:T(8,128)(2,1)S(1)} %pad_maximum_fusion.4), channel_id=1, source_target_pairs={{0,4},{1,5},{2,6},{3,7},{4,0},{5,1},{6,2},{7,3},{8,12},{9,13},{10,... | collective-permute-start | bytes 196616 | tf_op jit(solution)/shard_map/ppermute | solution.py:43
  42.1 5.0 %collective-permute-start.12 = (bf16[256,128]{1,0:T(8,128)(2,1)S(1)}, bf16[256,128]{1,0:T(8,128)(2,1)S(1)}, u32[]{:S(2)}, u32[]{:S(2)}) collective-permute-start(bf16[256,128]{1,0:T(8,128)(2,1)S(1)} %pad_maximum_fusion.4), channel_id=1, source_target_pairs={{0,6},{1,7},{2,4},{3,5},{4,2},{5,3},{6,0},{7,1},{8,14},{9,15},{10,... | collective-permute-start | bytes 196616 | tf_op jit(solution)/shard_map/ppermute | solution.py:43
  47.1 11.7 %collective-permute-start.15 = (bf16[1024,128]{1,0:T(8,128)(2,1)S(1)}, bf16[1024,128]{1,0:T(8,128)(2,1)S(1)}, u32[]{:S(2)}, u32[]{:S(2)}) collective-permute-start(bf16[1024,128]{1,0:T(8,128)(2,1)S(1)} %pad_maximum_fusion.1.rest_0_), channel_id=1, source_target_pairs={{0,16},{1,17},{2,18},{3,19},{4,20},{5,21},{6,22},{7,23},{8,24},{9,... | collective-permute-start | bytes 786440 | tf_op jit(solution)/shard_map/ppermute | solution.py:43
  47.6 5.9 %collective-permute-start.13 = (bf16[3,128,128]{2,1,0:T(8,128)(2,1)S(1)}, bf16[3,128,128]{2,1,0:T(8,128)(2,1)S(1)}, u32[]{:S(2)}, u32[]{:S(2)}) collective-permute-start(bf16[3,128,128]{2,1,0:T(8,128)(2,1)S(1)} %get-tuple-element.106), channel_id=1, source_target_pairs={{0,1},{1,0},{2,3},{3,2},{4,5},{5,4},{6,7},{7,6},{8,9},{9,8},{10,11... | collective-permute-start | bytes 294920 | tf_op jit(solution)/shard_map/ppermute | solution.py:43
  50.9 4.3 %collective-permute-start.14 = (bf16[3,128,128]{2,1,0:T(8,128)(2,1)S(1)}, bf16[3,128,128]{2,1,0:T(8,128)(2,1)S(1)}, u32[]{:S(2)}, u32[]{:S(2)}) collective-permute-start(bf16[3,128,128]{2,1,0:T(8,128)(2,1)S(1)} %get-tuple-element.107), channel_id=1, source_target_pairs={{0,31},{1,2},{2,1},{3,4},{4,3},{5,6},{6,5},{7,8},{8,7},{9,10},{10,... | collective-permute-start | bytes 294920 | tf_op jit(solution)/shard_map/ppermute | solution.py:43
  56.8 3.2 %collective-permute-start.16 = (bf16[1024,128]{1,0:T(8,128)(2,1)S(1)}, bf16[1024,128]{1,0:T(8,128)(2,1)S(1)}, u32[]{:S(2)}, u32[]{:S(2)}) collective-permute-start(bf16[1024,128]{1,0:T(8,128)(2,1)S(1)} %pad_maximum_fusion.1.rest_0_), channel_id=1, source_target_pairs={{0,1},{1,0},{2,3},{3,2},{4,5},{5,4},{6,7},{7,6},{8,9},{9,8},{10,11... | collective-permute-start | bytes 786440 | tf_op jit(solution)/shard_map/ppermute | solution.py:43
  60.6 5.0 %collective-permute-start.18 = (bf16[128,128]{1,0:T(8,128)(2,1)S(1)}, bf16[128,128]{1,0:T(8,128)(2,1)S(1)}, u32[]{:S(2)}, u32[]{:S(2)}) collective-permute-start(bf16[128,128]{1,0:T(8,128)(2,1)S(1)} %shard_map.72), channel_id=1, source_target_pairs={{0,12},{1,13},{2,14},{3,15},{4,8},{5,9},{6,10},{7,11},{8,4},{9,5},... | collective-permute-start | bytes 98312 | tf_op jit(solution)/shard_map/ppermute | solution.py:43
  65.5 3.6 %collective-permute-start.19 = (bf16[256,128]{1,0:T(8,128)(2,1)S(1)}, bf16[256,128]{1,0:T(8,128)(2,1)S(1)}, u32[]{:S(2)}, u32[]{:S(2)}) collective-permute-start(bf16[256,128]{1,0:T(8,128)(2,1)S(1)} %pad_maximum_fusion.5), channel_id=1, source_target_pairs={{0,2},{1,3},{2,0},{3,1},{4,6},{5,7},{6,4},{7,5},{8,10},{9,11},{10,... | collective-permute-start | bytes 196616 | tf_op jit(solution)/shard_map/ppermute | solution.py:43
  65.6 4.1 %collective-permute-start.20 = (bf16[256,128]{1,0:T(8,128)(2,1)S(1)}, bf16[256,128]{1,0:T(8,128)(2,1)S(1)}, u32[]{:S(2)}, u32[]{:S(2)}) collective-permute-start(bf16[256,128]{1,0:T(8,128)(2,1)S(1)} %pad_maximum_fusion.5), channel_id=1, source_target_pairs={{0,4},{1,5},{2,6},{3,7},{4,0},{5,1},{6,2},{7,3},{8,12},{9,13},{10,... | collective-permute-start | bytes 196616 | tf_op jit(solution)/shard_map/ppermute | solution.py:43
  67.9 5.5 %collective-permute-start.21 = (bf16[256,128]{1,0:T(8,128)(2,1)S(1)}, bf16[256,128]{1,0:T(8,128)(2,1)S(1)}, u32[]{:S(2)}, u32[]{:S(2)}) collective-permute-start(bf16[256,128]{1,0:T(8,128)(2,1)S(1)} %pad_maximum_fusion.5), channel_id=1, source_target_pairs={{0,6},{1,7},{2,4},{3,5},{4,2},{5,3},{6,0},{7,1},{8,14},{9,15},{10,... | collective-permute-start | bytes 196616 | tf_op jit(solution)/shard_map/ppermute | solution.py:43
  73.4 10.6 %collective-permute-start.24 = (bf16[1024,128]{1,0:T(8,128)(2,1)S(1)}, bf16[1024,128]{1,0:T(8,128)(2,1)S(1)}, u32[]{:S(2)}, u32[]{:S(2)}) collective-permute-start(bf16[1024,128]{1,0:T(8,128)(2,1)S(1)} %pad_maximum_fusion.2.rest_1_), channel_id=1, source_target_pairs={{0,16},{1,17},{2,18},{3,19},{4,20},{5,21},{6,22},{7,23},{8,24},{9,... | collective-permute-start | bytes 786440 | tf_op jit(solution)/shard_map/ppermute | solution.py:43
  73.5 5.4 %collective-permute-start.22 = (bf16[3,128,128]{2,1,0:T(8,128)(2,1)S(1)}, bf16[3,128,128]{2,1,0:T(8,128)(2,1)S(1)}, u32[]{:S(2)}, u32[]{:S(2)}) collective-permute-start(bf16[3,128,128]{2,1,0:T(8,128)(2,1)S(1)} %get-tuple-element.133), channel_id=1, source_target_pairs={{0,1},{1,0},{2,3},{3,2},{4,5},{5,4},{6,7},{7,6},{8,9},{9,8},{10,11... | collective-permute-start | bytes 294920 | tf_op jit(solution)/shard_map/ppermute | solution.py:43
  76.6 4.3 %collective-permute-start.23 = (bf16[3,128,128]{2,1,0:T(8,128)(2,1)S(1)}, bf16[3,128,128]{2,1,0:T(8,128)(2,1)S(1)}, u32[]{:S(2)}, u32[]{:S(2)}) collective-permute-start(bf16[3,128,128]{2,1,0:T(8,128)(2,1)S(1)} %get-tuple-element.134), channel_id=1, source_target_pairs={{0,31},{1,2},{2,1},{3,4},{4,3},{5,6},{6,5},{7,8},{8,7},{9,10},{10,... | collective-permute-start | bytes 294920 | tf_op jit(solution)/shard_map/ppermute | solution.py:43
  82.0 3.2 %collective-permute-start.25 = (bf16[1024,128]{1,0:T(8,128)(2,1)S(1)}, bf16[1024,128]{1,0:T(8,128)(2,1)S(1)}, u32[]{:S(2)}, u32[]{:S(2)}) collective-permute-start(bf16[1024,128]{1,0:T(8,128)(2,1)S(1)} %pad_maximum_fusion.2.rest_1_), channel_id=1, source_target_pairs={{0,1},{1,0},{2,3},{3,2},{4,5},{5,4},{6,7},{7,6},{8,9},{9,8},{10,11... | collective-permute-start | bytes 786440 | tf_op jit(solution)/shard_map/ppermute | solution.py:43
  (8 other events, 51.5 us)

commit v6 on v5

--- a/solution.py
+++ b/solution.py
@@ -290,7 +290,8 @@
         return inner, outer
 
     def exchange(rims):
-        return [permute(rim, pairs) for rim, pairs in zip(rims, (ACROSS_CORE, ACROSS_EDGE))]
+        outer = permute(rims[1], ACROSS_EDGE)
+        return [permute(rims[0], ACROSS_CORE), outer]
 
     table = embeddings.reshape(blocks, BLOCK, features)
     picked, columns = call(
@@ -327,7 +328,8 @@
         halos = exchange((rim_inner, rim_outer))
         extra = ([], [], tables[:-1])[level]
         band, *base = inner_products(level, offsets, table, band_tiles, extra)
-        *halos, band = together(*halos, band)
+        outer, inner, band = together(halos[1], halos[0], band)
+        halos = [inner, outer]
         extra = [columns] if level == 1 else []
         band, *more = rim_products(level, offsets, side, band, table, halos, band_tiles, extra)
         core_in, band, *more = together(column, band, *more)

time: 88.9 us -> 88.4 us (level)
  waiting for transfers between devices: 22.2 us -> 17.7 us
  starting transfers between devices: 39.3 us -> 43.2 us
    ppermute x27, waiting for transfers between devices: 22.2 us -> 17.7 us  [permute(): return lax.ppermute(array, 'row', pairs)]
    ppermute x27, starting transfers between devices: 39.3 us -> 43.2 us  [permute(): return lax.ppermute(array, 'row', pairs)]
  transfers between devices with their start and end apart: 27 -> 27, of which waited for: 15 -> 14; matrix products, arithmetic and copies ran while one was open for 3% -> 3% of each run, Pallas kernels for 15% -> 16%
where the time goes in v6:
time: 88.4 us; the launch traced here: 88.1 us
  starting transfers between devices  43.2 us (49%)
  Pallas kernels  20 us (23%)
  waiting for transfers between devices  17.7 us (20%)
  local copies, waits for them, and re-layouts  5.47 us (6%)
  other arithmetic  1.52 us (2%)
    ppermute x27, starting transfers between devices, permute(): return lax.ppermute(array, 'row', pairs)  43.2 us
    pallas_call x13, Pallas kernels, call(): pl.pallas_call(kernel, in_specs=[smem] * len(scalars) + [vmem] * len(arra...  20 us
    ppermute x27, waiting for transfers between devices, permute(): return lax.ppermute(array, 'row', pairs)  17.7 us
    unnamed x11, local copies, waits for them, and re-layouts  4.2 us
  transfers between devices with their start and end apart: 27, of which 14 were waited for; matrix products, arithmetic and copies ran while one was open for 3% of the time, Pallas kernels for 16%

profile of v6, /device:TPU:1, one launch (start us, length us, event | category | flops | bytes accessed | tf_op | source)
XLA Modules:
  0.0 88.1 jit_solution(13250409190769093066)
XLA Ops:
  2.4 6.9 %collective-permute-start = (bf16[128,128]{1,0:T(8,128)(2,1)S(1)}, bf16[128,128]{1,0:T(8,128)(2,1)S(1)}, u32[]{:S(2)}, u32[]{:S(2)}) collective-permute-start(bf16[128,128]{1,0:T(8,128)(2,1)S(1)} %get-tuple-element.74), channel_id=1, source_target_pairs={{0,12},{1,13},{2,14},{3,15},{4,8},{5,9},{6,10},{7,11},{8,4},{9,5},... | collective-permute-start | bytes 98312 | tf_op jit(solution)/shard_map/ppermute | solution.py:43
  13.1 1.6 %collective-permute-start.3 = (bf16[256,128]{1,0:T(8,128)(2,1)S(1)}, bf16[256,128]{1,0:T(8,128)(2,1)S(1)}, u32[]{:S(2)}, u32[]{:S(2)}) collective-permute-start(bf16[256,128]{1,0:T(8,128)(2,1)S(1)} %pad_maximum_fusion.3), channel_id=1, source_target_pairs={{0,6},{1,7},{2,4},{3,5},{4,2},{5,3},{6,0},{7,1},{8,14},{9,15},{10,... | collective-permute-start | bytes 196616 | tf_op jit(solution)/shard_map/ppermute | solution.py:43
  16.6 2.1 %collective-permute-done.3 = bf16[256,128]{1,0:T(8,128)(2,1)S(1)} collective-permute-done((bf16[256,128]{1,0:T(8,128)(2,1)S(1)}, bf16[256,128]{1,0:T(8,128)(2,1)S(1)}, u32[]{:S(2)}, u32[]{:S(2)}) %collective-permute-start.3) | collective-permute-done | bytes 65568 | tf_op jit(solution)/shard_map/ppermute | solution.py:43
  20.1 3.3 %collective-permute-start.4 = (bf16[3,128,128]{2,1,0:T(8,128)(2,1)S(1)}, bf16[3,128,128]{2,1,0:T(8,128)(2,1)S(1)}, u32[]{:S(2)}, u32[]{:S(2)}) collective-permute-start(bf16[3,128,128]{2,1,0:T(8,128)(2,1)S(1)} %get-tuple-element.85), channel_id=1, source_target_pairs={{0,31},{1,2},{2,1},{3,4},{4,3},{5,6},{6,5},{7,8},{8,7},{9,10},{10,... | collective-permute-start | bytes 294920 | tf_op jit(solution)/shard_map/ppermute | solution.py:43
  23.4 2.2 %copy-done = bf16[32,4,128,128]{3,2,1,0:T(8,128)(2,1)S(1)} copy-done((bf16[32,4,128,128]{3,2,1,0:T(8,128)(2,1)S(1)}, bf16[32,4,128,128]{3,2,1,0:T(8,128)(2,1)}, u32[]{:S(2)}) %copy-start) | copy-done | bytes 4194328
  25.6 1.7 %shard_map.65.band_ref = f32[32,128,128]{2,1,0:T(8,128)S(1)} custom-call(s32[128]{0:T(128)S(1)} %reshape.14.offsets_ref, bf16[32,128,128]{2,1,0:T(8,128)(2,1)S(1)} %bitcast.7, bf16[32,4,128,128]{3,2,1,0:T(8,128)(2,1)S(1)} %copy-done), custom_call_target="tpu_custom_call" | custom-call | flops 1 | bytes 1 | tf_op jit(solution)/shard_map/pallas_call | solution.py:73
  28.4 1.8 %collective-permute-start.7 = (bf16[1024,128]{1,0:T(8,128)(2,1)S(1)}, bf16[1024,128]{1,0:T(8,128)(2,1)S(1)}, u32[]{:S(2)}, u32[]{:S(2)}) collective-permute-start(bf16[1024,128]{1,0:T(8,128)(2,1)S(1)} %pad_maximum_fusion.rest_1_), channel_id=1, source_target_pairs={{0,1},{1,0},{2,3},{3,2},{4,5},{5,4},{6,7},{7,6},{8,9},{9,8},{10,11... | collective-permute-start | bytes 786440 | tf_op jit(solution)/shard_map/ppermute | solution.py:43
  31.8 2.4 %shard_map.67 = (bf16[32,128,128]{2,1,0:T(8,128)(2,1)S(1)}, bf16[128,128]{1,0:T(8,128)(2,1)S(1)}) custom-call(s32[128]{0:T(128)S(1)} %reshape.13.place_ref, bf16[32,4,128,128]{3,2,1,0:T(8,128)(2,1)S(1)} %copy-done.2, f32[32,128,128]{2,1,0:T(8,128)S(1)} %shard_map.66.band_ref, s32[2,128,128]{2,1,0:T(8,128)S(1)} %get-tuple-element.112.rest_0_.columns_ref, ...), custom_call_target="tpu_custom_call" | custom-call | flops 1 | bytes 1 | tf_op jit(solution)/shard_map/pallas_call | solution.py:73
  34.2 2.4 %collective-permute-start.9 = (bf16[128,128]{1,0:T(8,128)(2,1)S(1)}, bf16[128,128]{1,0:T(8,128)(2,1)S(1)}, u32[]{:S(2)}, u32[]{:S(2)}) collective-permute-start(bf16[128,128]{1,0:T(8,128)(2,1)S(1)} %get-tuple-element.96), channel_id=1, source_target_pairs={{0,12},{1,13},{2,14},{3,15},{4,8},{5,9},{6,10},{7,11},{8,4},{9,5},... | collective-permute-start | bytes 98312 | tf_op jit(solution)/shard_map/ppermute | solution.py:43
  36.6 2.3 %shard_map.68.spread_ref = bf16[32,128,128]{2,1,0:T(8,128)(2,1)S(1)} custom-call(s32[128]{0:T(128)S(1)} %reshape.13.place_ref, s32[2,128,128]{2,1,0:T(8,128)S(1)} %get-tuple-element.112.rest_0_.columns_ref, bf16[32,4,128,128]{3,2,1,0:T(8,128)(2,1)S(1)} %copy-done.2), custom_call_target="tpu_custom_call" | custom-call | flops 1 | bytes 1 | tf_op jit(solution)/shard_map/pallas_call | solution.py:73
  39.2 3.1 %collective-permute-start.11 = (bf16[256,128]{1,0:T(8,128)(2,1)S(1)}, bf16[256,128]{1,0:T(8,128)(2,1)S(1)}, u32[]{:S(2)}, u32[]{:S(2)}) collective-permute-start(bf16[256,128]{1,0:T(8,128)(2,1)S(1)} %pad_maximum_fusion.4), channel_id=1, source_target_pairs={{0,4},{1,5},{2,6},{3,7},{4,0},{5,1},{6,2},{7,3},{8,12},{9,13},{10,... | collective-permute-start | bytes 196616 | tf_op jit(solution)/shard_map/ppermute | solution.py:43
  42.7 1.8 %collective-permute-done.11 = bf16[256,128]{1,0:T(8,128)(2,1)S(1)} collective-permute-done((bf16[256,128]{1,0:T(8,128)(2,1)S(1)}, bf16[256,128]{1,0:T(8,128)(2,1)S(1)}, u32[]{:S(2)}, u32[]{:S(2)}) %collective-permute-start.11) | collective-permute-done | bytes 65568 | tf_op jit(solution)/shard_map/ppermute | solution.py:43
  44.6 2.8 %collective-permute-done.12 = bf16[256,128]{1,0:T(8,128)(2,1)S(1)} collective-permute-done((bf16[256,128]{1,0:T(8,128)(2,1)S(1)}, bf16[256,128]{1,0:T(8,128)(2,1)S(1)}, u32[]{:S(2)}, u32[]{:S(2)}) %collective-permute-start.12) | collective-permute-done | bytes 65568 | tf_op jit(solution)/shard_map/ppermute | solution.py:43
  47.9 1.8 %collective-permute-start.13 = (bf16[3,128,128]{2,1,0:T(8,128)(2,1)S(1)}, bf16[3,128,128]{2,1,0:T(8,128)(2,1)S(1)}, u32[]{:S(2)}, u32[]{:S(2)}) collective-permute-start(bf16[3,128,128]{2,1,0:T(8,128)(2,1)S(1)} %get-tuple-element.106), channel_id=1, source_target_pairs={{0,31},{1,2},{2,1},{3,4},{4,3},{5,6},{6,5},{7,8},{8,7},{9,10},{10,... | collective-permute-start | bytes 294920 | tf_op jit(solution)/shard_map/ppermute | solution.py:43
  51.0 1.7 %shard_map.69.band_ref = f32[32,128,128]{2,1,0:T(8,128)S(1)} custom-call(s32[128]{0:T(128)S(1)} %reshape.14.offsets_ref, bf16[32,128,128]{2,1,0:T(8,128)(2,1)S(1)} %get-tuple-element.108.table_ref.rest_1_, bf16[32,4,128,128]{3,2,1,0:T(8,128)(2,1)S(1)} %copy-done.1), custom_call_target="tpu_custom_call" | custom-call | flops 1 | bytes 1 | tf_op jit(solution)/shard_map/pallas_call | solution.py:73
  54.4 4.6 %collective-permute-start.16 = (bf16[1024,128]{1,0:T(8,128)(2,1)S(1)}, bf16[1024,128]{1,0:T(8,128)(2,1)S(1)}, u32[]{:S(2)}, u32[]{:S(2)}) collective-permute-start(bf16[1024,128]{1,0:T(8,128)(2,1)S(1)} %pad_maximum_fusion.1.rest_0_), channel_id=1, source_target_pairs={{0,1},{1,0},{2,3},{3,2},{4,5},{5,4},{6,7},{7,6},{8,9},{9,8},{10,11... | collective-permute-start | bytes 786440 | tf_op jit(solution)/shard_map/ppermute | solution.py:43
  60.8 2.1 %shard_map.73.table_ref = bf16[32,128,128]{2,1,0:T(8,128)(2,1)S(1)} custom-call(s32[128]{0:T(128)S(1)} %reshape.13.place_ref, bf16[32,4,128,128]{3,2,1,0:T(8,128)(2,1)S(1)} %copy-done.2, f32[32,128,128]{2,1,0:T(8,128)S(1)} %get-tuple-element.120.band_ref, bf16[1024,128]{1,0:T(8,128)(2,1)S(1)} %pad_maximum_fusion.1.rest_0_, ...), custom_call_target="tpu_custom_call" | custom-call | flops 1 | bytes 1 | tf_op jit(solution)/shard_map/pallas_call | solution.py:73
  62.9 2.7 %collective-permute-done.18 = bf16[128,128]{1,0:T(8,128)(2,1)S(1)} collective-permute-done((bf16[128,128]{1,0:T(8,128)(2,1)S(1)}, bf16[128,128]{1,0:T(8,128)(2,1)S(1)}, u32[]{:S(2)}, u32[]{:S(2)}) %collective-permute-start.18) | collective-permute-done | bytes 32800 | tf_op jit(solution)/shard_map/ppermute | solution.py:43
  65.8 3.4 %collective-permute-start.21 = (bf16[256,128]{1,0:T(8,128)(2,1)S(1)}, bf16[256,128]{1,0:T(8,128)(2,1)S(1)}, u32[]{:S(2)}, u32[]{:S(2)}) collective-permute-start(bf16[256,128]{1,0:T(8,128)(2,1)S(1)} %pad_maximum_fusion.5), channel_id=1, source_target_pairs={{0,6},{1,7},{2,4},{3,5},{4,2},{5,3},{6,0},{7,1},{8,14},{9,15},{10,... | collective-permute-start | bytes 196616 | tf_op jit(solution)/shard_map/ppermute | solution.py:43
  69.8 1.9 %collective-permute-done.21 = bf16[256,128]{1,0:T(8,128)(2,1)S(1)} collective-permute-done((bf16[256,128]{1,0:T(8,128)(2,1)S(1)}, bf16[256,128]{1,0:T(8,128)(2,1)S(1)}, u32[]{:S(2)}, u32[]{:S(2)}) %collective-permute-start.21) | collective-permute-done | bytes 65568 | tf_op jit(solution)/shard_map/ppermute | solution.py:43
  72.9 4.2 %collective-permute-start.22 = (bf16[3,128,128]{2,1,0:T(8,128)(2,1)S(1)}, bf16[3,128,128]{2,1,0:T(8,128)(2,1)S(1)}, u32[]{:S(2)}, u32[]{:S(2)}) collective-permute-start(bf16[3,128,128]{2,1,0:T(8,128)(2,1)S(1)} %get-tuple-element.133), channel_id=1, source_target_pairs={{0,31},{1,2},{2,1},{3,4},{4,3},{5,6},{6,5},{7,8},{8,7},{9,10},{10,... | collective-permute-start | bytes 294920 | tf_op jit(solution)/shard_map/ppermute | solution.py:43
  77.1 2.0 %shard_map.74 = (f32[32,128,128]{2,1,0:T(8,128)S(1)}, f32[32,128,128]{2,1,0:T(8,128)S(1)}) custom-call(s32[128]{0:T(128)S(1)} %reshape.14.offsets_ref, bf16[32,128,128]{2,1,0:T(8,128)(2,1)S(1)} %shard_map.73.table_ref, bf16[32,4,128,128]{3,2,1,0:T(8,128)(2,1)S(1)} %copy-done.1, bf16[32,128,128]{2,1,0:T(8,128)(2,1)S(1)} %bitcast.9, ...), custom_call_target="tpu_custom_call" | custom-call | flops 1 | bytes 1 | tf_op jit(solution)/shard_map/pallas_call | solution.py:73
  80.6 2.8 %collective-permute-start.25 = (bf16[1024,128]{1,0:T(8,128)(2,1)S(1)}, bf16[1024,128]{1,0:T(8,128)(2,1)S(1)}, u32[]{:S(2)}, u32[]{:S(2)}) collective-permute-start(bf16[1024,128]{1,0:T(8,128)(2,1)S(1)} %pad_maximum_fusion.2.rest_1_), channel_id=1, source_target_pairs={{0,1},{1,0},{2,3},{3,2},{4,5},{5,4},{6,7},{7,6},{8,9},{9,8},{10,11... | collective-permute-start | bytes 786440 | tf_op jit(solution)/shard_map/ppermute | solution.py:43
  85.0 3.1 %shard_map.76 = bf16[32,128,128]{2,1,0:T(8,128)(2,1)} custom-call(s32[128]{0:T(128)S(1)} %reshape.13.place_ref, bf16[32,4,128,128]{3,2,1,0:T(8,128)(2,1)S(1)} %copy-done.2, f32[32,128,128]{2,1,0:T(8,128)S(1)} %shard_map.75.band_ref, f32[32,128,128]{2,1,0:T(8,128)S(1)} %get-tuple-element.141.rest_0_, bf16[1024,128]{1,0:T(8,128)(2,1)S(1)} %pad_maximum_fusion.2.rest_1_, ...), custom_call_target="tpu_custom_call" | custom-call | flops 1 | bytes 1 | tf_op jit(solution)/shard_map/pallas_call | solution.py:73
  (69 shorter events, 23.0 us)
Async XLA Ops:
  2.4 8.7 %collective-permute-start = (bf16[128,128]{1,0:T(8,128)(2,1)S(1)}, bf16[128,128]{1,0:T(8,128)(2,1)S(1)}, u32[]{:S(2)}, u32[]{:S(2)}) collective-permute-start(bf16[128,128]{1,0:T(8,128)(2,1)S(1)} %get-tuple-element.74), channel_id=1, source_target_pairs={{0,12},{1,13},{2,14},{3,15},{4,8},{5,9},{6,10},{7,11},{8,4},{9,5},... | collective-permute-start | bytes 98312 | tf_op jit(solution)/shard_map/ppermute | solution.py:43
  11.1 4.6 %collective-permute-start.1 = (bf16[256,128]{1,0:T(8,128)(2,1)S(1)}, bf16[256,128]{1,0:T(8,128)(2,1)S(1)}, u32[]{:S(2)}, u32[]{:S(2)}) collective-permute-start(bf16[256,128]{1,0:T(8,128)(2,1)S(1)} %pad_maximum_fusion.3), channel_id=1, source_target_pairs={{0,2},{1,3},{2,0},{3,1},{4,6},{5,7},{6,4},{7,5},{8,10},{9,11},{10,... | collective-permute-start | bytes 196616 | tf_op jit(solution)/shard_map/ppermute | solution.py:43
  11.9 4.7 %collective-permute-start.2 = (bf16[256,128]{1,0:T(8,128)(2,1)S(1)}, bf16[256,128]{1,0:T(8,128)(2,1)S(1)}, u32[]{:S(2)}, u32[]{:S(2)}) collective-permute-start(bf16[256,128]{1,0:T(8,128)(2,1)S(1)} %pad_maximum_fusion.3), channel_id=1, source_target_pairs={{0,4},{1,5},{2,6},{3,7},{4,0},{5,1},{6,2},{7,3},{8,12},{9,13},{10,... | collective-permute-start | bytes 196616 | tf_op jit(solution)/shard_map/ppermute | solution.py:43
  13.1 5.6 %collective-permute-start.3 = (bf16[256,128]{1,0:T(8,128)(2,1)S(1)}, bf16[256,128]{1,0:T(8,128)(2,1)S(1)}, u32[]{:S(2)}, u32[]{:S(2)}) collective-permute-start(bf16[256,128]{1,0:T(8,128)(2,1)S(1)} %pad_maximum_fusion.3), channel_id=1, source_target_pairs={{0,6},{1,7},{2,4},{3,5},{4,2},{5,3},{6,0},{7,1},{8,14},{9,15},{10,... | collective-permute-start | bytes 196616 | tf_op jit(solution)/shard_map/ppermute | solution.py:43
  18.8 11.5 %collective-permute-start.6 = (bf16[1024,128]{1,0:T(8,128)(2,1)S(1)}, bf16[1024,128]{1,0:T(8,128)(2,1)S(1)}, u32[]{:S(2)}, u32[]{:S(2)}) collective-permute-start(bf16[1024,128]{1,0:T(8,128)(2,1)S(1)} %pad_maximum_fusion.rest_1_), channel_id=1, source_target_pairs={{0,16},{1,17},{2,18},{3,19},{4,20},{5,21},{6,22},{7,23},{8,24},{9,... | collective-permute-start | bytes 786440 | tf_op jit(solution)/shard_map/ppermute | solution.py:43
  20.1 7.3 %collective-permute-start.4 = (bf16[3,128,128]{2,1,0:T(8,128)(2,1)S(1)}, bf16[3,128,128]{2,1,0:T(8,128)(2,1)S(1)}, u32[]{:S(2)}, u32[]{:S(2)}) collective-permute-start(bf16[3,128,128]{2,1,0:T(8,128)(2,1)S(1)} %get-tuple-element.85), channel_id=1, source_target_pairs={{0,31},{1,2},{2,1},{3,4},{4,3},{5,6},{6,5},{7,8},{8,7},{9,10},{10,... | collective-permute-start | bytes 294920 | tf_op jit(solution)/shard_map/ppermute | solution.py:43
  23.3 4.0 %collective-permute-start.5 = (bf16[3,128,128]{2,1,0:T(8,128)(2,1)S(1)}, bf16[3,128,128]{2,1,0:T(8,128)(2,1)S(1)}, u32[]{:S(2)}, u32[]{:S(2)}) collective-permute-start(bf16[3,128,128]{2,1,0:T(8,128)(2,1)S(1)} %get-tuple-element.86), channel_id=1, source_target_pairs={{0,1},{1,0},{2,3},{3,2},{4,5},{5,4},{6,7},{7,6},{8,9},{9,8},{10,11... | collective-permute-start | bytes 294920 | tf_op jit(solution)/shard_map/ppermute | solution.py:43
  28.4 3.0 %collective-permute-start.7 = (bf16[1024,128]{1,0:T(8,128)(2,1)S(1)}, bf16[1024,128]{1,0:T(8,128)(2,1)S(1)}, u32[]{:S(2)}, u32[]{:S(2)}) collective-permute-start(bf16[1024,128]{1,0:T(8,128)(2,1)S(1)} %pad_maximum_fusion.rest_1_), channel_id=1, source_target_pairs={{0,1},{1,0},{2,3},{3,2},{4,5},{5,4},{6,7},{7,6},{8,9},{9,8},{10,11... | collective-permute-start | bytes 786440 | tf_op jit(solution)/shard_map/ppermute | solution.py:43
  34.2 5.0 %collective-permute-start.9 = (bf16[128,128]{1,0:T(8,128)(2,1)S(1)}, bf16[128,128]{1,0:T(8,128)(2,1)S(1)}, u32[]{:S(2)}, u32[]{:S(2)}) collective-permute-start(bf16[128,128]{1,0:T(8,128)(2,1)S(1)} %get-tuple-element.96), channel_id=1, source_target_pairs={{0,12},{1,13},{2,14},{3,15},{4,8},{5,9},{6,10},{7,11},{8,4},{9,5},... | collective-permute-start | bytes 98312 | tf_op jit(solution)/shard_map/ppermute | solution.py:43
  39.1 3.6 %collective-permute-start.10 = (bf16[256,128]{1,0:T(8,128)(2,1)S(1)}, bf16[256,128]{1,0:T(8,128)(2,1)S(1)}, u32[]{:S(2)}, u32[]{:S(2)}) collective-permute-start(bf16[256,128]{1,0:T(8,128)(2,1)S(1)} %pad_maximum_fusion.4), channel_id=1, source_target_pairs={{0,2},{1,3},{2,0},{3,1},{4,6},{5,7},{6,4},{7,5},{8,10},{9,11},{10,... | collective-permute-start | bytes 196616 | tf_op jit(solution)/shard_map/ppermute | solution.py:43
  39.2 5.4 %collective-permute-start.11 = (bf16[256,128]{1,0:T(8,128)(2,1)S(1)}, bf16[256,128]{1,0:T(8,128)(2,1)S(1)}, u32[]{:S(2)}, u32[]{:S(2)}) collective-permute-start(bf16[256,128]{1,0:T(8,128)(2,1)S(1)} %pad_maximum_fusion.4), channel_id=1, source_target_pairs={{0,4},{1,5},{2,6},{3,7},{4,0},{5,1},{6,2},{7,3},{8,12},{9,13},{10,... | collective-permute-start | bytes 196616 | tf_op jit(solution)/shard_map/ppermute | solution.py:43
  42.2 5.2 %collective-permute-start.12 = (bf16[256,128]{1,0:T(8,128)(2,1)S(1)}, bf16[256,128]{1,0:T(8,128)(2,1)S(1)}, u32[]{:S(2)}, u32[]{:S(2)}) collective-permute-start(bf16[256,128]{1,0:T(8,128)(2,1)S(1)} %pad_maximum_fusion.4), channel_id=1, source_target_pairs={{0,6},{1,7},{2,4},{3,5},{4,2},{5,3},{6,0},{7,1},{8,14},{9,15},{10,... | collective-permute-start | bytes 196616 | tf_op jit(solution)/shard_map/ppermute | solution.py:43
  47.4 11.5 %collective-permute-start.15 = (bf16[1024,128]{1,0:T(8,128)(2,1)S(1)}, bf16[1024,128]{1,0:T(8,128)(2,1)S(1)}, u32[]{:S(2)}, u32[]{:S(2)}) collective-permute-start(bf16[1024,128]{1,0:T(8,128)(2,1)S(1)} %pad_maximum_fusion.1.rest_0_), channel_id=1, source_target_pairs={{0,16},{1,17},{2,18},{3,19},{4,20},{5,21},{6,22},{7,23},{8,24},{9,... | collective-permute-start | bytes 786440 | tf_op jit(solution)/shard_map/ppermute | solution.py:43
  47.9 4.9 %collective-permute-start.13 = (bf16[3,128,128]{2,1,0:T(8,128)(2,1)S(1)}, bf16[3,128,128]{2,1,0:T(8,128)(2,1)S(1)}, u32[]{:S(2)}, u32[]{:S(2)}) collective-permute-start(bf16[3,128,128]{2,1,0:T(8,128)(2,1)S(1)} %get-tuple-element.106), channel_id=1, source_target_pairs={{0,31},{1,2},{2,1},{3,4},{4,3},{5,6},{6,5},{7,8},{8,7},{9,10},{10,... | collective-permute-start | bytes 294920 | tf_op jit(solution)/shard_map/ppermute | solution.py:43
  49.6 3.1 %collective-permute-start.14 = (bf16[3,128,128]{2,1,0:T(8,128)(2,1)S(1)}, bf16[3,128,128]{2,1,0:T(8,128)(2,1)S(1)}, u32[]{:S(2)}, u32[]{:S(2)}) collective-permute-start(bf16[3,128,128]{2,1,0:T(8,128)(2,1)S(1)} %get-tuple-element.107), channel_id=1, source_target_pairs={{0,1},{1,0},{2,3},{3,2},{4,5},{5,4},{6,7},{7,6},{8,9},{9,8},{10,11... | collective-permute-start | bytes 294920 | tf_op jit(solution)/shard_map/ppermute | solution.py:43
  54.4 5.7 %collective-permute-start.16 = (bf16[1024,128]{1,0:T(8,128)(2,1)S(1)}, bf16[1024,128]{1,0:T(8,128)(2,1)S(1)}, u32[]{:S(2)}, u32[]{:S(2)}) collective-permute-start(bf16[1024,128]{1,0:T(8,128)(2,1)S(1)} %pad_maximum_fusion.1.rest_0_), channel_id=1, source_target_pairs={{0,1},{1,0},{2,3},{3,2},{4,5},{5,4},{6,7},{7,6},{8,9},{9,8},{10,11... | collective-permute-start | bytes 786440 | tf_op jit(solution)/shard_map/ppermute | solution.py:43
  60.7 5.0 %collective-permute-start.18 = (bf16[128,128]{1,0:T(8,128)(2,1)S(1)}, bf16[128,128]{1,0:T(8,128)(2,1)S(1)}, u32[]{:S(2)}, u32[]{:S(2)}) collective-permute-start(bf16[128,128]{1,0:T(8,128)(2,1)S(1)} %shard_map.72), channel_id=1, source_target_pairs={{0,12},{1,13},{2,14},{3,15},{4,8},{5,9},{6,10},{7,11},{8,4},{9,5},... | collective-permute-start | bytes 98312 | tf_op jit(solution)/shard_map/ppermute | solution.py:43
  65.7 3.6 %collective-permute-start.19 = (bf16[256,128]{1,0:T(8,128)(2,1)S(1)}, bf16[256,128]{1,0:T(8,128)(2,1)S(1)}, u32[]{:S(2)}, u32[]{:S(2)}) collective-permute-start(bf16[256,128]{1,0:T(8,128)(2,1)S(1)} %pad_maximum_fusion.5), channel_id=1, source_target_pairs={{0,2},{1,3},{2,0},{3,1},{4,6},{5,7},{6,4},{7,5},{8,10},{9,11},{10,... | collective-permute-start | bytes 196616 | tf_op jit(solution)/shard_map/ppermute | solution.py:43
  65.7 4.1 %collective-permute-start.20 = (bf16[256,128]{1,0:T(8,128)(2,1)S(1)}, bf16[256,128]{1,0:T(8,128)(2,1)S(1)}, u32[]{:S(2)}, u32[]{:S(2)}) collective-permute-start(bf16[256,128]{1,0:T(8,128)(2,1)S(1)} %pad_maximum_fusion.5), channel_id=1, source_target_pairs={{0,4},{1,5},{2,6},{3,7},{4,0},{5,1},{6,2},{7,3},{8,12},{9,13},{10,... | collective-permute-start | bytes 196616 | tf_op jit(solution)/shard_map/ppermute | solution.py:43
  65.8 5.9 %collective-permute-start.21 = (bf16[256,128]{1,0:T(8,128)(2,1)S(1)}, bf16[256,128]{1,0:T(8,128)(2,1)S(1)}, u32[]{:S(2)}, u32[]{:S(2)}) collective-permute-start(bf16[256,128]{1,0:T(8,128)(2,1)S(1)} %pad_maximum_fusion.5), channel_id=1, source_target_pairs={{0,6},{1,7},{2,4},{3,5},{4,2},{5,3},{6,0},{7,1},{8,14},{9,15},{10,... | collective-permute-start | bytes 196616 | tf_op jit(solution)/shard_map/ppermute | solution.py:43
  71.7 11.7 %collective-permute-start.24 = (bf16[1024,128]{1,0:T(8,128)(2,1)S(1)}, bf16[1024,128]{1,0:T(8,128)(2,1)S(1)}, u32[]{:S(2)}, u32[]{:S(2)}) collective-permute-start(bf16[1024,128]{1,0:T(8,128)(2,1)S(1)} %pad_maximum_fusion.2.rest_1_), channel_id=1, source_target_pairs={{0,16},{1,17},{2,18},{3,19},{4,20},{5,21},{6,22},{7,23},{8,24},{9,... | collective-permute-start | bytes 786440 | tf_op jit(solution)/shard_map/ppermute | solution.py:43
  72.9 6.8 %collective-permute-start.22 = (bf16[3,128,128]{2,1,0:T(8,128)(2,1)S(1)}, bf16[3,128,128]{2,1,0:T(8,128)(2,1)S(1)}, u32[]{:S(2)}, u32[]{:S(2)}) collective-permute-start(bf16[3,128,128]{2,1,0:T(8,128)(2,1)S(1)} %get-tuple-element.133), channel_id=1, source_target_pairs={{0,31},{1,2},{2,1},{3,4},{4,3},{5,6},{6,5},{7,8},{8,7},{9,10},{10,... | collective-permute-start | bytes 294920 | tf_op jit(solution)/shard_map/ppermute | solution.py:43
  77.0 2.6 %collective-permute-start.23 = (bf16[3,128,128]{2,1,0:T(8,128)(2,1)S(1)}, bf16[3,128,128]{2,1,0:T(8,128)(2,1)S(1)}, u32[]{:S(2)}, u32[]{:S(2)}) collective-permute-start(bf16[3,128,128]{2,1,0:T(8,128)(2,1)S(1)} %get-tuple-element.134), channel_id=1, source_target_pairs={{0,1},{1,0},{2,3},{3,2},{4,5},{5,4},{6,7},{7,6},{8,9},{9,8},{10,11... | collective-permute-start | bytes 294920 | tf_op jit(solution)/shard_map/ppermute | solution.py:43
  80.6 3.9 %collective-permute-start.25 = (bf16[1024,128]{1,0:T(8,128)(2,1)S(1)}, bf16[1024,128]{1,0:T(8,128)(2,1)S(1)}, u32[]{:S(2)}, u32[]{:S(2)}) collective-permute-start(bf16[1024,128]{1,0:T(8,128)(2,1)S(1)} %pad_maximum_fusion.2.rest_1_), channel_id=1, source_target_pairs={{0,1},{1,0},{2,3},{3,2},{4,5},{5,4},{6,7},{7,6},{8,9},{9,8},{10,11... | collective-permute-start | bytes 786440 | tf_op jit(solution)/shard_map/ppermute | solution.py:43
  (8 other events, 50.8 us)

commit v7 on v6

--- a/solution.py
+++ b/solution.py
@@ -10,7 +10,7 @@
 BAND = 3
 LAYERS = 3
 BLOCK = 128
-STEP = 16
+STEP = 32
 CHUNK = 8
 DEVICES = 32
 

time: 88.4 us -> 87.9 us (level)
  transfers between devices with their start and end apart: 27 -> 27, of which waited for: 14 -> 14; matrix products, arithmetic and copies ran while one was open for 3% -> 3% of each run, Pallas kernels for 16% -> 15%
where the time goes in v7:
time: 87.9 us; the launch traced here: 87.7 us
  starting transfers between devices  43.2 us (49%)
  Pallas kernels  19.3 us (22%)
  waiting for transfers between devices  18 us (20%)
  local copies, waits for them, and re-layouts  5.47 us (6%)
  other arithmetic  1.52 us (2%)
    ppermute x27, starting transfers between devices, permute(): return lax.ppermute(array, 'row', pairs)  43.2 us
    pallas_call x13, Pallas kernels, call(): pl.pallas_call(kernel, in_specs=[smem] * len(scalars) + [vmem] * len(arra...  19.3 us
    ppermute x27, waiting for transfers between devices, permute(): return lax.ppermute(array, 'row', pairs)  18 us
    unnamed x11, local copies, waits for them, and re-layouts  4.2 us
  transfers between devices with their start and end apart: 27, of which 14 were waited for; matrix products, arithmetic and copies ran while one was open for 3% of the time, Pallas kernels for 15%

profile of v7, /device:TPU:1, one launch (start us, length us, event | category | flops | bytes accessed | tf_op | source)
XLA Modules:
  0.0 87.7 jit_solution(10689206084643182724)
XLA Ops:
  2.4 6.9 %collective-permute-start = (bf16[128,128]{1,0:T(8,128)(2,1)S(1)}, bf16[128,128]{1,0:T(8,128)(2,1)S(1)}, u32[]{:S(2)}, u32[]{:S(2)}) collective-permute-start(bf16[128,128]{1,0:T(8,128)(2,1)S(1)} %get-tuple-element.74), channel_id=1, source_target_pairs={{0,12},{1,13},{2,14},{3,15},{4,8},{5,9},{6,10},{7,11},{8,4},{9,5},... | collective-permute-start | bytes 98312 | tf_op jit(solution)/shard_map/ppermute | solution.py:43
  13.1 1.6 %collective-permute-start.3 = (bf16[256,128]{1,0:T(8,128)(2,1)S(1)}, bf16[256,128]{1,0:T(8,128)(2,1)S(1)}, u32[]{:S(2)}, u32[]{:S(2)}) collective-permute-start(bf16[256,128]{1,0:T(8,128)(2,1)S(1)} %pad_maximum_fusion.3), channel_id=1, source_target_pairs={{0,6},{1,7},{2,4},{3,5},{4,2},{5,3},{6,0},{7,1},{8,14},{9,15},{10,... | collective-permute-start | bytes 196616 | tf_op jit(solution)/shard_map/ppermute | solution.py:43
  16.6 2.1 %collective-permute-done.3 = bf16[256,128]{1,0:T(8,128)(2,1)S(1)} collective-permute-done((bf16[256,128]{1,0:T(8,128)(2,1)S(1)}, bf16[256,128]{1,0:T(8,128)(2,1)S(1)}, u32[]{:S(2)}, u32[]{:S(2)}) %collective-permute-start.3) | collective-permute-done | bytes 65568 | tf_op jit(solution)/shard_map/ppermute | solution.py:43
  20.1 3.3 %collective-permute-start.4 = (bf16[3,128,128]{2,1,0:T(8,128)(2,1)S(1)}, bf16[3,128,128]{2,1,0:T(8,128)(2,1)S(1)}, u32[]{:S(2)}, u32[]{:S(2)}) collective-permute-start(bf16[3,128,128]{2,1,0:T(8,128)(2,1)S(1)} %get-tuple-element.85), channel_id=1, source_target_pairs={{0,31},{1,2},{2,1},{3,4},{4,3},{5,6},{6,5},{7,8},{8,7},{9,10},{10,... | collective-permute-start | bytes 294920 | tf_op jit(solution)/shard_map/ppermute | solution.py:43
  23.4 2.2 %copy-done = bf16[32,4,128,128]{3,2,1,0:T(8,128)(2,1)S(1)} copy-done((bf16[32,4,128,128]{3,2,1,0:T(8,128)(2,1)S(1)}, bf16[32,4,128,128]{3,2,1,0:T(8,128)(2,1)}, u32[]{:S(2)}) %copy-start) | copy-done | bytes 4194328
  25.6 1.7 %shard_map.65.band_ref = f32[32,128,128]{2,1,0:T(8,128)S(1)} custom-call(s32[128]{0:T(128)S(1)} %reshape.14.offsets_ref, bf16[32,128,128]{2,1,0:T(8,128)(2,1)S(1)} %bitcast.7, bf16[32,4,128,128]{3,2,1,0:T(8,128)(2,1)S(1)} %copy-done), custom_call_target="tpu_custom_call" | custom-call | flops 1 | bytes 1 | tf_op jit(solution)/shard_map/pallas_call | solution.py:73
  28.4 1.8 %collective-permute-start.7 = (bf16[1024,128]{1,0:T(8,128)(2,1)S(1)}, bf16[1024,128]{1,0:T(8,128)(2,1)S(1)}, u32[]{:S(2)}, u32[]{:S(2)}) collective-permute-start(bf16[1024,128]{1,0:T(8,128)(2,1)S(1)} %pad_maximum_fusion.rest_1_), channel_id=1, source_target_pairs={{0,1},{1,0},{2,3},{3,2},{4,5},{5,4},{6,7},{7,6},{8,9},{9,8},{10,11... | collective-permute-start | bytes 786440 | tf_op jit(solution)/shard_map/ppermute | solution.py:43
  31.8 2.2 %shard_map.67 = (bf16[32,128,128]{2,1,0:T(8,128)(2,1)S(1)}, bf16[128,128]{1,0:T(8,128)(2,1)S(1)}) custom-call(s32[128]{0:T(128)S(1)} %reshape.13.place_ref, bf16[32,4,128,128]{3,2,1,0:T(8,128)(2,1)S(1)} %copy-done.2, f32[32,128,128]{2,1,0:T(8,128)S(1)} %shard_map.66.band_ref, s32[2,128,128]{2,1,0:T(8,128)S(1)} %get-tuple-element.112.rest_0_.columns_ref, ...), custom_call_target="tpu_custom_call" | custom-call | flops 1 | bytes 1 | tf_op jit(solution)/shard_map/pallas_call | solution.py:73
  34.0 2.4 %collective-permute-start.9 = (bf16[128,128]{1,0:T(8,128)(2,1)S(1)}, bf16[128,128]{1,0:T(8,128)(2,1)S(1)}, u32[]{:S(2)}, u32[]{:S(2)}) collective-permute-start(bf16[128,128]{1,0:T(8,128)(2,1)S(1)} %get-tuple-element.96), channel_id=1, source_target_pairs={{0,12},{1,13},{2,14},{3,15},{4,8},{5,9},{6,10},{7,11},{8,4},{9,5},... | collective-permute-start | bytes 98312 | tf_op jit(solution)/shard_map/ppermute | solution.py:43
  36.4 2.2 %shard_map.68.spread_ref = bf16[32,128,128]{2,1,0:T(8,128)(2,1)S(1)} custom-call(s32[128]{0:T(128)S(1)} %reshape.13.place_ref, s32[2,128,128]{2,1,0:T(8,128)S(1)} %get-tuple-element.112.rest_0_.columns_ref, bf16[32,4,128,128]{3,2,1,0:T(8,128)(2,1)S(1)} %copy-done.2), custom_call_target="tpu_custom_call" | custom-call | flops 1 | bytes 1 | tf_op jit(solution)/shard_map/pallas_call | solution.py:73
  39.0 3.1 %collective-permute-start.11 = (bf16[256,128]{1,0:T(8,128)(2,1)S(1)}, bf16[256,128]{1,0:T(8,128)(2,1)S(1)}, u32[]{:S(2)}, u32[]{:S(2)}) collective-permute-start(bf16[256,128]{1,0:T(8,128)(2,1)S(1)} %pad_maximum_fusion.4), channel_id=1, source_target_pairs={{0,4},{1,5},{2,6},{3,7},{4,0},{5,1},{6,2},{7,3},{8,12},{9,13},{10,... | collective-permute-start | bytes 196616 | tf_op jit(solution)/shard_map/ppermute | solution.py:43
  42.6 1.8 %collective-permute-done.11 = bf16[256,128]{1,0:T(8,128)(2,1)S(1)} collective-permute-done((bf16[256,128]{1,0:T(8,128)(2,1)S(1)}, bf16[256,128]{1,0:T(8,128)(2,1)S(1)}, u32[]{:S(2)}, u32[]{:S(2)}) %collective-permute-start.11) | collective-permute-done | bytes 65568 | tf_op jit(solution)/shard_map/ppermute | solution.py:43
  44.4 2.8 %collective-permute-done.12 = bf16[256,128]{1,0:T(8,128)(2,1)S(1)} collective-permute-done((bf16[256,128]{1,0:T(8,128)(2,1)S(1)}, bf16[256,128]{1,0:T(8,128)(2,1)S(1)}, u32[]{:S(2)}, u32[]{:S(2)}) %collective-permute-start.12) | collective-permute-done | bytes 65568 | tf_op jit(solution)/shard_map/ppermute | solution.py:43
  47.7 1.8 %collective-permute-start.13 = (bf16[3,128,128]{2,1,0:T(8,128)(2,1)S(1)}, bf16[3,128,128]{2,1,0:T(8,128)(2,1)S(1)}, u32[]{:S(2)}, u32[]{:S(2)}) collective-permute-start(bf16[3,128,128]{2,1,0:T(8,128)(2,1)S(1)} %get-tuple-element.106), channel_id=1, source_target_pairs={{0,31},{1,2},{2,1},{3,4},{4,3},{5,6},{6,5},{7,8},{8,7},{9,10},{10,... | collective-permute-start | bytes 294920 | tf_op jit(solution)/shard_map/ppermute | solution.py:43
  50.8 1.7 %shard_map.69.band_ref = f32[32,128,128]{2,1,0:T(8,128)S(1)} custom-call(s32[128]{0:T(128)S(1)} %reshape.14.offsets_ref, bf16[32,128,128]{2,1,0:T(8,128)(2,1)S(1)} %get-tuple-element.108.table_ref.rest_1_, bf16[32,4,128,128]{3,2,1,0:T(8,128)(2,1)S(1)} %copy-done.1), custom_call_target="tpu_custom_call" | custom-call | flops 1 | bytes 1 | tf_op jit(solution)/shard_map/pallas_call | solution.py:73
  54.0 4.6 %collective-permute-start.16 = (bf16[1024,128]{1,0:T(8,128)(2,1)S(1)}, bf16[1024,128]{1,0:T(8,128)(2,1)S(1)}, u32[]{:S(2)}, u32[]{:S(2)}) collective-permute-start(bf16[1024,128]{1,0:T(8,128)(2,1)S(1)} %pad_maximum_fusion.1.rest_0_), channel_id=1, source_target_pairs={{0,1},{1,0},{2,3},{3,2},{4,5},{5,4},{6,7},{7,6},{8,9},{9,8},{10,11... | collective-permute-start | bytes 786440 | tf_op jit(solution)/shard_map/ppermute | solution.py:43
  60.4 2.0 %shard_map.73.table_ref = bf16[32,128,128]{2,1,0:T(8,128)(2,1)S(1)} custom-call(s32[128]{0:T(128)S(1)} %reshape.13.place_ref, bf16[32,4,128,128]{3,2,1,0:T(8,128)(2,1)S(1)} %copy-done.2, f32[32,128,128]{2,1,0:T(8,128)S(1)} %get-tuple-element.120.band_ref, bf16[1024,128]{1,0:T(8,128)(2,1)S(1)} %pad_maximum_fusion.1.rest_0_, ...), custom_call_target="tpu_custom_call" | custom-call | flops 1 | bytes 1 | tf_op jit(solution)/shard_map/pallas_call | solution.py:73
  62.4 2.9 %collective-permute-done.18 = bf16[128,128]{1,0:T(8,128)(2,1)S(1)} collective-permute-done((bf16[128,128]{1,0:T(8,128)(2,1)S(1)}, bf16[128,128]{1,0:T(8,128)(2,1)S(1)}, u32[]{:S(2)}, u32[]{:S(2)}) %collective-permute-start.18) | collective-permute-done | bytes 32800 | tf_op jit(solution)/shard_map/ppermute | solution.py:43
  65.4 3.4 %collective-permute-start.21 = (bf16[256,128]{1,0:T(8,128)(2,1)S(1)}, bf16[256,128]{1,0:T(8,128)(2,1)S(1)}, u32[]{:S(2)}, u32[]{:S(2)}) collective-permute-start(bf16[256,128]{1,0:T(8,128)(2,1)S(1)} %pad_maximum_fusion.5), channel_id=1, source_target_pairs={{0,6},{1,7},{2,4},{3,5},{4,2},{5,3},{6,0},{7,1},{8,14},{9,15},{10,... | collective-permute-start | bytes 196616 | tf_op jit(solution)/shard_map/ppermute | solution.py:43
  69.4 1.9 %collective-permute-done.21 = bf16[256,128]{1,0:T(8,128)(2,1)S(1)} collective-permute-done((bf16[256,128]{1,0:T(8,128)(2,1)S(1)}, bf16[256,128]{1,0:T(8,128)(2,1)S(1)}, u32[]{:S(2)}, u32[]{:S(2)}) %collective-permute-start.21) | collective-permute-done | bytes 65568 | tf_op jit(solution)/shard_map/ppermute | solution.py:43
  72.5 4.2 %collective-permute-start.22 = (bf16[3,128,128]{2,1,0:T(8,128)(2,1)S(1)}, bf16[3,128,128]{2,1,0:T(8,128)(2,1)S(1)}, u32[]{:S(2)}, u32[]{:S(2)}) collective-permute-start(bf16[3,128,128]{2,1,0:T(8,128)(2,1)S(1)} %get-tuple-element.133), channel_id=1, source_target_pairs={{0,31},{1,2},{2,1},{3,4},{4,3},{5,6},{6,5},{7,8},{8,7},{9,10},{10,... | collective-permute-start | bytes 294920 | tf_op jit(solution)/shard_map/ppermute | solution.py:43
  76.6 2.0 %shard_map.74 = (f32[32,128,128]{2,1,0:T(8,128)S(1)}, f32[32,128,128]{2,1,0:T(8,128)S(1)}) custom-call(s32[128]{0:T(128)S(1)} %reshape.14.offsets_ref, bf16[32,128,128]{2,1,0:T(8,128)(2,1)S(1)} %shard_map.73.table_ref, bf16[32,4,128,128]{3,2,1,0:T(8,128)(2,1)S(1)} %copy-done.1, bf16[32,128,128]{2,1,0:T(8,128)(2,1)S(1)} %bitcast.9, ...), custom_call_target="tpu_custom_call" | custom-call | flops 1 | bytes 1 | tf_op jit(solution)/shard_map/pallas_call | solution.py:73
  80.2 2.8 %collective-permute-start.25 = (bf16[1024,128]{1,0:T(8,128)(2,1)S(1)}, bf16[1024,128]{1,0:T(8,128)(2,1)S(1)}, u32[]{:S(2)}, u32[]{:S(2)}) collective-permute-start(bf16[1024,128]{1,0:T(8,128)(2,1)S(1)} %pad_maximum_fusion.2.rest_1_), channel_id=1, source_target_pairs={{0,1},{1,0},{2,3},{3,2},{4,5},{5,4},{6,7},{7,6},{8,9},{9,8},{10,11... | collective-permute-start | bytes 786440 | tf_op jit(solution)/shard_map/ppermute | solution.py:43
  84.6 3.1 %shard_map.76 = bf16[32,128,128]{2,1,0:T(8,128)(2,1)} custom-call(s32[128]{0:T(128)S(1)} %reshape.13.place_ref, bf16[32,4,128,128]{3,2,1,0:T(8,128)(2,1)S(1)} %copy-done.2, f32[32,128,128]{2,1,0:T(8,128)S(1)} %shard_map.75.band_ref, f32[32,128,128]{2,1,0:T(8,128)S(1)} %get-tuple-element.141.rest_0_, bf16[1024,128]{1,0:T(8,128)(2,1)S(1)} %pad_maximum_fusion.2.rest_1_, ...), custom_call_target="tpu_custom_call" | custom-call | flops 1 | bytes 1 | tf_op jit(solution)/shard_map/pallas_call | solution.py:73
  (69 shorter events, 22.9 us)
Async XLA Ops:
  2.4 8.7 %collective-permute-start = (bf16[128,128]{1,0:T(8,128)(2,1)S(1)}, bf16[128,128]{1,0:T(8,128)(2,1)S(1)}, u32[]{:S(2)}, u32[]{:S(2)}) collective-permute-start(bf16[128,128]{1,0:T(8,128)(2,1)S(1)} %get-tuple-element.74), channel_id=1, source_target_pairs={{0,12},{1,13},{2,14},{3,15},{4,8},{5,9},{6,10},{7,11},{8,4},{9,5},... | collective-permute-start | bytes 98312 | tf_op jit(solution)/shard_map/ppermute | solution.py:43
  11.1 4.6 %collective-permute-start.1 = (bf16[256,128]{1,0:T(8,128)(2,1)S(1)}, bf16[256,128]{1,0:T(8,128)(2,1)S(1)}, u32[]{:S(2)}, u32[]{:S(2)}) collective-permute-start(bf16[256,128]{1,0:T(8,128)(2,1)S(1)} %pad_maximum_fusion.3), channel_id=1, source_target_pairs={{0,2},{1,3},{2,0},{3,1},{4,6},{5,7},{6,4},{7,5},{8,10},{9,11},{10,... | collective-permute-start | bytes 196616 | tf_op jit(solution)/shard_map/ppermute | solution.py:43
  11.9 4.7 %collective-permute-start.2 = (bf16[256,128]{1,0:T(8,128)(2,1)S(1)}, bf16[256,128]{1,0:T(8,128)(2,1)S(1)}, u32[]{:S(2)}, u32[]{:S(2)}) collective-permute-start(bf16[256,128]{1,0:T(8,128)(2,1)S(1)} %pad_maximum_fusion.3), channel_id=1, source_target_pairs={{0,4},{1,5},{2,6},{3,7},{4,0},{5,1},{6,2},{7,3},{8,12},{9,13},{10,... | collective-permute-start | bytes 196616 | tf_op jit(solution)/shard_map/ppermute | solution.py:43
  13.1 5.6 %collective-permute-start.3 = (bf16[256,128]{1,0:T(8,128)(2,1)S(1)}, bf16[256,128]{1,0:T(8,128)(2,1)S(1)}, u32[]{:S(2)}, u32[]{:S(2)}) collective-permute-start(bf16[256,128]{1,0:T(8,128)(2,1)S(1)} %pad_maximum_fusion.3), channel_id=1, source_target_pairs={{0,6},{1,7},{2,4},{3,5},{4,2},{5,3},{6,0},{7,1},{8,14},{9,15},{10,... | collective-permute-start | bytes 196616 | tf_op jit(solution)/shard_map/ppermute | solution.py:43
  18.8 11.5 %collective-permute-start.6 = (bf16[1024,128]{1,0:T(8,128)(2,1)S(1)}, bf16[1024,128]{1,0:T(8,128)(2,1)S(1)}, u32[]{:S(2)}, u32[]{:S(2)}) collective-permute-start(bf16[1024,128]{1,0:T(8,128)(2,1)S(1)} %pad_maximum_fusion.rest_1_), channel_id=1, source_target_pairs={{0,16},{1,17},{2,18},{3,19},{4,20},{5,21},{6,22},{7,23},{8,24},{9,... | collective-permute-start | bytes 786440 | tf_op jit(solution)/shard_map/ppermute | solution.py:43
  20.1 7.3 %collective-permute-start.4 = (bf16[3,128,128]{2,1,0:T(8,128)(2,1)S(1)}, bf16[3,128,128]{2,1,0:T(8,128)(2,1)S(1)}, u32[]{:S(2)}, u32[]{:S(2)}) collective-permute-start(bf16[3,128,128]{2,1,0:T(8,128)(2,1)S(1)} %get-tuple-element.85), channel_id=1, source_target_pairs={{0,31},{1,2},{2,1},{3,4},{4,3},{5,6},{6,5},{7,8},{8,7},{9,10},{10,... | collective-permute-start | bytes 294920 | tf_op jit(solution)/shard_map/ppermute | solution.py:43
  23.3 4.0 %collective-permute-start.5 = (bf16[3,128,128]{2,1,0:T(8,128)(2,1)S(1)}, bf16[3,128,128]{2,1,0:T(8,128)(2,1)S(1)}, u32[]{:S(2)}, u32[]{:S(2)}) collective-permute-start(bf16[3,128,128]{2,1,0:T(8,128)(2,1)S(1)} %get-tuple-element.86), channel_id=1, source_target_pairs={{0,1},{1,0},{2,3},{3,2},{4,5},{5,4},{6,7},{7,6},{8,9},{9,8},{10,11... | collective-permute-start | bytes 294920 | tf_op jit(solution)/shard_map/ppermute | solution.py:43
  28.4 3.0 %collective-permute-start.7 = (bf16[1024,128]{1,0:T(8,128)(2,1)S(1)}, bf16[1024,128]{1,0:T(8,128)(2,1)S(1)}, u32[]{:S(2)}, u32[]{:S(2)}) collective-permute-start(bf16[1024,128]{1,0:T(8,128)(2,1)S(1)} %pad_maximum_fusion.rest_1_), channel_id=1, source_target_pairs={{0,1},{1,0},{2,3},{3,2},{4,5},{5,4},{6,7},{7,6},{8,9},{9,8},{10,11... | collective-permute-start | bytes 786440 | tf_op jit(solution)/shard_map/ppermute | solution.py:43
  34.0 5.0 %collective-permute-start.9 = (bf16[128,128]{1,0:T(8,128)(2,1)S(1)}, bf16[128,128]{1,0:T(8,128)(2,1)S(1)}, u32[]{:S(2)}, u32[]{:S(2)}) collective-permute-start(bf16[128,128]{1,0:T(8,128)(2,1)S(1)} %get-tuple-element.96), channel_id=1, source_target_pairs={{0,12},{1,13},{2,14},{3,15},{4,8},{5,9},{6,10},{7,11},{8,4},{9,5},... | collective-permute-start | bytes 98312 | tf_op jit(solution)/shard_map/ppermute | solution.py:43
  39.0 3.6 %collective-permute-start.10 = (bf16[256,128]{1,0:T(8,128)(2,1)S(1)}, bf16[256,128]{1,0:T(8,128)(2,1)S(1)}, u32[]{:S(2)}, u32[]{:S(2)}) collective-permute-start(bf16[256,128]{1,0:T(8,128)(2,1)S(1)} %pad_maximum_fusion.4), channel_id=1, source_target_pairs={{0,2},{1,3},{2,0},{3,1},{4,6},{5,7},{6,4},{7,5},{8,10},{9,11},{10,... | collective-permute-start | bytes 196616 | tf_op jit(solution)/shard_map/ppermute | solution.py:43
  39.0 5.4 %collective-permute-start.11 = (bf16[256,128]{1,0:T(8,128)(2,1)S(1)}, bf16[256,128]{1,0:T(8,128)(2,1)S(1)}, u32[]{:S(2)}, u32[]{:S(2)}) collective-permute-start(bf16[256,128]{1,0:T(8,128)(2,1)S(1)} %pad_maximum_fusion.4), channel_id=1, source_target_pairs={{0,4},{1,5},{2,6},{3,7},{4,0},{5,1},{6,2},{7,3},{8,12},{9,13},{10,... | collective-permute-start | bytes 196616 | tf_op jit(solution)/shard_map/ppermute | solution.py:43
  42.0 5.2 %collective-permute-start.12 = (bf16[256,128]{1,0:T(8,128)(2,1)S(1)}, bf16[256,128]{1,0:T(8,128)(2,1)S(1)}, u32[]{:S(2)}, u32[]{:S(2)}) collective-permute-start(bf16[256,128]{1,0:T(8,128)(2,1)S(1)} %pad_maximum_fusion.4), channel_id=1, source_target_pairs={{0,6},{1,7},{2,4},{3,5},{4,2},{5,3},{6,0},{7,1},{8,14},{9,15},{10,... | collective-permute-start | bytes 196616 | tf_op jit(solution)/shard_map/ppermute | solution.py:43
  47.3 11.3 %collective-permute-start.15 = (bf16[1024,128]{1,0:T(8,128)(2,1)S(1)}, bf16[1024,128]{1,0:T(8,128)(2,1)S(1)}, u32[]{:S(2)}, u32[]{:S(2)}) collective-permute-start(bf16[1024,128]{1,0:T(8,128)(2,1)S(1)} %pad_maximum_fusion.1.rest_0_), channel_id=1, source_target_pairs={{0,16},{1,17},{2,18},{3,19},{4,20},{5,21},{6,22},{7,23},{8,24},{9,... | collective-permute-start | bytes 786440 | tf_op jit(solution)/shard_map/ppermute | solution.py:43
  47.7 4.9 %collective-permute-start.13 = (bf16[3,128,128]{2,1,0:T(8,128)(2,1)S(1)}, bf16[3,128,128]{2,1,0:T(8,128)(2,1)S(1)}, u32[]{:S(2)}, u32[]{:S(2)}) collective-permute-start(bf16[3,128,128]{2,1,0:T(8,128)(2,1)S(1)} %get-tuple-element.106), channel_id=1, source_target_pairs={{0,31},{1,2},{2,1},{3,4},{4,3},{5,6},{6,5},{7,8},{8,7},{9,10},{10,... | collective-permute-start | bytes 294920 | tf_op jit(solution)/shard_map/ppermute | solution.py:43
  49.5 3.1 %collective-permute-start.14 = (bf16[3,128,128]{2,1,0:T(8,128)(2,1)S(1)}, bf16[3,128,128]{2,1,0:T(8,128)(2,1)S(1)}, u32[]{:S(2)}, u32[]{:S(2)}) collective-permute-start(bf16[3,128,128]{2,1,0:T(8,128)(2,1)S(1)} %get-tuple-element.107), channel_id=1, source_target_pairs={{0,1},{1,0},{2,3},{3,2},{4,5},{5,4},{6,7},{7,6},{8,9},{9,8},{10,11... | collective-permute-start | bytes 294920 | tf_op jit(solution)/shard_map/ppermute | solution.py:43
  54.0 5.7 %collective-permute-start.16 = (bf16[1024,128]{1,0:T(8,128)(2,1)S(1)}, bf16[1024,128]{1,0:T(8,128)(2,1)S(1)}, u32[]{:S(2)}, u32[]{:S(2)}) collective-permute-start(bf16[1024,128]{1,0:T(8,128)(2,1)S(1)} %pad_maximum_fusion.1.rest_0_), channel_id=1, source_target_pairs={{0,1},{1,0},{2,3},{3,2},{4,5},{5,4},{6,7},{7,6},{8,9},{9,8},{10,11... | collective-permute-start | bytes 786440 | tf_op jit(solution)/shard_map/ppermute | solution.py:43
  60.3 5.0 %collective-permute-start.18 = (bf16[128,128]{1,0:T(8,128)(2,1)S(1)}, bf16[128,128]{1,0:T(8,128)(2,1)S(1)}, u32[]{:S(2)}, u32[]{:S(2)}) collective-permute-start(bf16[128,128]{1,0:T(8,128)(2,1)S(1)} %shard_map.72), channel_id=1, source_target_pairs={{0,12},{1,13},{2,14},{3,15},{4,8},{5,9},{6,10},{7,11},{8,4},{9,5},... | collective-permute-start | bytes 98312 | tf_op jit(solution)/shard_map/ppermute | solution.py:43
  65.3 3.6 %collective-permute-start.19 = (bf16[256,128]{1,0:T(8,128)(2,1)S(1)}, bf16[256,128]{1,0:T(8,128)(2,1)S(1)}, u32[]{:S(2)}, u32[]{:S(2)}) collective-permute-start(bf16[256,128]{1,0:T(8,128)(2,1)S(1)} %pad_maximum_fusion.5), channel_id=1, source_target_pairs={{0,2},{1,3},{2,0},{3,1},{4,6},{5,7},{6,4},{7,5},{8,10},{9,11},{10,... | collective-permute-start | bytes 196616 | tf_op jit(solution)/shard_map/ppermute | solution.py:43
  65.3 4.1 %collective-permute-start.20 = (bf16[256,128]{1,0:T(8,128)(2,1)S(1)}, bf16[256,128]{1,0:T(8,128)(2,1)S(1)}, u32[]{:S(2)}, u32[]{:S(2)}) collective-permute-start(bf16[256,128]{1,0:T(8,128)(2,1)S(1)} %pad_maximum_fusion.5), channel_id=1, source_target_pairs={{0,4},{1,5},{2,6},{3,7},{4,0},{5,1},{6,2},{7,3},{8,12},{9,13},{10,... | collective-permute-start | bytes 196616 | tf_op jit(solution)/shard_map/ppermute | solution.py:43
  65.4 5.9 %collective-permute-start.21 = (bf16[256,128]{1,0:T(8,128)(2,1)S(1)}, bf16[256,128]{1,0:T(8,128)(2,1)S(1)}, u32[]{:S(2)}, u32[]{:S(2)}) collective-permute-start(bf16[256,128]{1,0:T(8,128)(2,1)S(1)} %pad_maximum_fusion.5), channel_id=1, source_target_pairs={{0,6},{1,7},{2,4},{3,5},{4,2},{5,3},{6,0},{7,1},{8,14},{9,15},{10,... | collective-permute-start | bytes 196616 | tf_op jit(solution)/shard_map/ppermute | solution.py:43
  71.3 11.7 %collective-permute-start.24 = (bf16[1024,128]{1,0:T(8,128)(2,1)S(1)}, bf16[1024,128]{1,0:T(8,128)(2,1)S(1)}, u32[]{:S(2)}, u32[]{:S(2)}) collective-permute-start(bf16[1024,128]{1,0:T(8,128)(2,1)S(1)} %pad_maximum_fusion.2.rest_1_), channel_id=1, source_target_pairs={{0,16},{1,17},{2,18},{3,19},{4,20},{5,21},{6,22},{7,23},{8,24},{9,... | collective-permute-start | bytes 786440 | tf_op jit(solution)/shard_map/ppermute | solution.py:43
  72.5 6.8 %collective-permute-start.22 = (bf16[3,128,128]{2,1,0:T(8,128)(2,1)S(1)}, bf16[3,128,128]{2,1,0:T(8,128)(2,1)S(1)}, u32[]{:S(2)}, u32[]{:S(2)}) collective-permute-start(bf16[3,128,128]{2,1,0:T(8,128)(2,1)S(1)} %get-tuple-element.133), channel_id=1, source_target_pairs={{0,31},{1,2},{2,1},{3,4},{4,3},{5,6},{6,5},{7,8},{8,7},{9,10},{10,... | collective-permute-start | bytes 294920 | tf_op jit(solution)/shard_map/ppermute | solution.py:43
  76.6 2.6 %collective-permute-start.23 = (bf16[3,128,128]{2,1,0:T(8,128)(2,1)S(1)}, bf16[3,128,128]{2,1,0:T(8,128)(2,1)S(1)}, u32[]{:S(2)}, u32[]{:S(2)}) collective-permute-start(bf16[3,128,128]{2,1,0:T(8,128)(2,1)S(1)} %get-tuple-element.134), channel_id=1, source_target_pairs={{0,1},{1,0},{2,3},{3,2},{4,5},{5,4},{6,7},{7,6},{8,9},{9,8},{10,11... | collective-permute-start | bytes 294920 | tf_op jit(solution)/shard_map/ppermute | solution.py:43
  80.2 3.9 %collective-permute-start.25 = (bf16[1024,128]{1,0:T(8,128)(2,1)S(1)}, bf16[1024,128]{1,0:T(8,128)(2,1)S(1)}, u32[]{:S(2)}, u32[]{:S(2)}) collective-permute-start(bf16[1024,128]{1,0:T(8,128)(2,1)S(1)} %pad_maximum_fusion.2.rest_1_), channel_id=1, source_target_pairs={{0,1},{1,0},{2,3},{3,2},{4,5},{5,4},{6,7},{7,6},{8,9},{9,8},{10,11... | collective-permute-start | bytes 786440 | tf_op jit(solution)/shard_map/ppermute | solution.py:43
  (8 other events, 50.8 us)
